TPU v7x, 256 devices: a whole 4x4x8 slice. The times are simulated.
256 devices in a mesh: dp: 32 (over x, z), ctx: 8 (over y, core).
Axes of the slice: x: 4, y: 4, z: 8, core: 2. Of those that a mesh axis runs over, the one named last changes fastest.
Arguments:
- gen_rows: bfloat16 [65536, 5120], P(('dp', 'ctx')), may hold values from -6 to 6
- gen_queries: bfloat16 [65536, 2560], P(('dp', 'ctx')), may hold values from -400 to 400
- place: int32 [65536], P(('dp', 'ctx')), may hold values from 0 to 65535, as said below
- segment: int32 [32, 2048], P('dp', 'ctx'), may hold values from 0 to 3, never falling along the last dimension, each value on 1 to 1024 neighbouring positions
- key_value_weight: bfloat16 [5120, 1024], P('dp'), may hold values from -0.078125 to 0.078125
- key_norm_gain: float32 [512], replicated, may hold values from 0.1 to 1.9
Outputs:
- attended: bfloat16 [65536, 2560], P(('dp', 'ctx'))
Inputs may be any that keep to these rules, and one draw needn't show every extreme that they name: `place`: each trainer row appears exactly once. A generated row held by the device at dp index s and ctx index c goes to a trainer row of the block (d * 8 + c) * 256 to (d * 8 + c + 1) * 256 - 1 for some d. At most 16 rows of one device go to one dp index d, and in every draw some devices send exactly 16 rows to some d.
All inputs are finite; a program needn't handle non-finite values.
Results may differ from a plain program's by a relative error of at most 0.011.
Values may be sent and summed in bfloat16 or wider, within the bound.
No kernel may reach another device: no remote copies, remote signals or barrier semaphores. Data moves between devices by JAX's collectives and lax.ppermute only.
A program may use at most 128 MiB of HBM per device.

v0:
```python
import jax
import jax.numpy as jnp
from jax import lax
from jax.sharding import PartitionSpec as P

HEAD_SIZE = 128
QUERY_HEADS = 20
KEY_VALUE_HEADS = 4


def project_kv(rows, key_value_weight, key_norm_gain):
    proj = jnp.dot(
        rows,
        lax.all_gather(key_value_weight, "dp", axis=0, tiled=True),
        preferred_element_type=jnp.float32,
    )
    row_width = key_value_weight.shape[1] // 2
    kraw = proj[:, :row_width]
    key_rows = (
        kraw * lax.rsqrt(jnp.mean(kraw * kraw, axis=-1, keepdims=True) + 1e-06) * key_norm_gain
    )
    return jnp.concatenate(
        [key_rows.astype(jnp.bfloat16), proj[:, row_width:].astype(jnp.bfloat16)], axis=1
    )


def build_slots(place):
    local_rows = place.shape[0]
    ranks = lax.axis_size("dp")
    capacity = 2 * local_rows // ranks
    target = place // (lax.axis_size("ctx") * local_rows)
    onehot = (target[:, None] == jnp.arange(ranks)[None, :]).astype(jnp.int32)
    earlier = jnp.cumsum(onehot, axis=0) - onehot
    order_in = jnp.sum(earlier * onehot, axis=1)
    slot = target * capacity + order_in
    source = (
        jnp.full((ranks * capacity,), local_rows, jnp.int32)
        .at[slot]
        .set(jnp.arange(local_rows, dtype=jnp.int32))
    )
    posted = jnp.full((ranks * capacity,), local_rows, jnp.int32).at[slot].set(place % local_rows)
    return (source, posted.reshape(ranks, capacity), ranks, capacity)


def fill_slots(value_states, source, ranks, capacity):
    taken = jnp.take(value_states, source, axis=0, mode="fill", fill_value=0)
    return taken.reshape(ranks, capacity, value_states.shape[1])


def unpack(received, posted, local_rows):
    flat_pos = posted.reshape(-1)
    row_of = (
        jnp.zeros((local_rows,), jnp.int32)
        .at[flat_pos]
        .set(jnp.arange(flat_pos.shape[0], dtype=jnp.int32), mode="drop")
    )
    flat = received.reshape(-1, received.shape[2])
    return jnp.take(flat, row_of, axis=0)


def body(gen_rows, gen_queries, place, segment, key_value_weight, key_norm_gain):
    local_rows = gen_rows.shape[0]
    source, posted, ranks, capacity = build_slots(place)
    query_slots = fill_slots(gen_queries, source, ranks, capacity)
    row_slots = fill_slots(gen_rows, source, ranks, capacity)
    got_rows, got_queries, got_pos = (
        lax.all_to_all(row_slots, "dp", split_axis=0, concat_axis=0, tiled=True),
        lax.all_to_all(query_slots, "dp", split_axis=0, concat_axis=0, tiled=True),
        lax.all_to_all(posted, "dp", split_axis=0, concat_axis=0, tiled=True),
    )
    kv_rows = project_kv(unpack(got_rows, got_pos, local_rows), key_value_weight, key_norm_gain)
    query_rows = unpack(got_queries, got_pos, local_rows)
    head_groups = QUERY_HEADS // KEY_VALUE_HEADS
    row_width = KEY_VALUE_HEADS * HEAD_SIZE
    query_rows4 = query_rows.reshape(local_rows, KEY_VALUE_HEADS, head_groups, HEAD_SIZE)
    query_seg = segment.reshape(local_rows)
    query_pos = lax.axis_index("ctx") * local_rows + jnp.arange(local_rows)
    scale = HEAD_SIZE ** (-0.5)
    key_value_piece = lax.all_gather(kv_rows, "ctx", axis=0, tiled=True)
    seg_piece = lax.all_gather(query_seg, "ctx", axis=0, tiled=True)
    row_count = key_value_piece.shape[0]
    key_pos = jnp.arange(row_count)
    allowed = (key_pos[None, :] <= query_pos[:, None]) & (seg_piece[None, :] == query_seg[:, None])
    best_choice = jnp.full((KEY_VALUE_HEADS, head_groups, local_rows), -1e30, jnp.float32)
    key_rows = key_value_piece[:, :row_width].reshape(row_count, KEY_VALUE_HEADS, HEAD_SIZE)
    value_rows = key_value_piece[:, row_width:].reshape(row_count, KEY_VALUE_HEADS, HEAD_SIZE)
    scores = (
        jnp.einsum("qhgd,khd->hgqk", query_rows4, key_rows, preferred_element_type=jnp.float32)
        * scale
    )
    masked = jnp.where(allowed, scores, jnp.float32(-1e30))
    fresh = jnp.maximum(best_choice, jnp.max(masked, axis=-1))
    weights = jnp.where(allowed, jnp.exp(masked - fresh[..., None]), jnp.float32(0.0))
    total = jnp.sum(weights, axis=-1)
    summed = jnp.einsum(
        "hgqk,khd->qhgd",
        weights.astype(jnp.bfloat16),
        value_rows,
        preferred_element_type=jnp.float32,
    )
    accum = summed
    best_choice, total, accum = (fresh, total, accum)
    result = accum / jnp.transpose(total, (2, 0, 1))[..., None]
    return result.reshape(local_rows, QUERY_HEADS * HEAD_SIZE).astype(jnp.bfloat16)


def solution(mesh):
    placed = (
        P(("dp", "ctx"), None),
        P(("dp", "ctx"), None),
        P(("dp", "ctx")),
        P("dp", "ctx"),
        P("dp", None),
        P(),
    )
    return jax.shard_map(
        body, mesh=mesh, in_specs=placed, out_specs=P(("dp", "ctx"), None), check_vma=False
    )
```

profile of v0, /device:TPU:1, one launch (start us, length us, event | category | flops | bytes accessed | tf_op | source)
XLA Modules:
  0.0 378.7 jit_solution(2724222412125014789)
XLA Ops:
  6.5 0.7 all-gather.4.cloned.1.call-update
  7.3 0.8 and_select_fusion
  8.0 0.6 reduce-window.6
  8.6 0.2 slice_reduce_fusion
  8.8 0.1 fusion.21
  9.0 1.4 scatter_custom_fusion
  10.4 0.7 all_to_all.12
  11.0 11.9 %all-to-all-start = ((s32[32,1,16]{2,1,0:T(1,128)}), s32[32,1,16]{2,1,0:T(1,128)S(1)}, u32[]{:S(2)}, u32[]{:S(2)}) async-start(s32[32,1,16]{2,1,0:T(1,128)} %bitcast.2), calls=%async_computation | async-start | bytes 32768 | tf_op jit(solution)/shard_map/all_to_all | solution.py:69
  22.9 1.4 scatter_custom_fusion.2
  24.3 0.1 broadcast_in_dim.78
  24.5 0.0 copy-done
  24.5 5.0 %gather_fusion = bf16[512,5120]{1,0:T(8,128)(2,1)} fusion(bf16[256,5120]{1,0:T(8,128)(2,1)S(1)} %copy-done, s32[1024]{0:T(1024)S(1)} %pad_clamp_fusion.1), kind=kCustom, calls=%fused_computation | custom fusion | bytes 10487808 | tf_op jit(solution)/shard_map/jit(_take)/gather | solution.py:46
  29.5 5.3 %broadcast_select_fusion = bf16[32,16,5120]{2,1,0:T(8,128)(2,1)} fusion(bf16[32,16,5120]{2,1,0:T(8,128)(2,1)} %bitcast.60, pred[32,16]{1,0:T(8,128)(4,1)S(1)} %broadcast_in_dim.78), kind=kLoop, calls=%fused_computation.14 | loop fusion | flops 2621440 | bytes 10486272 | tf_op jit(solution)/shard_map/jit(_take)/select_n | solution.py:46
  34.8 0.0 all-to-all-done
  34.8 9.4 %all-to-all-start.1 = ((bf16[32,16,5120]{2,1,0:T(8,128)(2,1)}), bf16[32,16,5120]{2,1,0:T(8,128)(2,1)}, u32[]{:S(2)}, u32[]{:S(2)}) async-start(bf16[32,16,5120]{2,1,0:T(8,128)(2,1)} %broadcast_select_fusion), calls=%async_computation.1 | async-start | bytes 10485760 | tf_op jit(solution)/shard_map/all_to_all | solution.py:67
  44.2 0.0 all-gather.6.cloned.1.call-start
  44.3 0.5 broadcast.147
  44.8 0.7 reduce.5
  45.5 0.1 reshape.119
  45.6 2.6 scatter_custom_fusion.1
  48.2 153.8 %all-to-all-done.1 = bf16[32,16,5120]{2,1,0:T(8,128)(2,1)} async-done(((bf16[32,16,5120]{2,1,0:T(8,128)(2,1)}), bf16[32,16,5120]{2,1,0:T(8,128)(2,1)}, u32[]{:S(2)}, u32[]{:S(2)}) %all-to-all-start.1) | async-done | bytes 5242912 | tf_op jit(solution)/shard_map/all_to_all | solution.py:67
  202.1 7.9 %gather_fusion.1 = bf16[256,5120]{1,0:T(8,128)(2,1)S(1)} fusion(bf16[512,5120]{1,0:T(8,128)(2,1)} %bitcast.5, s32[1024]{0:T(1024)S(1)} %pad_clamp_fusion), kind=kCustom, calls=%fused_computation.1 | custom fusion | bytes 5243904 | tf_op jit(solution)/shard_map/jit(_take)/gather | solution.py:58
  210.0 0.0 copy-start.4
  210.0 3.8 all-gather.4.cloned.1.call-done
  213.7 5.6 %fusion.7 = f32[256,1024]{1,0:T(8,128)S(1)} fusion(bf16[5120,1024]{1,0:T(8,128)(2,1)} %all-gather.4.cloned.1.call-done, bf16[256,5120]{1,0:T(8,128)(2,1)S(1)} %gather_fusion.1, pred[256]{0:T(512)(128)(4,1)S(1)} %compare_and_fusion.1), kind=kOutput, calls=%fused_computation.17 | convolution fusion | flops 2685665280 | bytes 14156032 | tf_op jit(solution)/shard_map/dot_general | solution.py:12
  219.4 0.0 copy-start.2
  219.4 0.1 multiply_reduce_fusion
  219.6 0.0 copy-done.4
  219.6 0.1 multiply_convert_fusion
  219.7 0.9 pad_maximum_fusion
  220.6 0.0 all-gather.6.cloned.1.call-update
  220.6 0.1 copy-done.2
  220.7 3.5 gather_fusion.2
  224.2 3.5 broadcast_select_fusion.1
  227.8 9.7 %all-to-all-start.2 = ((bf16[32,16,2560]{2,1,0:T(8,128)(2,1)}), bf16[32,16,2560]{2,1,0:T(8,128)(2,1)S(1)}, u32[]{:S(2)}, u32[]{:S(2)}) async-start(bf16[32,16,2560]{2,1,0:T(8,128)(2,1)} %broadcast_select_fusion.1), calls=%async_computation.2 | async-start | bytes 5242880 | tf_op jit(solution)/shard_map/all_to_all | solution.py:68
  237.5 12.1 %all-gather = s32[1,2048]{1,0:T(1,128)S(1)} all-gather(s32[1,256]{1,0:T(1,128)S(1)} %copy-done.3), channel_id=2, replica_groups=mesh['dp'=32,'ctx'=8] {'ctx'}, dimensions={1}, use_global_device_ids=true | all-gather | bytes 9216 | tf_op jit(solution)/shard_map/all_gather | solution.py:80
  249.6 0.6 fusion.12
  250.2 47.3 %all-to-all-done.2 = bf16[32,16,2560]{2,1,0:T(8,128)(2,1)S(1)} async-done(((bf16[32,16,2560]{2,1,0:T(8,128)(2,1)}), bf16[32,16,2560]{2,1,0:T(8,128)(2,1)S(1)}, u32[]{:S(2)}, u32[]{:S(2)}) %all-to-all-start.2) | async-done | bytes 2621472 | tf_op jit(solution)/shard_map/all_to_all | solution.py:68
  297.5 2.5 gather_fusion.3
  300.0 2.4 copy.21
  302.4 3.8 %fusion.34 = (bf16[2048,512]{1,0:T(8,128)(2,1)}, bf16[2048,512]{1,0:T(8,128)(2,1)S(1)}) fusion(bf16[2048,1024]{1,0:T(8,128)(2,1)} %all-gather.6.cloned.1.call-done), kind=kLoop, calls=%fused_computation.70 | loop fusion | bytes 8388608 | tf_op jit(solution)/shard_map/slice | solution.py:85
  306.3 3.9 %reshape.123 = bf16[2048,4,128]{2,1,0:T(4,128)(2,1)} reshape(bf16[2048,512]{1,0:T(8,128)(2,1)} %get-tuple-element.5) | data formatting | bytes 4194304 | tf_op jit(solution)/shard_map/reshape | solution.py:85
  310.2 2.5 copy.31
  312.7 18.3 %fusion = (f32[4,5,256]{2,1,0:T(8,128)S(1)}, f32[4,2048,256,5]{2,1,3,0:T(8,128)}) fusion(pred[256,2048]{0,1:T(8,128)(4,1)S(1)} %fusion.12, bf16[256,4,5,128]{0,3,2,1:T(8,128)(2,1)} %bitcast.64, pred[256]{0:T(512)(128)(4,1)S(1)} %compare_and_fusion.1, bf16[2048,4,128,1]{2,1,0,3:T(4,128)(2,1)} %bitcast.63), kind=kOutput, calls=%fused_computation.9 | convolution fusion | flops 2716462080 | bytes 45895936 | tf_op jit(solution)/shard_map/qhgd,khd->hgqk/dot_general | solution.py:88
  331.0 18.4 %fusion.1 = f32[4,5,256]{2,1,0:T(8,128)S(1)} fusion(f32[4,2048,256,5]{2,1,3,0:T(8,128)} %get-tuple-element.10, f32[4,5,256]{2,1,0:T(8,128)S(1)} %broadcast_maximum_fusion, pred[256,2048]{0,1:T(8,128)(4,1)S(1)} %fusion.12), kind=kLoop, calls=%fused_computation.10 | loop fusion | flops 52423680 | bytes 42508288 | tf_op jit(solution)/shard_map/reduce_sum | solution.py:94
  349.4 0.0 copy-start.1
  349.4 20.0 %fusion.6 = bf16[256,4,5,128]{0,3,2,1:T(8,128)(2,1)} fusion(bf16[2048,4,128,1]{0,2,3,1:T(8,128)(2,1)} %bitcast.62, f32[4,2048,256,5]{2,1,3,0:T(8,128)} %get-tuple-element.10, f32[4,5,256]{2,1,0:T(8,128)S(1)} %broadcast_maximum_fusion, pred[256,2048]{0,1:T(8,128)(4,1)S(1)} %fusion.12, f32[256,4,5]{0,2,1:T(8,128)S(1)} %bitcast.67), kind=kOutput, calls=%fused_computation.16 | convolution fusion | flops 2738094080 | bytes 45916160 | tf_op jit(solution)/shard_map/hgqk,khd->qhgd/dot_general | solution.py:95
  369.4 2.4 copy.26
  (23 shorter events, 0.2 us)
Async XLA Ops:
  6.5 17.9 %copy-start = (bf16[256,5120]{1,0:T(8,128)(2,1)S(1)}, bf16[256,5120]{1,0:T(8,128)(2,1)}, u32[]{:S(2)}) copy-start(bf16[256,5120]{1,0:T(8,128)(2,1)} %param.6) | copy-start | bytes 7864324
  6.5 207.2 %all-gather.4.cloned.1.call-start = ((), (), s32[]{:S(2)}) async-start(), calls=%async_computation.3 | async-start | bytes 10813440 | tf_op jit(solution)/shard_map/all_gather | solution.py:14
  11.0 23.7 %all-to-all-start = ((s32[32,1,16]{2,1,0:T(1,128)}), s32[32,1,16]{2,1,0:T(1,128)S(1)}, u32[]{:S(2)}, u32[]{:S(2)}) async-start(s32[32,1,16]{2,1,0:T(1,128)} %bitcast.2), calls=%async_computation | async-start | bytes 32768 | tf_op jit(solution)/shard_map/all_to_all | solution.py:69
  34.8 167.3 %all-to-all-start.1 = ((bf16[32,16,5120]{2,1,0:T(8,128)(2,1)}), bf16[32,16,5120]{2,1,0:T(8,128)(2,1)}, u32[]{:S(2)}, u32[]{:S(2)}) async-start(bf16[32,16,5120]{2,1,0:T(8,128)(2,1)} %broadcast_select_fusion), calls=%async_computation.1 | async-start | bytes 10485760 | tf_op jit(solution)/shard_map/all_to_all | solution.py:67
  44.2 258.2 %all-gather.6.cloned.1.call-start = ((), (), s32[]{:S(2)}) async-start(), calls=%async_computation.4 | async-start | bytes 4718592 | tf_op jit(solution)/shard_map/all_gather | solution.py:79
  210.0 9.6 %copy-start.4 = (f32[512]{0:T(512)S(1)}, f32[512]{0:T(512)}, u32[]{:S(2)}) copy-start(f32[512]{0:T(512)} %param.11) | copy-start | bytes 6148
  219.4 1.3 copy-start.2
  227.8 9.7 %copy-start.3 = (s32[1,256]{1,0:T(1,128)S(1)}, s32[1,256]{1,0:T(1,128)}, u32[]{:S(2)}) copy-start(s32[1,256]{1,0:T(1,128)} %param.9) | copy-start | bytes 3076
  227.8 69.7 %all-to-all-start.2 = ((bf16[32,16,2560]{2,1,0:T(8,128)(2,1)}), bf16[32,16,2560]{2,1,0:T(8,128)(2,1)S(1)}, u32[]{:S(2)}, u32[]{:S(2)}) async-start(bf16[32,16,2560]{2,1,0:T(8,128)(2,1)} %broadcast_select_fusion.1), calls=%async_computation.2 | async-start | bytes 5242880 | tf_op jit(solution)/shard_map/all_to_all | solution.py:68
  349.4 22.4 %copy-start.1 = (bf16[256,5120]{1,0:T(8,128)(2,1)S(1)}, bf16[256,5120]{1,0:T(8,128)(2,1)}, u32[]{:S(2)}) copy-start(bf16[256,5120]{1,0:T(8,128)(2,1)} %param.6) | copy-start | bytes 7864324
Sparse Core Ops, SparseCore 0:
  9.9 203.7 all-gather.3
  220.7 37.1 all-gather.5
where the time goes:
time: 382 us; the launch traced here: 379 us
  waiting for transfers between devices  206 us (54%)
  matrix products  43.9 us (11%)
  local copies, waits for them, and re-layouts  41.2 us (11%)
  other arithmetic  31.2 us (8%)
  starting transfers between devices  31 us (8%)
  between operations  13.6 us (4%)
  blocking collectives  12.1 us (3%)
    all_to_all x1, waiting for transfers between devices, body(): lax.all_to_all(row_slots, 'dp', split_axis=0, concat_axis=0, tiled=True)  154 us
    all_to_all x1, waiting for transfers between devices, body(): lax.all_to_all(query_slots, 'dp', split_axis=0, concat_axis=0, tiled=True)  47.3 us
    dot_general x1, matrix products, body(): jnp.einsum('hgqk,khd->qhgd', weights.astype(jnp.bfloat16), value_rows, pr...  20 us
    reduce_sum x1, other arithmetic, body(): total = jnp.sum(weights, axis=-1)  18.4 us
    dot_general x1, matrix products, body(): jnp.einsum('qhgd,khd->hgqk', query_rows4, key_rows, preferred_element_typ...  18.3 us
    gather x3, local copies, waits for them, and re-layouts, unpack(): return jnp.take(flat, row_of, axis=0)  12.8 us
    all_gather x1, blocking collectives, body(): seg_piece = lax.all_gather(query_seg, 'ctx', axis=0, tiled=True)  12.1 us
    all_to_all x1, starting transfers between devices, body(): lax.all_to_all(posted, 'dp', split_axis=0, concat_axis=0, tiled=True)  11.9 us
  transfers between devices with their start and end apart: 5, of which 3 were waited for; matrix products, arithmetic and copies ran while one was open for 10% of the time, Pallas kernels for 0%

commit v1 on v0

v1 whole, which is shorter than its diff:
```python
import functools

import jax
import jax.numpy as jnp
from jax import lax
from jax.experimental import pallas as pl
from jax.experimental.pallas import tpu as pltpu
from jax.sharding import PartitionSpec as P

LOC = 256
RANKS = 32
CAPACITY = 16
SLOTS = RANKS * CAPACITY
WIDTH = 5120
HEAD_SIZE = 128
QUERY_HEADS = 20
KEY_VALUE_HEADS = 4
HEAD_GROUP = QUERY_HEADS // KEY_VALUE_HEADS
ROW_WIDTH = KEY_VALUE_HEADS * HEAD_SIZE
QUERY_WIDTH = QUERY_HEADS * HEAD_SIZE
RANK_POSITIONS = 2048
PAIR = 2 * LOC
REACH = 1024
WINDOW = REACH + LOC
SENT = PAIR + 16
SCORE_BASE2 = 1.4426950408889634 * HEAD_SIZE ** (-0.5)
BF16 = jnp.bfloat16
F32 = jnp.float32
PARAMS = dict(vmem_limit_bytes=48 << 20)


def whole(shape):
    return pl.BlockSpec(shape, lambda *_: (0,) * len(shape))


def iota(shape, dim):
    return lax.broadcasted_iota(jnp.int32, shape, dim)


def order_rows(col, row):
    same = (col // RANK_POSITIONS) == (row // RANK_POSITIONS)
    earlier = iota((LOC, LOC), 0) < iota((LOC, LOC), 1)
    order = jnp.sum((same & earlier).astype(jnp.int32), axis=0, keepdims=True)
    return row // RANK_POSITIONS, order


def order_cols(col, row):
    same = (col // RANK_POSITIONS) == (row // RANK_POSITIONS)
    earlier = iota((LOC, LOC), 1) < iota((LOC, LOC), 0)
    order = jnp.sum((same & earlier).astype(jnp.int32), axis=1, keepdims=True)
    return col // RANK_POSITIONS, order


def onehot(mask):
    return jnp.where(mask, F32(1), F32(0)).astype(BF16)


def pick(mask, values):
    return jnp.dot(onehot(mask), values, preferred_element_type=F32).astype(BF16)


def pack_queries_kernel(col_ref, row_ref, sib_col_ref, sib_row_ref, core_ref, q_ref, out_ref, code_ref):
    core = core_ref[0]
    target, order = order_rows(col_ref[...], row_ref[...])
    slot = target * CAPACITY + order
    out_ref[...] = pick(iota((SLOTS, LOC), 0) == slot, q_ref[...])

    @pl.when(pl.program_id(0) == 0)
    def _():
        code = jnp.zeros((8, 2 * SLOTS), F32)
        for col, row, k in ((col_ref, row_ref, core), (sib_col_ref, sib_row_ref, 1 - core)):
            target_c, order_c = order_cols(col[...], row[...])
            slot_c = target_c * (2 * CAPACITY) + k * CAPACITY + order_c
            hot = onehot(iota((LOC, 2 * SLOTS), 1) == slot_c)
            pos = jnp.broadcast_to(row[...] % LOC + 1, (8, LOC)).astype(F32).astype(BF16)
            code += jnp.dot(pos, hot, preferred_element_type=F32)
        code_ref[...] = code[0:1].astype(jnp.int32)


def pack_queries(col, row, sib_col, sib_row, core, queries):
    steps = 4
    width = QUERY_WIDTH // steps
    return pl.pallas_call(
        pack_queries_kernel,
        grid=(steps,),
        in_specs=[
            whole((LOC, 1)),
            whole((1, LOC)),
            whole((LOC, 1)),
            whole((1, LOC)),
            pl.BlockSpec(memory_space=pltpu.SMEM),
            pl.BlockSpec((LOC, width), lambda i: (0, i)),
        ],
        out_specs=[pl.BlockSpec((SLOTS, width), lambda i: (0, i)), whole((1, 2 * SLOTS))],
        out_shape=[
            jax.ShapeDtypeStruct((SLOTS, QUERY_WIDTH), BF16),
            jax.ShapeDtypeStruct((1, 2 * SLOTS), jnp.int32),
        ],
        compiler_params=pltpu.CompilerParams(**PARAMS),
        cost_estimate=pl.CostEstimate(
            flops=2 * SLOTS * LOC * QUERY_WIDTH, bytes_accessed=4 << 20, transcendentals=0
        ),
        name="pack_queries",
    )(col, row, sib_col, sib_row, core, queries)


def project_kernel(
    steps, col_ref, row_ref, sib_col_ref, sib_row_ref, core_ref, x_ref, sib_ref, w_ref, gain_ref, out_ref, acc
):
    step = pl.program_id(0)

    @pl.when(step == 0)
    def _():
        acc[...] = jnp.zeros_like(acc)

    acc[0:LOC, :] += jnp.dot(x_ref[...], w_ref[...], preferred_element_type=F32)
    acc[LOC:PAIR, :] += jnp.dot(sib_ref[...], w_ref[...], preferred_element_type=F32)

    @pl.when(step == steps - 1)
    def _():
        core = core_ref[0]
        is_key = core == 0
        raw = acc[...]
        level = lax.rsqrt(jnp.mean(raw * raw, axis=-1, keepdims=True) + 1e-06)
        level = jnp.where(is_key, level, F32(1))
        gain = jnp.where(is_key, gain_ref[...], F32(1))
        done = (raw * level * gain).astype(BF16)
        hots = []
        for col, row, k in ((col_ref, row_ref, core), (sib_col_ref, sib_row_ref, 1 - core)):
            target, order = order_rows(col[...], row[...])
            slot = target * (2 * CAPACITY) + k * CAPACITY + order
            hots.append(iota((2 * SLOTS, LOC), 0) == slot)
        out_ref[...] = pick(jnp.concatenate(hots, axis=1), done)


def project(col, row, sib_col, sib_row, core, rows, sib_rows, weight, gain):
    steps = 4
    depth = WIDTH // steps
    return pl.pallas_call(
        functools.partial(project_kernel, steps),
        grid=(steps,),
        in_specs=[
            whole((LOC, 1)),
            whole((1, LOC)),
            whole((LOC, 1)),
            whole((1, LOC)),
            pl.BlockSpec(memory_space=pltpu.SMEM),
            pl.BlockSpec((LOC, depth), lambda i: (0, i)),
            pl.BlockSpec((LOC, depth), lambda i: (0, i)),
            pl.BlockSpec((depth, ROW_WIDTH), lambda i: (i, 0)),
            whole((1, ROW_WIDTH)),
        ],
        out_specs=whole((2 * SLOTS, ROW_WIDTH)),
        out_shape=jax.ShapeDtypeStruct((2 * SLOTS, ROW_WIDTH), BF16),
        scratch_shapes=[pltpu.VMEM((PAIR, ROW_WIDTH), F32)],
        compiler_params=pltpu.CompilerParams(**PARAMS),
        cost_estimate=pl.CostEstimate(
            flops=2 * PAIR * WIDTH * ROW_WIDTH, bytes_accessed=12 << 20, transcendentals=0
        ),
        name="project",
    )(col, row, sib_col, sib_row, core, rows, sib_rows, weight, gain)


def unpack_kernel(code_ref, seg_ref, got_ref, out_ref):
    code = code_ref[...]
    half = (iota((1, 2 * SLOTS), 1) // CAPACITY) % 2
    where = jnp.where(code > 0, code - 1 + half * LOC, -1)
    out_ref[0:PAIR, :] = pick(iota((PAIR, 2 * SLOTS), 0) == where, got_ref[...])
    seg = jnp.broadcast_to(seg_ref[...], (16, PAIR))
    out_ref[PAIR:SENT, :] = seg.astype(F32).astype(BF16)


def unpack(code, seg, got):
    return pl.pallas_call(
        unpack_kernel,
        out_shape=jax.ShapeDtypeStruct((SENT, ROW_WIDTH), BF16),
        compiler_params=pltpu.CompilerParams(**PARAMS),
        cost_estimate=pl.CostEstimate(
            flops=2 * PAIR * 2 * SLOTS * ROW_WIDTH, bytes_accessed=2 << 20, transcendentals=0
        ),
        name="unpack",
    )(code, seg, got)


def attend_kernel(
    where_ref, code_ref, seg_ref, q_ref, a0, a1, a2, b0, b1, b2, out_ref, keys, values, bias, qs
):
    core = where_ref[0]
    ctx = where_ref[1]

    @pl.when(pl.program_id(0) == 0)
    def _():
        @pl.when(core == 0)
        def _():
            for dst, (s0, s1, s2) in ((keys, (a0, a1, a2)), (values, (b0, b1, b2))):
                dst[0:PAIR, :] = s2[0:PAIR, :]
                dst[PAIR : 2 * PAIR, :] = s1[0:PAIR, :]
                dst[2 * PAIR : WINDOW, :] = s0[0:LOC, :]

        @pl.when(core != 0)
        def _():
            for dst, (s0, s1, s2) in ((keys, (b0, b1, b2)), (values, (a0, a1, a2))):
                dst[0:LOC, :] = s2[LOC:PAIR, :]
                dst[LOC : LOC + PAIR, :] = s1[0:PAIR, :]
                dst[LOC + PAIR : WINDOW, :] = s0[0:PAIR, :]

        segs = [a[PAIR : PAIR + 16, :][0:1].astype(F32) for a in (a2, a1, a0)]
        left = jnp.concatenate([segs[0], segs[1], segs[2][:, 0:LOC]], axis=1)
        right = jnp.concatenate([segs[0][:, LOC:PAIR], segs[1], segs[2]], axis=1)
        key_seg = jnp.where(core == 0, left, right)
        query_seg = seg_ref[...].astype(F32)
        k = iota((LOC, WINDOW), 1)
        q = iota((LOC, WINDOW), 0)
        allowed = (k <= q + REACH) & (k >= REACH - ctx * LOC) & (key_seg == query_seg)
        bias[...] = jnp.where(allowed, F32(0), F32(-1e30))

    code = code_ref[...]
    qs[...] = pick(iota((LOC, SLOTS), 0) == code - 1, q_ref[...])
    head = pl.multiple_of(pl.program_id(0) * HEAD_SIZE, HEAD_SIZE)
    key_rows = keys[:, pl.ds(head, HEAD_SIZE)]
    value_rows = values[:, pl.ds(head, HEAD_SIZE)]
    for g in range(HEAD_GROUP):
        cols = slice(g * HEAD_SIZE, (g + 1) * HEAD_SIZE)
        scores = lax.dot_general(
            qs[:, cols], key_rows, (((1,), (1,)), ((), ())), preferred_element_type=F32
        )
        scores = scores + bias[...]
        best = jnp.max(scores, axis=-1, keepdims=True)
        p = jnp.exp2((scores - best) * SCORE_BASE2)
        total = jnp.sum(p, axis=-1, keepdims=True)
        summed = jnp.dot(p.astype(BF16), value_rows, preferred_element_type=F32)
        out_ref[:, cols] = (summed / total).astype(BF16)


def attend(where, code, seg_col, got_queries, mine, other):
    width = HEAD_GROUP * HEAD_SIZE
    block = whole((SENT, ROW_WIDTH))
    return pl.pallas_call(
        attend_kernel,
        grid=(KEY_VALUE_HEADS,),
        in_specs=[
            pl.BlockSpec(memory_space=pltpu.SMEM),
            whole((1, SLOTS)),
            whole((LOC, 1)),
            pl.BlockSpec((SLOTS, width), lambda i: (0, i)),
        ]
        + [block] * 6,
        out_specs=pl.BlockSpec((LOC, width), lambda i: (0, i)),
        out_shape=jax.ShapeDtypeStruct((LOC, QUERY_WIDTH), BF16),
        scratch_shapes=[
            pltpu.VMEM((WINDOW, ROW_WIDTH), BF16),
            pltpu.VMEM((WINDOW, ROW_WIDTH), BF16),
            pltpu.VMEM((LOC, WINDOW), F32),
            pltpu.VMEM((LOC, width), BF16),
        ],
        compiler_params=pltpu.CompilerParams(**PARAMS),
        cost_estimate=pl.CostEstimate(
            flops=4 * LOC * WINDOW * QUERY_WIDTH,
            bytes_accessed=8 << 20,
            transcendentals=LOC * WINDOW * QUERY_HEADS,
        ),
        name="attend",
    )(where, code, seg_col, got_queries, *mine, *other)


def swap_cores(array):
    return lax.ppermute(array, "ctx", [(i, i ^ 1) for i in range(8)])


def send_up(array, by):
    pairs = [(y * 2 + k, (y + by) * 2 + k) for y in range(4 - by) for k in range(2)]
    return lax.ppermute(array, "ctx", pairs)


def body(gen_rows, gen_queries, place, segment, key_value_weight, key_norm_gain):
    ctx = lax.axis_index("ctx")
    core = ctx % 2
    seg = segment.reshape(LOC)
    sib = swap_cores(jnp.stack([place, seg]))
    sib_rows = swap_cores(gen_rows)
    col, row = place.reshape(LOC, 1), place.reshape(1, LOC)
    sib_col, sib_row = sib[0].reshape(LOC, 1), sib[0].reshape(1, LOC)
    core_s = core.reshape(1)
    pair_seg = jnp.where(core == 0, jnp.concatenate([seg, sib[1]]), jnp.concatenate([sib[1], seg]))
    pair_seg = pair_seg.reshape(1, PAIR)

    query_slots, code = pack_queries(col, row, sib_col, sib_row, core_s, gen_queries)
    got_code = lax.all_to_all(
        code.reshape(RANKS, 2 * CAPACITY), "dp", split_axis=0, concat_axis=0, tiled=True
    )
    got_queries = lax.all_to_all(
        query_slots.reshape(RANKS, CAPACITY, QUERY_WIDTH), "dp", split_axis=0, concat_axis=0, tiled=True
    ).reshape(SLOTS, QUERY_WIDTH)

    half = lax.dynamic_slice_in_dim(key_value_weight, core * ROW_WIDTH, ROW_WIDTH, 1)
    weight = lax.all_gather(half, "dp", axis=0, tiled=True)
    slots = project(
        col, row, sib_col, sib_row, core_s, gen_rows, sib_rows, weight, key_norm_gain.reshape(1, ROW_WIDTH)
    )
    got = lax.all_to_all(
        slots.reshape(RANKS, 2 * CAPACITY, ROW_WIDTH), "dp", split_axis=0, concat_axis=0, tiled=True
    ).reshape(2 * SLOTS, ROW_WIDTH)
    mine0 = unpack(got_code.reshape(1, 2 * SLOTS), pair_seg, got)
    mine = [mine0, send_up(mine0, 1), send_up(mine0, 2)]
    other = [swap_cores(m) for m in mine]
    own_code = lax.dynamic_slice_in_dim(got_code, core * CAPACITY, CAPACITY, 1)
    where = jnp.stack([core, ctx])
    return attend(where, own_code.reshape(1, SLOTS), seg.reshape(LOC, 1), got_queries, mine, other)


def solution(mesh):
    placed = (
        P(("dp", "ctx"), None),
        P(("dp", "ctx"), None),
        P(("dp", "ctx")),
        P("dp", "ctx"),
        P("dp", None),
        P(),
    )
    return jax.shard_map(
        body, mesh=mesh, in_specs=placed, out_specs=P(("dp", "ctx"), None), check_vma=False
    )
```

time: 382 us -> 226 us (0.59)
  waiting for transfers between devices: 206 us -> 93.7 us
  matrix products: 43.9 us -> 0 us
  local copies, waits for them, and re-layouts: 41.2 us -> 10.6 us
  other arithmetic: 31.2 us -> 1.96 us
  Pallas kernels: 0 us -> 28.8 us
  starting transfers between devices: 31 us -> 47.7 us
  blocking collectives: 12.1 us -> 26.7 us
    all_to_all x3 -> x2, waiting for transfers between devices: 201 us -> 26.9 us  [the longest x1 26.9 us: body(): lax.all_to_all(query_slots.reshape(RANKS, CAPACITY, QUERY_WIDTH), 'dp', s...]
    all_gather x2 -> x1, waiting for transfers between devices: 3.76 us -> 62.5 us  [body(): weight = lax.all_gather(half, 'dp', axis=0, tiled=True)]
    dot_general x3 -> x0, matrix products: 43.9 us -> none  [the longest x1 20 us: body(): jnp.einsum('hgqk,khd->qhgd', weights.astype(jnp.bfloat16), value_rows, pr...]
    ppermute x0 -> x7, starting transfers between devices: none -> 29.5 us  [the longest x5 21.2 us: swap_cores(): return lax.ppermute(array, 'ctx', [(i, i ^ 1) for i in range(8)])]
    pallas_call x0 -> x4, Pallas kernels: none -> 28.8 us  [the longest x1 17.2 us: attend(): pl.pallas_call(attend_kernel, grid=(KEY_VALUE_HEADS,), in_specs=[pl.Block...]
    all_to_all x0 -> x1, blocking collectives: none -> 26.7 us  [body(): lax.all_to_all(slots.reshape(RANKS, 2 * CAPACITY, ROW_WIDTH), 'dp', split...]
    gather x5 -> x0, local copies, waits for them, and re-layouts: 21.4 us -> none  [the longest x3 12.8 us: unpack(): return jnp.take(flat, row_of, axis=0)]
    reduce_sum x3 -> x0, other arithmetic: 18.7 us -> none  [the longest x1 18.4 us: body(): total = jnp.sum(weights, axis=-1)]
  transfers between devices with their start and end apart: 5 -> 10, of which waited for: 3 -> 4; matrix products, arithmetic and copies ran while one was open for 10% -> 2% of each run, Pallas kernels for 0% -> 5%
where the time goes in v1:
time: 226 us; the launch traced here: 223 us
  waiting for transfers between devices  93.7 us (41%)
  starting transfers between devices  47.7 us (21%)
  Pallas kernels  28.8 us (13%)
  blocking collectives  26.7 us (12%)
  between operations  13.6 us (6%)
  local copies, waits for them, and re-layouts  10.6 us (5%)
    all_gather x1, waiting for transfers between devices, body(): weight = lax.all_gather(half, 'dp', axis=0, tiled=True)  62.5 us
    all_to_all x1, waiting for transfers between devices, body(): lax.all_to_all(query_slots.reshape(RANKS, CAPACITY, QUERY_WIDTH), 'dp', s...  26.9 us
    all_to_all x1, blocking collectives, body(): lax.all_to_all(slots.reshape(RANKS, 2 * CAPACITY, ROW_WIDTH), 'dp', split...  26.7 us
    ppermute x5, starting transfers between devices, swap_cores(): return lax.ppermute(array, 'ctx', [(i, i ^ 1) for i in range(8)])  21.2 us
    pallas_call x1, Pallas kernels, attend(): pl.pallas_call(attend_kernel, grid=(KEY_VALUE_HEADS,), in_specs=[pl.Block...  17.2 us
    all_to_all x1, starting transfers between devices, body(): lax.all_to_all(code.reshape(RANKS, 2 * CAPACITY), 'dp', split_axis=0, con...  9.3 us
    all_to_all x1, starting transfers between devices, body(): lax.all_to_all(query_slots.reshape(RANKS, CAPACITY, QUERY_WIDTH), 'dp', s...  8.84 us
    ppermute x2, starting transfers between devices, send_up(): return lax.ppermute(array, 'ctx', pairs)  8.29 us
  transfers between devices with their start and end apart: 10, of which 4 were waited for; matrix products, arithmetic and copies ran while one was open for 2% of the time, Pallas kernels for 5%

profile of v1, /device:TPU:1, one launch (start us, length us, event | category | flops | bytes accessed | tf_op | source)
XLA Modules:
  0.0 223.0 jit_solution(11122799727249631340)
XLA Ops:
  6.5 0.0 copy-start
  6.5 0.0 all-gather.2.cloned.1.call-start
  6.6 0.9 copy-done
  7.5 0.7 constant_dynamic-slice_fusion
  8.2 0.0 all-gather.2.cloned.1.call-update
  8.2 3.3 %collective-permute-start.1 = (bf16[256,5120]{1,0:T(8,128)(2,1)}, bf16[256,5120]{1,0:T(8,128)(2,1)}, u32[]{:S(2)}, u32[]{:S(2)}) collective-permute-start(bf16[256,5120]{1,0:T(8,128)(2,1)} %x_ref.1), channel_id=1, source_target_pairs={{0,1},{1,0},{2,3},{3,2},{4,5},{5,4},{6,7},{7,6},{8,9},{9,8},{10,11... | collective-permute-start | bytes 7864328 | tf_op jit(solution)/shard_map/ppermute | solution.py:267
  11.5 0.7 pad_add_fusion
  12.2 0.0 collective-permute-start
  12.3 0.8 copy.12.col_ref
  13.1 3.0 %collective-permute-done = s32[2,256]{1,0:T(2,128)S(1)} collective-permute-done((s32[2,256]{1,0:T(2,128)S(1)}, s32[2,256]{1,0:T(2,128)S(1)}, u32[]{:S(2)}, u32[]{:S(2)}) %collective-permute-start) | collective-permute-done | bytes 2080 | tf_op jit(solution)/shard_map/ppermute | solution.py:267
  16.1 0.1 copy.13.sib_col_ref
  16.2 0.0 copy-start.4
  16.2 0.7 copy-done.4
  16.9 1.3 copy-done.7
  18.2 3.2 %pack_queries.1 = (bf16[512,2560]{1,0:T(8,128)(2,1)S(1)}, s32[1,1024]{1,0:T(1,128)S(1)}) custom-call(s32[256,1]{1,0:T(8,128)S(1)} %copy.12.col_ref, s32[1,256]{1,0:T(1,128)S(1)} %bitcast.19, s32[256,1]{1,0:T(8,128)S(1)} %copy.13.sib_col_ref, s32[1,256]{1,0:T(1,128)S(1)} %get-tuple-element.11.sib_row_ref, s32[1]{0:T(128)} %bitcast.core_ref, ...), custom_call_target="tpu_custom_call" | custom-call | flops 671088640 | bytes 4194304 | tf_op jit(solution)/shard_map/pack_queries/pallas_call | solution.py:83
  21.4 1.5 copy-done.1
  22.9 0.5 broadcast.17
  23.4 0.6 reduce.10
  24.0 0.7 all_to_all.12
  24.6 9.3 %all-to-all-start = ((s32[32,1,32]{2,1,0:T(1,128)}), s32[32,1,32]{2,1,0:T(1,128)S(1)}, u32[]{:S(2)}, u32[]{:S(2)}) async-start(s32[32,1,32]{2,1,0:T(1,128)} %bitcast.5), calls=%async_computation | async-start | bytes 32768 | tf_op jit(solution)/shard_map/all_to_all | solution.py:288
  33.9 0.0 collective-permute-done.1.sib_ref
  33.9 62.5 %all-gather.2.cloned.1.call-done.w_ref = bf16[5120,512]{1,0:T(8,128)(2,1)} async-done(((bf16[160,512]{1,0:T(8,128)(2,1)}), bf16[5120,512]{1,0:T(8,128)(2,1)}) %all-gather.2.cloned.1.call-update) | async-done | bytes 5242896 | tf_op jit(solution)/shard_map/all_gather | solution.py:296
  96.5 0.0 copy-done.6
  96.5 1.7 copy-done.2
  98.2 7.0 %project.1 = bf16[1024,512]{1,0:T(8,128)(2,1)S(1)} custom-call(s32[256,1]{1,0:T(8,128)S(1)} %copy.12.col_ref, s32[1,256]{1,0:T(1,128)S(1)} %bitcast.20, s32[256,1]{1,0:T(8,128)S(1)} %copy.13.sib_col_ref, s32[1,256]{1,0:T(1,128)S(1)} %get-tuple-element.11.sib_row_ref, s32[1]{0:T(128)} %bitcast.core_ref, bf16[256,5120]{1,0:T(8,128)(2,1)S(1)} %copy-done.2, ...), custom_call_target="tpu_custom_call" | custom-call | flops 2684354560 | bytes 12582912 | tf_op jit(solution)/shard_map/project/pallas_call | solution.py:139
  105.2 0.0 all-to-all-done
  105.2 26.7 %all_to_all.19 = bf16[32,32,512]{2,1,0:T(8,128)(2,1)} all-to-all(bf16[32,32,512]{2,1,0:T(8,128)(2,1)S(1)} %bitcast.13), channel_id=1, replica_groups=mesh['dp'=32,'ctx'=8] {'dp'}, dimensions={0} | all-to-all | bytes 2097152 | tf_op jit(solution)/shard_map/all_to_all | solution.py:300
  131.9 8.8 %all-to-all-start.1 = ((bf16[32,16,2560]{2,1,0:T(8,128)(2,1)}), bf16[32,16,2560]{2,1,0:T(8,128)(2,1)S(1)}, u32[]{:S(2)}, u32[]{:S(2)}) async-start(bf16[32,16,2560]{2,1,0:T(8,128)(2,1)} %bitcast.14), calls=%async_computation.1 | async-start | bytes 5242880 | tf_op jit(solution)/shard_map/all_to_all | solution.py:291
  140.8 0.6 reduce.11
  141.4 0.1 reshape.89.code_ref
  141.5 1.2 copy-done.3
  142.7 1.5 unpack.1.a0
  144.2 3.9 %collective-permute-start.2 = (bf16[528,512]{1,0:T(8,128)(2,1)}, bf16[528,512]{1,0:T(8,128)(2,1)}, u32[]{:S(2)}, u32[]{:S(2)}) collective-permute-start(bf16[528,512]{1,0:T(8,128)(2,1)} %unpack.1.a0), channel_id=1, source_target_pairs={{0,2},{1,3},{2,4},{3,5},{4,6},{5,7},{8,10},{9,11},{10,12},{11,13},... | collective-permute-start | bytes 1622024 | tf_op jit(solution)/shard_map/ppermute | solution.py:272
  148.1 4.4 %collective-permute-start.3 = (bf16[528,512]{1,0:T(8,128)(2,1)}, bf16[528,512]{1,0:T(8,128)(2,1)}, u32[]{:S(2)}, u32[]{:S(2)}) collective-permute-start(bf16[528,512]{1,0:T(8,128)(2,1)} %unpack.1.a0), channel_id=1, source_target_pairs={{0,4},{1,5},{2,6},{3,7},{8,12},{9,13},{10,14},{11,15},{16,20},{17,... | collective-permute-start | bytes 1622024 | tf_op jit(solution)/shard_map/ppermute | solution.py:272
  152.5 5.0 %collective-permute-start.4 = (bf16[528,512]{1,0:T(8,128)(2,1)}, bf16[528,512]{1,0:T(8,128)(2,1)}, u32[]{:S(2)}, u32[]{:S(2)}) collective-permute-start(bf16[528,512]{1,0:T(8,128)(2,1)} %unpack.1.a0), channel_id=1, source_target_pairs={{0,1},{1,0},{2,3},{3,2},{4,5},{5,4},{6,7},{7,6},{8,9},{9,8},{10,11... | collective-permute-start | bytes 1622024 | tf_op jit(solution)/shard_map/ppermute | solution.py:267
  157.5 0.0 collective-permute-done.2.a1
  157.5 7.6 %collective-permute-start.5 = (bf16[528,512]{1,0:T(8,128)(2,1)}, bf16[528,512]{1,0:T(8,128)(2,1)}, u32[]{:S(2)}, u32[]{:S(2)}) collective-permute-start(bf16[528,512]{1,0:T(8,128)(2,1)} %collective-permute-done.2.a1), channel_id=1, source_target_pairs={{0,1},{1,0},{2,3},{3,2},{4,5},{5,4},{6,7},{7,6},{8,9},{9,8},{10,11... | collective-permute-start | bytes 1622024 | tf_op jit(solution)/shard_map/ppermute | solution.py:267
  165.0 1.3 collective-permute-done.3.a2
  166.3 5.3 %collective-permute-start.6 = (bf16[528,512]{1,0:T(8,128)(2,1)}, bf16[528,512]{1,0:T(8,128)(2,1)}, u32[]{:S(2)}, u32[]{:S(2)}) collective-permute-start(bf16[528,512]{1,0:T(8,128)(2,1)} %collective-permute-done.3.a2), channel_id=1, source_target_pairs={{0,1},{1,0},{2,3},{3,2},{4,5},{5,4},{6,7},{7,6},{8,9},{9,8},{10,11... | collective-permute-start | bytes 1622024 | tf_op jit(solution)/shard_map/ppermute | solution.py:267
  171.7 0.1 copy.17.seg_ref
  171.8 0.1 pad_add_fusion.1.where_ref
  171.9 0.1 dynamic-slice_reduce_fusion
  172.0 0.1 reshape.86.code_ref
  172.1 26.9 %all-to-all-done.1 = bf16[32,16,2560]{2,1,0:T(8,128)(2,1)S(1)} async-done(((bf16[32,16,2560]{2,1,0:T(8,128)(2,1)}), bf16[32,16,2560]{2,1,0:T(8,128)(2,1)S(1)}, u32[]{:S(2)}, u32[]{:S(2)}) %all-to-all-start.1) | async-done | bytes 2621472 | tf_op jit(solution)/shard_map/all_to_all | solution.py:291
  199.0 0.0 collective-permute-done.4.b0
  199.0 0.0 collective-permute-done.5.b1
  199.0 0.0 collective-permute-done.6.b2
  199.0 17.2 %attend.1 = bf16[256,2560]{1,0:T(8,128)(2,1)} custom-call(s32[2]{0:T(128)S(1)} %pad_add_fusion.1.where_ref, s32[1,512]{1,0:T(1,128)S(1)} %reshape.86.code_ref, s32[256,1]{1,0:T(8,128)S(1)} %copy.17.seg_ref, bf16[512,2560]{1,0:T(8,128)(2,1)S(1)} %bitcast.15, bf16[528,512]{1,0:T(8,128)(2,1)} %unpack.1.a0, bf16[528,512]{1,0:T(8,128)(2,1)} %collective-permute-done.2.a1, ...), custom_call_target="tpu_custom_call" | custom-call | flops 3355443200 | bytes 8388608 | tf_op jit(solution)/shard_map/attend/pallas_call | solution.py:238
  (11 shorter events, 0.0 us)
Async XLA Ops:
  6.5 1.0 copy-start
  6.5 89.9 %copy-start.5 = (s32[256]{0:T(256)S(1)}, s32[256]{0:T(256)}, u32[]{:S(2)}) copy-start(s32[256]{0:T(256)} %param.8) | copy-start | bytes 3076
  6.5 89.9 %copy-start.6 = (f32[512]{0:T(512)S(1)}, f32[512]{0:T(512)}, u32[]{:S(2)}) copy-start(f32[512]{0:T(512)} %param.11) | copy-start | bytes 6148
  6.5 89.9 %all-gather.2.cloned.1.call-start = ((), (), s32[]{:S(2)}) async-start(), calls=%async_computation.3 | async-start | bytes 5406720 | tf_op jit(solution)/shard_map/all_gather | solution.py:296
  8.2 25.7 %collective-permute-start.1 = (bf16[256,5120]{1,0:T(8,128)(2,1)}, bf16[256,5120]{1,0:T(8,128)(2,1)}, u32[]{:S(2)}, u32[]{:S(2)}) collective-permute-start(bf16[256,5120]{1,0:T(8,128)(2,1)} %x_ref.1), channel_id=1, source_target_pairs={{0,1},{1,0},{2,3},{3,2},{4,5},{5,4},{6,7},{7,6},{8,9},{9,8},{10,11... | collective-permute-start | bytes 7864328 | tf_op jit(solution)/shard_map/ppermute | solution.py:267
  12.2 3.8 %collective-permute-start = (s32[2,256]{1,0:T(2,128)S(1)}, s32[2,256]{1,0:T(2,128)S(1)}, u32[]{:S(2)}, u32[]{:S(2)}) collective-permute-start(s32[2,256]{1,0:T(2,128)S(1)} %pad_add_fusion), channel_id=1, source_target_pairs={{0,1},{1,0},{2,3},{3,2},{4,5},{5,4},{6,7},{7,6},{8,9},{9,8},{10,11... | collective-permute-start | bytes 6152 | tf_op jit(solution)/shard_map/ppermute | solution.py:267
  16.2 0.7 copy-start.4
  16.9 1.3 copy-start.7
  21.4 1.5 copy-start.1
  24.6 80.6 %all-to-all-start = ((s32[32,1,32]{2,1,0:T(1,128)}), s32[32,1,32]{2,1,0:T(1,128)S(1)}, u32[]{:S(2)}, u32[]{:S(2)}) async-start(s32[32,1,32]{2,1,0:T(1,128)} %bitcast.5), calls=%async_computation | async-start | bytes 32768 | tf_op jit(solution)/shard_map/all_to_all | solution.py:288
  96.5 1.7 copy-start.2
  131.9 8.9 %copy-start.8 = (s32[1,256]{1,0:T(1,128)S(1)}, s32[1,256]{1,0:T(1,128)}, u32[]{:S(2)}) copy-start(s32[1,256]{1,0:T(1,128)} %param.9) | copy-start | bytes 3076
  131.9 67.1 %all-to-all-start.1 = ((bf16[32,16,2560]{2,1,0:T(8,128)(2,1)}), bf16[32,16,2560]{2,1,0:T(8,128)(2,1)S(1)}, u32[]{:S(2)}, u32[]{:S(2)}) async-start(bf16[32,16,2560]{2,1,0:T(8,128)(2,1)} %bitcast.14), calls=%async_computation.1 | async-start | bytes 5242880 | tf_op jit(solution)/shard_map/all_to_all | solution.py:291
  141.5 1.2 copy-start.3
  144.2 13.3 %collective-permute-start.2 = (bf16[528,512]{1,0:T(8,128)(2,1)}, bf16[528,512]{1,0:T(8,128)(2,1)}, u32[]{:S(2)}, u32[]{:S(2)}) collective-permute-start(bf16[528,512]{1,0:T(8,128)(2,1)} %unpack.1.a0), channel_id=1, source_target_pairs={{0,2},{1,3},{2,4},{3,5},{4,6},{5,7},{8,10},{9,11},{10,12},{11,13},... | collective-permute-start | bytes 1622024 | tf_op jit(solution)/shard_map/ppermute | solution.py:272
  148.1 18.2 %collective-permute-start.3 = (bf16[528,512]{1,0:T(8,128)(2,1)}, bf16[528,512]{1,0:T(8,128)(2,1)}, u32[]{:S(2)}, u32[]{:S(2)}) collective-permute-start(bf16[528,512]{1,0:T(8,128)(2,1)} %unpack.1.a0), channel_id=1, source_target_pairs={{0,4},{1,5},{2,6},{3,7},{8,12},{9,13},{10,14},{11,15},{16,20},{17,... | collective-permute-start | bytes 1622024 | tf_op jit(solution)/shard_map/ppermute | solution.py:272
  152.5 46.5 %collective-permute-start.4 = (bf16[528,512]{1,0:T(8,128)(2,1)}, bf16[528,512]{1,0:T(8,128)(2,1)}, u32[]{:S(2)}, u32[]{:S(2)}) collective-permute-start(bf16[528,512]{1,0:T(8,128)(2,1)} %unpack.1.a0), channel_id=1, source_target_pairs={{0,1},{1,0},{2,3},{3,2},{4,5},{5,4},{6,7},{7,6},{8,9},{9,8},{10,11... | collective-permute-start | bytes 1622024 | tf_op jit(solution)/shard_map/ppermute | solution.py:267
  157.5 41.5 %collective-permute-start.5 = (bf16[528,512]{1,0:T(8,128)(2,1)}, bf16[528,512]{1,0:T(8,128)(2,1)}, u32[]{:S(2)}, u32[]{:S(2)}) collective-permute-start(bf16[528,512]{1,0:T(8,128)(2,1)} %collective-permute-done.2.a1), channel_id=1, source_target_pairs={{0,1},{1,0},{2,3},{3,2},{4,5},{5,4},{6,7},{7,6},{8,9},{9,8},{10,11... | collective-permute-start | bytes 1622024 | tf_op jit(solution)/shard_map/ppermute | solution.py:267
  166.3 32.7 %collective-permute-start.6 = (bf16[528,512]{1,0:T(8,128)(2,1)}, bf16[528,512]{1,0:T(8,128)(2,1)}, u32[]{:S(2)}, u32[]{:S(2)}) collective-permute-start(bf16[528,512]{1,0:T(8,128)(2,1)} %collective-permute-done.3.a2), channel_id=1, source_target_pairs={{0,1},{1,0},{2,3},{3,2},{4,5},{5,4},{6,7},{7,6},{8,9},{9,8},{10,11... | collective-permute-start | bytes 1622024 | tf_op jit(solution)/shard_map/ppermute | solution.py:267
Sparse Core Ops, SparseCore 0:
  9.9 86.4 all-gather.1

commit v2 on v1

v2 whole, which is shorter than its diff:
```python
import functools

import jax
import jax.numpy as jnp
from jax import lax
from jax.experimental import pallas as pl
from jax.experimental.pallas import tpu as pltpu
from jax.sharding import PartitionSpec as P

LOC = 256
RANKS = 32
CAPACITY = 16
SLOTS = RANKS * CAPACITY
WIDTH = 5120
HEAD_SIZE = 128
QUERY_HEADS = 20
KEY_VALUE_HEADS = 4
HEAD_GROUP = QUERY_HEADS // KEY_VALUE_HEADS
ROW_WIDTH = KEY_VALUE_HEADS * HEAD_SIZE
QUERY_WIDTH = QUERY_HEADS * HEAD_SIZE
RANK_POSITIONS = 2048
PAIR = 2 * LOC
REACH = 1024
CODE_WIDTH = 128
NEAR = (0, -1, 1, -2)
RUN = WIDTH // 4
GROUP_WIDTH = HEAD_GROUP * HEAD_SIZE
EARLY = 2
WINDOW = REACH + LOC
SENT = PAIR + 16
SCORE_BASE2 = 1.4426950408889634 * HEAD_SIZE ** (-0.5)
BF16 = jnp.bfloat16
F32 = jnp.float32
PARAMS = dict(vmem_limit_bytes=60 << 20)


def whole(shape):
    return pl.BlockSpec(shape, lambda *_: (0,) * len(shape))


def iota(shape, dim):
    return lax.broadcasted_iota(jnp.int32, shape, dim)


def order_rows(col, row):
    same = (col // RANK_POSITIONS) == (row // RANK_POSITIONS)
    earlier = iota((LOC, LOC), 0) < iota((LOC, LOC), 1)
    order = jnp.sum((same & earlier).astype(jnp.int32), axis=0, keepdims=True)
    return row // RANK_POSITIONS, order


def order_cols(col, row):
    same = (col // RANK_POSITIONS) == (row // RANK_POSITIONS)
    earlier = iota((LOC, LOC), 1) < iota((LOC, LOC), 0)
    order = jnp.sum((same & earlier).astype(jnp.int32), axis=1, keepdims=True)
    return col // RANK_POSITIONS, order


def onehot(mask):
    return jnp.where(mask, F32(1), F32(0)).astype(BF16)


def pick(mask, values):
    return jnp.dot(onehot(mask), values, preferred_element_type=F32).astype(BF16)


def pack_queries_kernel(col_ref, row_ref, q_ref, early_ref, late_ref, hot):
    step = pl.program_id(0)

    @pl.when(step == 0)
    def _():
        target, order = order_rows(col_ref[...], row_ref[...])
        hot[...] = onehot(iota((SLOTS, LOC), 0) == target * CAPACITY + order)
        code = jnp.broadcast_to(col_ref[...] % LOC + 1, (LOC, CODE_WIDTH)).astype(F32).astype(BF16)
        early_ref[:, EARLY * GROUP_WIDTH :] = jnp.dot(
            hot[...], code, preferred_element_type=F32
        ).astype(BF16)

    packed = jnp.dot(hot[...], q_ref[...], preferred_element_type=F32).astype(BF16)
    for group in range(KEY_VALUE_HEADS):
        ref, first = (early_ref, 0) if group < EARLY else (late_ref, EARLY)

        @pl.when(step == group)
        def _(ref=ref, first=first, group=group):
            ref[:, (group - first) * GROUP_WIDTH : (group - first + 1) * GROUP_WIDTH] = packed


def pack_queries(col, row, queries):
    widths = (EARLY * GROUP_WIDTH + CODE_WIDTH, (KEY_VALUE_HEADS - EARLY) * GROUP_WIDTH)
    return pl.pallas_call(
        pack_queries_kernel,
        grid=(KEY_VALUE_HEADS,),
        in_specs=[
            whole((LOC, 1)),
            whole((1, LOC)),
            pl.BlockSpec((LOC, GROUP_WIDTH), lambda i: (0, i)),
        ],
        out_specs=[whole((SLOTS, w)) for w in widths],
        out_shape=[jax.ShapeDtypeStruct((SLOTS, w), BF16) for w in widths],
        scratch_shapes=[pltpu.VMEM((SLOTS, LOC), BF16)],
        compiler_params=pltpu.CompilerParams(**PARAMS),
        cost_estimate=pl.CostEstimate(
            flops=2 * SLOTS * LOC * QUERY_WIDTH, bytes_accessed=4 << 20, transcendentals=0
        ),
        name="pack_queries",
    )(col, row, queries)


def row_places_kernel(core_ref, col_ref, row_ref, sib_col_ref, sib_row_ref, out_ref):
    core = core_ref[0]
    for n, (col, row, k) in enumerate(((col_ref, row_ref, core), (sib_col_ref, sib_row_ref, 1 - core))):
        target, order = order_rows(col[...], row[...])
        slot = target * (2 * CAPACITY) + k * CAPACITY + order
        out_ref[:, n * LOC : (n + 1) * LOC] = onehot(iota((2 * SLOTS, LOC), 0) == slot)


def row_places(core, col, row, sib_col, sib_row):
    return pl.pallas_call(
        row_places_kernel,
        in_specs=[pl.BlockSpec(memory_space=pltpu.SMEM)] + [pl.BlockSpec(memory_space=pltpu.VMEM)] * 4,
        out_shape=jax.ShapeDtypeStruct((2 * SLOTS, PAIR), BF16),
        compiler_params=pltpu.CompilerParams(**PARAMS),
        cost_estimate=pl.CostEstimate(
            flops=2 * SLOTS * PAIR * 8, bytes_accessed=1 << 20, transcendentals=0
        ),
        name="row_places",
    )(core, col, row, sib_col, sib_row)


def project_kernel(
    table_ref, hot_ref, gain_ref, x_ref, sib_ref, w0, w1, w2, w3, out_ref, weight, acc, sems
):
    step = pl.program_id(0)
    core = table_ref[8]
    sources = (w0, w1, w2, w3)

    def copy(source, i, x, y):
        return pltpu.make_async_copy(
            source.at[pl.ds(i * RUN, RUN), :],
            weight.at[
                pl.ds(pl.multiple_of(x * RUN, RUN), RUN),
                pl.ds(pl.multiple_of(y * HEAD_SIZE, HEAD_SIZE), HEAD_SIZE),
            ],
            sems.at[x, y],
        )

    @pl.when(step == 0)
    def _():
        @pl.when(core == 0)
        def _():
            for i in range(4):
                for j in range(4):
                    copy(sources[j], i, table_ref[i], table_ref[4 + j]).start()

        @pl.when(core != 0)
        def _():
            for j in range(4):
                for i in range(4):
                    copy(sources[j], i, table_ref[j], table_ref[4 + i]).start()

    x = table_ref[step]
    for y in range(4):
        copy(w0, 0, x, y).wait()
    w = weight[pl.ds(pl.multiple_of(x * RUN, RUN), RUN), :]
    for n, ref in enumerate((x_ref, sib_ref)):
        now = jnp.dot(ref[...], w, preferred_element_type=F32)
        part = slice(n * LOC, (n + 1) * LOC)

        @pl.when(step == 0)
        def _(now=now, part=part):
            acc[part, :] = now

        @pl.when(step > 0)
        def _(now=now, part=part):
            acc[part, :] += now

    @pl.when(step == 3)
    def _():
        is_key = core == 0
        raw = acc[...]
        level = lax.rsqrt(jnp.mean(raw * raw, axis=-1, keepdims=True) + 1e-06)
        level = jnp.where(is_key, level, F32(1))
        gain = jnp.where(is_key, gain_ref[...], F32(1))
        done = (raw * level * gain).astype(BF16)
        out_ref[...] = jnp.dot(hot_ref[...], done, preferred_element_type=F32).astype(BF16)


def project(table, hot, gain, rows, sib_rows, weights):
    across = pl.BlockSpec((LOC, RUN), lambda t, table: (0, table[t]))
    return pl.pallas_call(
        project_kernel,
        grid_spec=pltpu.PrefetchScalarGridSpec(
            num_scalar_prefetch=1,
            grid=(4,),
            in_specs=[
                whole((2 * SLOTS, PAIR)),
                whole((1, ROW_WIDTH)),
                across,
                across,
            ]
            + [pl.BlockSpec(memory_space=pl.ANY)] * 4,
            out_specs=whole((2 * SLOTS, ROW_WIDTH)),
            scratch_shapes=[
                pltpu.VMEM((WIDTH, ROW_WIDTH), BF16),
                pltpu.VMEM((PAIR, ROW_WIDTH), F32),
                pltpu.SemaphoreType.DMA((4, 4)),
            ],
        ),
        out_shape=jax.ShapeDtypeStruct((2 * SLOTS, ROW_WIDTH), BF16),
        compiler_params=pltpu.CompilerParams(**PARAMS),
        cost_estimate=pl.CostEstimate(
            flops=2 * PAIR * WIDTH * ROW_WIDTH, bytes_accessed=12 << 20, transcendentals=0
        ),
        name="project",
    )(table, hot, gain, rows, sib_rows, *weights)


def places_kernel(core_ref, own_ref, sib_ref, out_ref):
    for n, code in enumerate((own_ref, sib_ref)):
        k = core_ref[0] if n == 0 else 1 - core_ref[0]
        row = code[...].astype(F32).T[0:1].astype(jnp.int32) - 1
        out_ref[k] = onehot(iota((LOC, SLOTS), 0) == row)


def places(core, own_code, sib_code):
    return pl.pallas_call(
        places_kernel,
        in_specs=[pl.BlockSpec(memory_space=pltpu.SMEM)] + [pl.BlockSpec(memory_space=pltpu.VMEM)] * 2,
        out_shape=jax.ShapeDtypeStruct((2, LOC, SLOTS), BF16),
        compiler_params=pltpu.CompilerParams(**PARAMS),
        cost_estimate=pl.CostEstimate(flops=SLOTS * LOC * 8, bytes_accessed=1 << 20, transcendentals=0),
        name="places",
    )(core, own_code, sib_code)


def unpack_queries_kernel(core_ref, hot_ref, q_ref, out_ref):
    out_ref[...] = jnp.dot(hot_ref[core_ref[0]], q_ref[...], preferred_element_type=F32).astype(BF16)


def unpack_queries(core, hots, got, groups):
    return pl.pallas_call(
        unpack_queries_kernel,
        grid=(groups,),
        in_specs=[
            pl.BlockSpec(memory_space=pltpu.SMEM),
            whole((2, LOC, SLOTS)),
            pl.BlockSpec((SLOTS, GROUP_WIDTH), lambda i: (0, i)),
        ],
        out_specs=pl.BlockSpec((LOC, GROUP_WIDTH), lambda i: (0, i)),
        out_shape=jax.ShapeDtypeStruct((LOC, groups * GROUP_WIDTH), BF16),
        compiler_params=pltpu.CompilerParams(**PARAMS),
        cost_estimate=pl.CostEstimate(
            flops=2 * SLOTS * LOC * groups * GROUP_WIDTH, bytes_accessed=4 << 20, transcendentals=0
        ),
        name="unpack_queries",
    )(core, hots, got)


def unpack_kernel(hot_ref, seg_ref, got_ref, out_ref):
    got = got_ref[...].reshape(RANKS, 2, CAPACITY, ROW_WIDTH)
    for k in range(2):
        part = got[:, k].reshape(SLOTS, ROW_WIDTH)
        out_ref[k * LOC : (k + 1) * LOC, :] = jnp.dot(
            hot_ref[k], part, preferred_element_type=F32
        ).astype(BF16)
    out_ref[PAIR:SENT, :] = jnp.broadcast_to(seg_ref[...].astype(F32).astype(BF16), (16, PAIR))


def unpack(hots, seg, got):
    return pl.pallas_call(
        unpack_kernel,
        out_shape=jax.ShapeDtypeStruct((SENT, ROW_WIDTH), BF16),
        compiler_params=pltpu.CompilerParams(**PARAMS),
        cost_estimate=pl.CostEstimate(
            flops=2 * PAIR * SLOTS * ROW_WIDTH, bytes_accessed=3 << 20, transcendentals=0
        ),
        name="unpack",
    )(hots, seg, got)


def attend_kernel(
    where_ref, seg_ref, early_ref, late_ref, a0, a1, a2, b0, b1, b2, out_ref, keys, values, bias, queries
):
    core = where_ref[0]
    ctx = where_ref[3]
    head = pl.program_id(0)

    @pl.when(head == 0)
    def _():
        @pl.when(core == 0)
        def _():
            for dst, (s0, s1, s2) in ((keys, (a0, a1, a2)), (values, (b0, b1, b2))):
                dst[0:PAIR, :] = s2[0:PAIR, :]
                dst[PAIR : 2 * PAIR, :] = s1[0:PAIR, :]
                dst[2 * PAIR : WINDOW, :] = s0[0:LOC, :]

        @pl.when(core != 0)
        def _():
            for dst, (s0, s1, s2) in ((keys, (b0, b1, b2)), (values, (a0, a1, a2))):
                dst[0:LOC, :] = s2[LOC:PAIR, :]
                dst[LOC : LOC + PAIR, :] = s1[0:PAIR, :]
                dst[LOC + PAIR : WINDOW, :] = s0[0:PAIR, :]

        segs = [a[PAIR:SENT, :][0:1].astype(F32) for a in (a2, a1, a0)]
        left = jnp.concatenate([segs[0], segs[1], segs[2][:, 0:LOC]], axis=1)
        right = jnp.concatenate([segs[0][:, LOC:PAIR], segs[1], segs[2]], axis=1)
        key_seg = jnp.where(core == 0, left, right)
        query_seg = seg_ref[...].astype(F32)
        k = iota((LOC, WINDOW), 1)
        q = iota((LOC, WINDOW), 0)
        allowed = (k <= q + REACH) & (k >= REACH - ctx * LOC) & (key_seg == query_seg)
        bias[...] = jnp.where(allowed, F32(0), F32(-1e30))

    @pl.when(head < EARLY)
    def _():
        queries[...] = early_ref[...]

    @pl.when(head >= EARLY)
    def _():
        queries[...] = late_ref[...]

    columns = pl.ds(pl.multiple_of(head * HEAD_SIZE, HEAD_SIZE), HEAD_SIZE)
    key_rows = keys[:, columns]
    value_rows = values[:, columns]
    value_rows = jnp.concatenate([value_rows, jnp.ones_like(value_rows)], axis=1)
    for g in range(HEAD_GROUP):
        cols = slice(g * HEAD_SIZE, (g + 1) * HEAD_SIZE)
        scores = lax.dot_general(
            queries[:, cols], key_rows, (((1,), (1,)), ((), ())), preferred_element_type=F32
        )
        scores = scores + bias[...]
        best = jnp.max(scores, axis=-1, keepdims=True)
        p = jnp.exp2((scores - best) * SCORE_BASE2).astype(BF16)
        summed = jnp.dot(p, value_rows, preferred_element_type=F32)
        out_ref[:, cols] = (summed[:, :HEAD_SIZE] / summed[:, HEAD_SIZE:]).astype(BF16)


def attend(where, seg_col, early, late, mine, other):
    return pl.pallas_call(
        attend_kernel,
        grid=(KEY_VALUE_HEADS,),
        in_specs=[
            pl.BlockSpec(memory_space=pltpu.SMEM),
            whole((LOC, 1)),
            pl.BlockSpec((LOC, GROUP_WIDTH), lambda i: (0, jnp.minimum(i, EARLY - 1))),
            pl.BlockSpec((LOC, GROUP_WIDTH), lambda i: (0, jnp.maximum(i - EARLY, 0))),
        ]
        + [whole((SENT, ROW_WIDTH))] * 6,
        out_specs=pl.BlockSpec((LOC, GROUP_WIDTH), lambda i: (0, i)),
        out_shape=jax.ShapeDtypeStruct((LOC, QUERY_WIDTH), BF16),
        scratch_shapes=[
            pltpu.VMEM((WINDOW, ROW_WIDTH), BF16),
            pltpu.VMEM((WINDOW, ROW_WIDTH), BF16),
            pltpu.VMEM((LOC, WINDOW), F32),
            pltpu.VMEM((LOC, GROUP_WIDTH), BF16),
        ],
        compiler_params=pltpu.CompilerParams(**PARAMS),
        cost_estimate=pl.CostEstimate(
            flops=4 * LOC * WINDOW * QUERY_WIDTH,
            bytes_accessed=8 << 20,
            transcendentals=LOC * WINDOW * QUERY_HEADS,
        ),
        name="attend",
    )(where, seg_col, early, late, *mine, *other)


def chips():
    return [(x, y, z, k) for x in range(4) for z in range(8) for y in range(4) for k in range(2)]


def device(x, y, z, k):
    return (x % 4 * 8 + z % 8) * 8 + y % 4 * 2 + k


def shift(array, moved):
    pairs = [(device(*c), device(*moved(*c))) for c in chips()]
    return lax.ppermute(array, ("dp", "ctx"), pairs)


def swap_cores(array):
    return shift(array, lambda x, y, z, k: (x, y, z, 1 - k))


def send_up(array, by):
    pairs = [(device(*c), device(c[0], c[1] + by, c[2], c[3])) for c in chips() if c[1] + by < 4]
    return lax.ppermute(array, ("dp", "ctx"), pairs)


def along_z(array):
    groups = [[device(x, y, z, k) for z in range(8)] for x in range(4) for y in range(4) for k in range(2)]
    copies = jnp.broadcast_to(array[None], (8,) + array.shape)
    got = lax.all_to_all(copies, ("dp", "ctx"), 0, 0, axis_index_groups=groups, tiled=True)
    return got.reshape(8 * array.shape[0], array.shape[1])


def along_first(array, by):
    return shift(array, lambda x, y, z, k: (x + by, y, z, k) if k == 0 else (x, y + by, z, k))


def along_second(array, by):
    return shift(array, lambda x, y, z, k: (x, y + by, z, k) if k == 0 else (x + by, y, z, k))


def move(slots, rows):
    width = slots.shape[1]
    sent = slots.reshape(RANKS, rows, width)
    return lax.all_to_all(sent, "dp", split_axis=0, concat_axis=0, tiled=True).reshape(RANKS * rows, width)


def body(gen_rows, gen_queries, place, segment, key_value_weight, key_norm_gain):
    ctx = lax.axis_index("ctx")
    core, chip_y = ctx % 2, ctx // 2
    chip_x = lax.axis_index("dp") // 8
    where = jnp.stack([core, chip_x, chip_y, ctx])
    core_s = core.reshape(1)
    seg = segment.reshape(LOC)
    col, row = place.reshape(LOC, 1), place.reshape(1, LOC)

    part = lax.dynamic_slice_in_dim(
        key_value_weight, core * ROW_WIDTH + chip_y * HEAD_SIZE, HEAD_SIZE, 1
    )
    run = along_z(part)
    early_slots, late_slots = pack_queries(col, row, gen_queries)
    line = jnp.concatenate([run] + [along_first(run, -by) for by in NEAR[1:]])
    early_slots, line = lax.optimization_barrier((early_slots, line))
    got_early = move(early_slots, CAPACITY)

    sib = swap_cores(jnp.stack([place, seg]))
    sib_rows = swap_cores(gen_rows)
    sib_col, sib_row = sib[0].reshape(LOC, 1), sib[0].reshape(1, LOC)
    pair_seg = jnp.where(core == 0, jnp.concatenate([seg, sib[1]]), jnp.concatenate([sib[1], seg]))
    pair_seg = pair_seg.reshape(1, PAIR)

    weights = [line] + [along_second(line, -by) for by in NEAR[1:]]
    hot = row_places(core_s, col, row, sib_col, sib_row)
    near = jnp.array(NEAR)
    table = jnp.concatenate([(chip_x + near) % 4, (chip_y + near) % 4, core_s])
    slots = project(table, hot, key_norm_gain.reshape(1, ROW_WIDTH), gen_rows, sib_rows, weights)
    slots, got_early = lax.optimization_barrier((slots, got_early))
    got = move(slots, 2 * CAPACITY)
    own_code = got_early[:, EARLY * GROUP_WIDTH :]
    hots = places(core_s, own_code, swap_cores(own_code))
    early = unpack_queries(core_s, hots, got_early, EARLY)
    got, early, hots = lax.optimization_barrier((got, early, hots))
    own = unpack(hots, pair_seg, got)
    late_slots, own = lax.optimization_barrier((late_slots, own))
    up = [send_up(own, 1), send_up(own, 2)]
    got_late = move(late_slots, CAPACITY)
    late = unpack_queries(core_s, hots, got_late, KEY_VALUE_HEADS - EARLY)
    other = [swap_cores(m) for m in [own] + up]
    return attend(where, seg.reshape(LOC, 1), early, late, [own] + up, other)


def solution(mesh):
    placed = (
        P(("dp", "ctx"), None),
        P(("dp", "ctx"), None),
        P(("dp", "ctx")),
        P("dp", "ctx"),
        P("dp", None),
        P(),
    )
    return jax.shard_map(
        body, mesh=mesh, in_specs=placed, out_specs=P(("dp", "ctx"), None), check_vma=False
    )
```

time: 226 us -> 180 us (0.80); the launches traced: 223 us -> 179 us
  waiting for transfers between devices: 93.7 us -> 68 us
  Pallas kernels: 28.8 us -> 43.2 us
  between operations: 13.6 us -> 0.2 us
  starting transfers between devices: 47.7 us -> 38.1 us
  blocking collectives: 26.7 us -> 20.5 us
  local copies, waits for them, and re-layouts: 10.6 us -> 7.39 us
    all_gather x1 -> x0, waiting for transfers between devices: 62.5 us -> none  [body(): weight = lax.all_gather(half, 'dp', axis=0, tiled=True)]
    ppermute x7 -> x14, waiting for transfers between devices: 4.32 us -> 49.7 us  [the longest x12 37.3 us: shift(): return lax.ppermute(array, ('dp', 'ctx'), pairs)]
    pallas_call x2 -> x6, Pallas kernels: 10.1 us -> 25.9 us  [the longest x1 10.3 us: project(): pl.pallas_call(project_kernel, grid_spec=pltpu.PrefetchScalarGridSpec(num...]
    all_to_all x2 -> x3, waiting for transfers between devices: 26.9 us -> 18.3 us  [move(): lax.all_to_all(sent, 'dp', split_axis=0, concat_axis=0, tiled=True)]
    ppermute x7 -> x14, starting transfers between devices: 29.5 us -> 21.6 us  [the longest x12 14 us: shift(): return lax.ppermute(array, ('dp', 'ctx'), pairs)]
    all_to_all x1, blocking collectives: 26.7 us -> 20.5 us  [along_z(): lax.all_to_all(copies, ('dp', 'ctx'), 0, 0, axis_index_groups=groups, til...]
    unnamed x18 -> x24, local copies, waits for them, and re-layouts: 7.38 us -> 3.72 us
    pallas_call x1, Pallas kernels: 17.2 us -> 14.7 us  [attend(): pl.pallas_call(attend_kernel, grid=(KEY_VALUE_HEADS,), in_specs=[pl.Block...]
  transfers between devices with their start and end apart: 10 -> 17, of which waited for: 4 -> 8; matrix products, arithmetic and copies ran while one was open for 2% -> 3% of each run, Pallas kernels for 5% -> 14%
where the time goes in v2:
time: 180 us; the launch traced here: 179 us
  waiting for transfers between devices  68 us (38%)
  Pallas kernels  43.2 us (24%)
  starting transfers between devices  38.1 us (21%)
  blocking collectives  20.5 us (11%)
  local copies, waits for them, and re-layouts  7.39 us (4%)
  other arithmetic  2.01 us (1%)
    ppermute x12, waiting for transfers between devices, shift(): return lax.ppermute(array, ('dp', 'ctx'), pairs)  37.3 us
    all_to_all x1, blocking collectives, along_z(): lax.all_to_all(copies, ('dp', 'ctx'), 0, 0, axis_index_groups=groups, til...  20.5 us
    all_to_all x3, waiting for transfers between devices, move(): lax.all_to_all(sent, 'dp', split_axis=0, concat_axis=0, tiled=True)  18.3 us
    all_to_all x3, starting transfers between devices, move(): lax.all_to_all(sent, 'dp', split_axis=0, concat_axis=0, tiled=True)  16.5 us
    pallas_call x1, Pallas kernels, attend(): pl.pallas_call(attend_kernel, grid=(KEY_VALUE_HEADS,), in_specs=[pl.Block...  14.7 us
    ppermute x12, starting transfers between devices, shift(): return lax.ppermute(array, ('dp', 'ctx'), pairs)  14 us
    ppermute x2, waiting for transfers between devices, send_up(): return lax.ppermute(array, ('dp', 'ctx'), pairs)  12.4 us
    pallas_call x1, Pallas kernels, project(): pl.pallas_call(project_kernel, grid_spec=pltpu.PrefetchScalarGridSpec(num...  10.3 us
  transfers between devices with their start and end apart: 17, of which 8 were waited for; matrix products, arithmetic and copies ran while one was open for 3% of the time, Pallas kernels for 14%

profile of v2, /device:TPU:1, one launch (start us, length us, event | category | flops | bytes accessed | tf_op | source)
XLA Modules:
  0.0 179.4 jit_solution(13814964500913732820)
XLA Ops:
  0.0 1.0 copy-done
  1.0 20.5 %all_to_all.20 = bf16[8,160,128]{2,1,0:T(8,128)(2,1)S(1)} all-to-all(bf16[8,160,128]{2,1,0:T(8,128)(2,1)S(1)} %broadcast_in_dim.2), channel_id=1, replica_groups={{0,8,16,24,32,40,48,56},{1,9,17,25,33,41,49,57},{2,10,18,26,34,42,50,58..., dimensions={0} | all-to-all | bytes 655360 | tf_op jit(solution)/shard_map/all_to_all | solution.py:392
  21.5 1.3 collective-permute-start.2
  22.8 1.4 collective-permute-start.3
  24.3 1.6 collective-permute-start.4
  25.9 3.2 %collective-permute-start.1 = (bf16[256,5120]{1,0:T(8,128)(2,1)}, bf16[256,5120]{1,0:T(8,128)(2,1)}, u32[]{:S(2)}, u32[]{:S(2)}) collective-permute-start(bf16[256,5120]{1,0:T(8,128)(2,1)} %x_ref.1), channel_id=1, source_target_pairs={{0,1},{1,0},{2,3},{3,2},{4,5},{5,4},{6,7},{7,6},{8,9},{9,8},{10,11... | collective-permute-start | bytes 7864328 | tf_op jit(solution)/shard_map/ppermute | solution.py:377
  29.1 1.5 copy.8.col_ref
  30.6 5.3 %pack_queries.1 = (bf16[512,1408]{1,0:T(8,128)(2,1)}, bf16[512,1280]{1,0:T(8,128)(2,1)}) custom-call(s32[256,1]{1,0:T(8,128)} %copy.8.col_ref, s32[1,256]{1,0:T(1,128)} %bitcast.29, bf16[256,2560]{1,0:T(8,128)(2,1)} %q_ref.1), custom_call_target="tpu_custom_call" | custom-call | flops 671088640 | bytes 4194304 | tf_op jit(solution)/shard_map/pack_queries/pallas_call | solution.py:90
  35.9 0.0 collective-permute-done.2
  36.0 0.1 pad_maximum_fusion.w0
  36.1 0.0 copy-start.8
  36.1 0.0 copy-start.9
  36.1 0.0 copy-start.10
  36.1 4.1 %all-to-all-start.1 = ((bf16[32,16,1408]{2,1,0:T(8,128)(2,1)}), bf16[32,16,1408]{2,1,0:T(8,128)(2,1)S(1)}, u32[]{:S(2)}, u32[]{:S(2)}) async-start(bf16[32,16,1408]{2,1,0:T(8,128)(2,1)} %bitcast.22), calls=%async_computation.1 | async-start | bytes 2883584 | tf_op jit(solution)/shard_map/all_to_all | solution.py:407
  40.2 1.2 collective-permute-start.5
  41.5 1.5 collective-permute-start.6
  43.0 1.5 collective-permute-start.7
  44.5 2.0 %collective-permute-start = (s32[2,256]{1,0:T(2,128)S(1)}, s32[2,256]{1,0:T(2,128)S(1)}, u32[]{:S(2)}, u32[]{:S(2)}) collective-permute-start(s32[2,256]{1,0:T(2,128)S(1)} %pad_add_fusion), channel_id=1, source_target_pairs={{0,1},{1,0},{2,3},{3,2},{4,5},{5,4},{6,7},{7,6},{8,9},{9,8},{10,11... | collective-permute-start | bytes 6152 | tf_op jit(solution)/shard_map/ppermute | solution.py:377
  46.5 0.7 pad_add_fusion.2.table_ref
  47.2 0.2 collective-permute-done
  47.3 0.5 fusion.2
  47.9 0.8 copy.9.sib_col_ref
  48.7 2.6 %row_places.1.hot_ref = bf16[1024,512]{1,0:T(8,128)(2,1)} custom-call(s32[1]{0:T(128)} %bitcast.core_ref, s32[256,1]{1,0:T(8,128)} %copy.8.col_ref, s32[1,256]{1,0:T(1,128)} %bitcast.30, s32[256,1]{1,0:T(8,128)} %copy.9.sib_col_ref, s32[1,256]{1,0:T(1,128)} %get-tuple-element.29.sib_row_ref), custom_call_target="tpu_custom_call" | custom-call | flops 4194304 | bytes 1048576 | tf_op jit(solution)/shard_map/row_places/pallas_call | solution.py:118
  51.3 20.8 %collective-permute-done.5.w1 = bf16[5120,128]{1,0:T(8,128)(2,1)} collective-permute-done((bf16[5120,128]{1,0:T(8,128)(2,1)S(1)}, bf16[5120,128]{1,0:T(8,128)(2,1)}, u32[]{:S(2)}, u32[]{:S(2)}) %collective-permute-start.5) | collective-permute-done | bytes 1310752 | tf_op jit(solution)/shard_map/ppermute | solution.py:377
  72.1 15.6 %collective-permute-done.7.w3 = bf16[5120,128]{1,0:T(8,128)(2,1)} collective-permute-done((bf16[5120,128]{1,0:T(8,128)(2,1)S(1)}, bf16[5120,128]{1,0:T(8,128)(2,1)}, u32[]{:S(2)}, u32[]{:S(2)}) %collective-permute-start.7) | collective-permute-done | bytes 1310752 | tf_op jit(solution)/shard_map/ppermute | solution.py:377
  87.7 10.3 %project.1 = bf16[1024,512]{1,0:T(8,128)(2,1)} custom-call(s32[9]{0:T(128)} %pad_add_fusion.2.table_ref, bf16[1024,512]{1,0:T(8,128)(2,1)} %row_places.1.hot_ref, f32[1,512]{1,0:T(1,128)} %bitcast.33, bf16[256,5120]{1,0:T(8,128)(2,1)} %x_ref.1, bf16[256,5120]{1,0:T(8,128)(2,1)} %collective-permute-done.1.sib_ref, bf16[5120,128]{1,0:T(8,128)(2,1)} %copy-done.3, ...), custom_call_target="tpu_custom_call" | custom-call | flops 2684354560 | bytes 12582912 | tf_op jit(solution)/shard_map/project/pallas_call | solution.py:190
  98.1 7.7 %all-to-all-start.2 = ((bf16[32,32,512]{2,1,0:T(8,128)(2,1)}), bf16[32,32,512]{2,1,0:T(8,128)(2,1)S(1)}, u32[]{:S(2)}, u32[]{:S(2)}) async-start(bf16[32,32,512]{2,1,0:T(8,128)(2,1)} %bitcast.21), calls=%async_computation.2 | async-start | bytes 2097152 | tf_op jit(solution)/shard_map/all_to_all | solution.py:407
  105.8 0.1 collective-permute-start.8
  105.9 0.6 broadcast_select_fusion.seg_ref
  106.5 0.7 collective-permute-done.8.sib_ref
  107.2 0.7 copy-done.7
  107.9 2.1 %places.1.hot_ref = bf16[2,256,512]{2,1,0:T(8,128)(2,1)} custom-call(s32[1]{0:T(128)} %bitcast.core_ref, bf16[512,128]{1,0:T(8,128)(2,1)} %copy-done.6, bf16[512,128]{1,0:T(8,128)(2,1)} %copy-done.7), custom_call_target="tpu_custom_call" | custom-call | flops 1048576 | bytes 1048576 | tf_op jit(solution)/shard_map/places/pallas_call | solution.py:226
  110.0 2.7 %unpack_queries.2.early_ref = bf16[256,1280]{1,0:T(8,128)(2,1)} custom-call(s32[1]{0:T(128)} %bitcast.core_ref, bf16[2,256,512]{2,1,0:T(8,128)(2,1)} %places.1.hot_ref, bf16[512,1408]{1,0:T(8,128)(2,1)} %bitcast.18), custom_call_target="tpu_custom_call" | custom-call | flops 335544320 | bytes 4194304 | tf_op jit(solution)/shard_map/unpack_queries/pallas_call | solution.py:241
  112.7 12.5 %all-to-all-done.2 = bf16[32,32,512]{2,1,0:T(8,128)(2,1)S(1)} async-done(((bf16[32,32,512]{2,1,0:T(8,128)(2,1)}), bf16[32,32,512]{2,1,0:T(8,128)(2,1)S(1)}, u32[]{:S(2)}, u32[]{:S(2)}) %all-to-all-start.2) | async-done | bytes 1048608 | tf_op jit(solution)/shard_map/all_to_all | solution.py:407
  125.2 1.0 copy-done.4
  126.2 2.6 %unpack.1.a0 = bf16[528,512]{1,0:T(8,128)(2,1)} custom-call(bf16[2,256,512]{2,1,0:T(8,128)(2,1)} %places.1.hot_ref, s32[1,512]{1,0:T(1,128)} %broadcast_select_fusion.seg_ref, bf16[1024,512]{1,0:T(8,128)(2,1)} %bitcast.20), custom_call_target="tpu_custom_call" | custom-call | flops 268435456 | bytes 3145728 | tf_op jit(solution)/shard_map/unpack/pallas_call | solution.py:270
  128.8 4.7 %all-to-all-start.3 = ((bf16[32,16,1280]{2,1,0:T(8,128)(2,1)}), bf16[32,16,1280]{2,1,0:T(8,128)(2,1)S(1)}, u32[]{:S(2)}, u32[]{:S(2)}) async-start(bf16[32,16,1280]{2,1,0:T(8,128)(2,1)} %bitcast.27), calls=%async_computation.3 | async-start | bytes 2621440 | tf_op jit(solution)/shard_map/all_to_all | solution.py:407
  133.5 3.1 %collective-permute-start.9 = (bf16[528,512]{1,0:T(8,128)(2,1)S(1)}, bf16[528,512]{1,0:T(8,128)(2,1)S(1)}, u32[]{:S(2)}, u32[]{:S(2)}) collective-permute-start(bf16[528,512]{1,0:T(8,128)(2,1)S(1)} %copy-done.5), channel_id=1, source_target_pairs={{0,2},{1,3},{2,4},{3,5},{4,6},{5,7},{8,10},{9,11},{10,12},{11,13},... | collective-permute-start | bytes 1622024 | tf_op jit(solution)/shard_map/ppermute | solution.py:386
  136.6 4.5 %collective-permute-start.10 = (bf16[528,512]{1,0:T(8,128)(2,1)S(1)}, bf16[528,512]{1,0:T(8,128)(2,1)}, u32[]{:S(2)}, u32[]{:S(2)}) collective-permute-start(bf16[528,512]{1,0:T(8,128)(2,1)S(1)} %copy-done.5), channel_id=1, source_target_pairs={{0,4},{1,5},{2,6},{3,7},{8,12},{9,13},{10,14},{11,15},{16,20},{17,... | collective-permute-start | bytes 1622024 | tf_op jit(solution)/shard_map/ppermute | solution.py:386
  141.2 0.0 collective-permute-start.11
  141.2 6.6 %collective-permute-done.9.a1 = bf16[528,512]{1,0:T(8,128)(2,1)S(1)} collective-permute-done((bf16[528,512]{1,0:T(8,128)(2,1)S(1)}, bf16[528,512]{1,0:T(8,128)(2,1)S(1)}, u32[]{:S(2)}, u32[]{:S(2)}) %collective-permute-start.9) | collective-permute-done | bytes 540704 | tf_op jit(solution)/shard_map/ppermute | solution.py:386
  147.7 5.8 %collective-permute-done.10.a2 = bf16[528,512]{1,0:T(8,128)(2,1)} collective-permute-done((bf16[528,512]{1,0:T(8,128)(2,1)S(1)}, bf16[528,512]{1,0:T(8,128)(2,1)}, u32[]{:S(2)}, u32[]{:S(2)}) %collective-permute-start.10) | collective-permute-done | bytes 540704 | tf_op jit(solution)/shard_map/ppermute | solution.py:386
  153.5 0.8 copy.11.seg_ref
  154.3 0.7 pad_add_fusion.1.where_ref
  155.0 5.8 %all-to-all-done.3 = bf16[32,16,1280]{2,1,0:T(8,128)(2,1)S(1)} async-done(((bf16[32,16,1280]{2,1,0:T(8,128)(2,1)}), bf16[32,16,1280]{2,1,0:T(8,128)(2,1)S(1)}, u32[]{:S(2)}, u32[]{:S(2)}) %all-to-all-start.3) | async-done | bytes 1310752 | tf_op jit(solution)/shard_map/all_to_all | solution.py:407
  160.8 1.1 copy-done.2
  161.9 2.7 %unpack_queries.3.late_ref = bf16[256,1280]{1,0:T(8,128)(2,1)} custom-call(s32[1]{0:T(128)} %bitcast.core_ref, bf16[2,256,512]{2,1,0:T(8,128)(2,1)} %places.1.hot_ref, bf16[512,1280]{1,0:T(8,128)(2,1)} %bitcast.19), custom_call_target="tpu_custom_call" | custom-call | flops 335544320 | bytes 4194304 | tf_op jit(solution)/shard_map/unpack_queries/pallas_call | solution.py:241
  164.6 14.7 %attend.1 = bf16[256,2560]{1,0:T(8,128)(2,1)} custom-call(s32[4]{0:T(128)} %pad_add_fusion.1.where_ref, s32[256,1]{1,0:T(8,128)} %copy.11.seg_ref, bf16[256,1280]{1,0:T(8,128)(2,1)} %unpack_queries.2.early_ref, bf16[256,1280]{1,0:T(8,128)(2,1)} %unpack_queries.3.late_ref, bf16[528,512]{1,0:T(8,128)(2,1)} %unpack.1.a0, bf16[528,512]{1,0:T(8,128)(2,1)} %copy-done.11, ...), custom_call_target="tpu_custom_call" | custom-call | flops 3355443200 | bytes 8388608 | tf_op jit(solution)/shard_map/attend/pallas_call | solution.py:339
  (32 shorter events, 0.1 us)
Async XLA Ops:
  0.0 1.0 copy-start
  21.5 14.4 %collective-permute-start.2 = (bf16[1280,128]{1,0:T(8,128)(2,1)S(1)}, bf16[1280,128]{1,0:T(8,128)(2,1)S(1)}, u32[]{:S(2)}, u32[]{:S(2)}) collective-permute-start(bf16[1280,128]{1,0:T(8,128)(2,1)S(1)} %bitcast.23), channel_id=1, source_target_pairs={{0,64},{1,3},{2,66},{3,5},{4,68},{5,7},{6,70},{7,1},{8,72},{9,11},... | collective-permute-start | bytes 983048 | tf_op jit(solution)/shard_map/ppermute | solution.py:377
  22.8 13.1 %collective-permute-start.3 = (bf16[1280,128]{1,0:T(8,128)(2,1)S(1)}, bf16[1280,128]{1,0:T(8,128)(2,1)S(1)}, u32[]{:S(2)}, u32[]{:S(2)}) collective-permute-start(bf16[1280,128]{1,0:T(8,128)(2,1)S(1)} %bitcast.24), channel_id=1, source_target_pairs={{0,192},{1,7},{2,194},{3,1},{4,196},{5,3},{6,198},{7,5},{8,200},{9... | collective-permute-start | bytes 983048 | tf_op jit(solution)/shard_map/ppermute | solution.py:377
  24.3 11.7 %collective-permute-start.4 = (bf16[1280,128]{1,0:T(8,128)(2,1)S(1)}, bf16[1280,128]{1,0:T(8,128)(2,1)S(1)}, u32[]{:S(2)}, u32[]{:S(2)}) collective-permute-start(bf16[1280,128]{1,0:T(8,128)(2,1)S(1)} %bitcast.25), channel_id=1, source_target_pairs={{0,128},{1,5},{2,130},{3,7},{4,132},{5,1},{6,134},{7,3},{8,136},{9... | collective-permute-start | bytes 983048 | tf_op jit(solution)/shard_map/ppermute | solution.py:377
  25.9 61.8 %collective-permute-start.1 = (bf16[256,5120]{1,0:T(8,128)(2,1)}, bf16[256,5120]{1,0:T(8,128)(2,1)}, u32[]{:S(2)}, u32[]{:S(2)}) collective-permute-start(bf16[256,5120]{1,0:T(8,128)(2,1)} %x_ref.1), channel_id=1, source_target_pairs={{0,1},{1,0},{2,3},{3,2},{4,5},{5,4},{6,7},{7,6},{8,9},{9,8},{10,11... | collective-permute-start | bytes 7864328 | tf_op jit(solution)/shard_map/ppermute | solution.py:377
  36.1 6.9 %copy-start.3 = (bf16[5120,128]{1,0:T(8,128)(2,1)}, bf16[5120,128]{1,0:T(8,128)(2,1)S(1)}, u32[]{:S(2)}) copy-start(bf16[5120,128]{1,0:T(8,128)(2,1)S(1)} %pad_maximum_fusion.w0) | copy-start | bytes 3932164
  36.1 8.4 %copy-start.8 = (s32[256]{0:T(256)S(1)}, s32[256]{0:T(256)}, u32[]{:S(2)}) copy-start(s32[256]{0:T(256)} %param.9) | copy-start | bytes 3076
  36.1 8.4 %copy-start.9 = (s32[1,256]{1,0:T(1,128)S(1)}, s32[1,256]{1,0:T(1,128)}, u32[]{:S(2)}) copy-start(s32[1,256]{1,0:T(1,128)} %param.10) | copy-start | bytes 3076
  36.1 10.4 %copy-start.10 = (s32[4]{0:T(128)S(1)}, s32[4]{0:T(128)}, u32[]{:S(2)}) copy-start(s32[4]{0:T(128)} %constant.71.clone) | copy-start | bytes 52
  36.1 62.0 %all-to-all-start.1 = ((bf16[32,16,1408]{2,1,0:T(8,128)(2,1)}), bf16[32,16,1408]{2,1,0:T(8,128)(2,1)S(1)}, u32[]{:S(2)}, u32[]{:S(2)}) async-start(bf16[32,16,1408]{2,1,0:T(8,128)(2,1)} %bitcast.22), calls=%async_computation.1 | async-start | bytes 2883584 | tf_op jit(solution)/shard_map/all_to_all | solution.py:407
  40.2 31.9 %collective-permute-start.5 = (bf16[5120,128]{1,0:T(8,128)(2,1)S(1)}, bf16[5120,128]{1,0:T(8,128)(2,1)}, u32[]{:S(2)}, u32[]{:S(2)}) collective-permute-start(bf16[5120,128]{1,0:T(8,128)(2,1)S(1)} %pad_maximum_fusion.w0), channel_id=1, source_target_pairs={{0,2},{1,65},{2,4},{3,67},{4,6},{5,69},{6,0},{7,71},{8,10},{9,73},... | collective-permute-start | bytes 3932168 | tf_op jit(solution)/shard_map/ppermute | solution.py:377
  41.5 30.7 %collective-permute-start.6 = (bf16[5120,128]{1,0:T(8,128)(2,1)S(1)}, bf16[5120,128]{1,0:T(8,128)(2,1)}, u32[]{:S(2)}, u32[]{:S(2)}) collective-permute-start(bf16[5120,128]{1,0:T(8,128)(2,1)S(1)} %pad_maximum_fusion.w0), channel_id=1, source_target_pairs={{0,6},{1,193},{2,0},{3,195},{4,2},{5,197},{6,4},{7,199},{8,14},{9,... | collective-permute-start | bytes 3932168 | tf_op jit(solution)/shard_map/ppermute | solution.py:377
  43.0 44.7 %collective-permute-start.7 = (bf16[5120,128]{1,0:T(8,128)(2,1)S(1)}, bf16[5120,128]{1,0:T(8,128)(2,1)}, u32[]{:S(2)}, u32[]{:S(2)}) collective-permute-start(bf16[5120,128]{1,0:T(8,128)(2,1)S(1)} %pad_maximum_fusion.w0), channel_id=1, source_target_pairs={{0,4},{1,129},{2,6},{3,131},{4,0},{5,133},{6,2},{7,135},{8,12},{9,... | collective-permute-start | bytes 3932168 | tf_op jit(solution)/shard_map/ppermute | solution.py:377
  44.5 2.8 %collective-permute-start = (s32[2,256]{1,0:T(2,128)S(1)}, s32[2,256]{1,0:T(2,128)S(1)}, u32[]{:S(2)}, u32[]{:S(2)}) collective-permute-start(s32[2,256]{1,0:T(2,128)S(1)} %pad_add_fusion), channel_id=1, source_target_pairs={{0,1},{1,0},{2,3},{3,2},{4,5},{5,4},{6,7},{7,6},{8,9},{9,8},{10,11... | collective-permute-start | bytes 6152 | tf_op jit(solution)/shard_map/ppermute | solution.py:377
  98.1 11.9 %copy-start.1 = (bf16[32,16,1408]{2,1,0:T(8,128)(2,1)}, bf16[32,16,1408]{2,1,0:T(8,128)(2,1)S(1)}, u32[]{:S(2)}) copy-start(bf16[32,16,1408]{2,1,0:T(8,128)(2,1)S(1)} %all-to-all-done.1) | copy-start | bytes 4325380
  98.1 27.1 %all-to-all-start.2 = ((bf16[32,32,512]{2,1,0:T(8,128)(2,1)}), bf16[32,32,512]{2,1,0:T(8,128)(2,1)S(1)}, u32[]{:S(2)}, u32[]{:S(2)}) async-start(bf16[32,32,512]{2,1,0:T(8,128)(2,1)} %bitcast.21), calls=%async_computation.2 | async-start | bytes 2097152 | tf_op jit(solution)/shard_map/all_to_all | solution.py:407
  105.8 1.4 copy-start.6
  105.8 1.4 collective-permute-start.8
  107.2 0.7 copy-start.7
  125.2 1.0 copy-start.4
  128.8 4.7 %copy-start.5 = (bf16[528,512]{1,0:T(8,128)(2,1)S(1)}, bf16[528,512]{1,0:T(8,128)(2,1)}, u32[]{:S(2)}) copy-start(bf16[528,512]{1,0:T(8,128)(2,1)} %unpack.1.a0) | copy-start | bytes 1622020
  128.8 32.0 %all-to-all-start.3 = ((bf16[32,16,1280]{2,1,0:T(8,128)(2,1)}), bf16[32,16,1280]{2,1,0:T(8,128)(2,1)S(1)}, u32[]{:S(2)}, u32[]{:S(2)}) async-start(bf16[32,16,1280]{2,1,0:T(8,128)(2,1)} %bitcast.27), calls=%async_computation.3 | async-start | bytes 2621440 | tf_op jit(solution)/shard_map/all_to_all | solution.py:407
  133.5 14.2 %collective-permute-start.9 = (bf16[528,512]{1,0:T(8,128)(2,1)S(1)}, bf16[528,512]{1,0:T(8,128)(2,1)S(1)}, u32[]{:S(2)}, u32[]{:S(2)}) collective-permute-start(bf16[528,512]{1,0:T(8,128)(2,1)S(1)} %copy-done.5), channel_id=1, source_target_pairs={{0,2},{1,3},{2,4},{3,5},{4,6},{5,7},{8,10},{9,11},{10,12},{11,13},... | collective-permute-start | bytes 1622024 | tf_op jit(solution)/shard_map/ppermute | solution.py:386
  136.6 16.9 %collective-permute-start.10 = (bf16[528,512]{1,0:T(8,128)(2,1)S(1)}, bf16[528,512]{1,0:T(8,128)(2,1)}, u32[]{:S(2)}, u32[]{:S(2)}) collective-permute-start(bf16[528,512]{1,0:T(8,128)(2,1)S(1)} %copy-done.5), channel_id=1, source_target_pairs={{0,4},{1,5},{2,6},{3,7},{8,12},{9,13},{10,14},{11,15},{16,20},{17,... | collective-permute-start | bytes 1622024 | tf_op jit(solution)/shard_map/ppermute | solution.py:386
  141.2 23.4 %collective-permute-start.11 = (bf16[528,512]{1,0:T(8,128)(2,1)S(1)}, bf16[528,512]{1,0:T(8,128)(2,1)}, u32[]{:S(2)}, u32[]{:S(2)}) collective-permute-start(bf16[528,512]{1,0:T(8,128)(2,1)S(1)} %copy-done.5), channel_id=1, source_target_pairs={{0,1},{1,0},{2,3},{3,2},{4,5},{5,4},{6,7},{7,6},{8,9},{9,8},{10,11... | collective-permute-start | bytes 1622024 | tf_op jit(solution)/shard_map/ppermute | solution.py:377
  147.7 16.9 %copy-start.11 = (bf16[528,512]{1,0:T(8,128)(2,1)}, bf16[528,512]{1,0:T(8,128)(2,1)S(1)}, u32[]{:S(2)}) copy-start(bf16[528,512]{1,0:T(8,128)(2,1)S(1)} %collective-permute-done.9.a1) | copy-start | bytes 1622020
  147.7 16.9 %collective-permute-start.12 = (bf16[528,512]{1,0:T(8,128)(2,1)S(1)}, bf16[528,512]{1,0:T(8,128)(2,1)}, u32[]{:S(2)}, u32[]{:S(2)}) collective-permute-start(bf16[528,512]{1,0:T(8,128)(2,1)S(1)} %collective-permute-done.9.a1), channel_id=1, source_target_pairs={{0,1},{1,0},{2,3},{3,2},{4,5},{5,4},{6,7},{7,6},{8,9},{9,8},{10,11... | collective-permute-start | bytes 1622024 | tf_op jit(solution)/shard_map/ppermute | solution.py:377
  153.5 11.1 %collective-permute-start.13 = (bf16[528,512]{1,0:T(8,128)(2,1)}, bf16[528,512]{1,0:T(8,128)(2,1)}, u32[]{:S(2)}, u32[]{:S(2)}) collective-permute-start(bf16[528,512]{1,0:T(8,128)(2,1)} %collective-permute-done.10.a2), channel_id=1, source_target_pairs={{0,1},{1,0},{2,3},{3,2},{4,5},{5,4},{6,7},{7,6},{8,9},{9,8},{10,11... | collective-permute-start | bytes 1622024 | tf_op jit(solution)/shard_map/ppermute | solution.py:377
  160.8 1.1 copy-start.2

commit v3 on v2

--- a/solution.py
+++ b/solution.py
@@ -27,11 +27,12 @@
 GROUP_WIDTH = HEAD_GROUP * HEAD_SIZE
 EARLY = 2
 WINDOW = REACH + LOC
-SENT = PAIR + 16
+SENT = PAIR + 32
+HALF = ROW_WIDTH // 2
 SCORE_BASE2 = 1.4426950408889634 * HEAD_SIZE ** (-0.5)
 BF16 = jnp.bfloat16
 F32 = jnp.float32
-PARAMS = dict(vmem_limit_bytes=60 << 20)
+PARAMS = dict(vmem_limit_bytes=24 << 20)
 
 
 def whole(shape):
@@ -128,15 +129,15 @@
 
 
 def project_kernel(
-    table_ref, hot_ref, gain_ref, x_ref, sib_ref, w0, w1, w2, w3, out_ref, weight, acc, sems
+    table_ref, hot_ref, gain_ref, x_ref, sib_ref, *rest
 ):
     step = pl.program_id(0)
     core = table_ref[8]
-    sources = (w0, w1, w2, w3)
-
-    def copy(source, i, x, y):
+    sources, (out_ref, weight, acc, sems) = rest[:8], rest[8:]
+
+    def copy(j, i, x, y):
         return pltpu.make_async_copy(
-            source.at[pl.ds(i * RUN, RUN), :],
+            sources[2 * j + i // 2].at[pl.ds(i % 2 * RUN, RUN), :],
             weight.at[
                 pl.ds(pl.multiple_of(x * RUN, RUN), RUN),
                 pl.ds(pl.multiple_of(y * HEAD_SIZE, HEAD_SIZE), HEAD_SIZE),
@@ -150,17 +151,17 @@
         def _():
             for i in range(4):
                 for j in range(4):
-                    copy(sources[j], i, table_ref[i], table_ref[4 + j]).start()
+                    copy(j, i, table_ref[i], table_ref[4 + j]).start()
 
         @pl.when(core != 0)
         def _():
             for j in range(4):
                 for i in range(4):
-                    copy(sources[j], i, table_ref[j], table_ref[4 + i]).start()
+                    copy(j, i, table_ref[j], table_ref[4 + i]).start()
 
     x = table_ref[step]
     for y in range(4):
-        copy(w0, 0, x, y).wait()
+        copy(0, 0, x, y).wait()
     w = weight[pl.ds(pl.multiple_of(x * RUN, RUN), RUN), :]
     for n, ref in enumerate((x_ref, sib_ref)):
         now = jnp.dot(ref[...], w, preferred_element_type=F32)
@@ -198,7 +199,7 @@
                 across,
                 across,
             ]
-            + [pl.BlockSpec(memory_space=pl.ANY)] * 4,
+            + [pl.BlockSpec(memory_space=pl.ANY)] * 8,
             out_specs=whole((2 * SLOTS, ROW_WIDTH)),
             scratch_shapes=[
                 pltpu.VMEM((WIDTH, ROW_WIDTH), BF16),
@@ -263,7 +264,10 @@
         out_ref[k * LOC : (k + 1) * LOC, :] = jnp.dot(
             hot_ref[k], part, preferred_element_type=F32
         ).astype(BF16)
-    out_ref[PAIR:SENT, :] = jnp.broadcast_to(seg_ref[...].astype(F32).astype(BF16), (16, PAIR))
+    seg = seg_ref[...].astype(F32).astype(BF16)
+    for k in range(2):
+        both = jnp.concatenate([seg[:, k * LOC : (k + 1) * LOC]] * 2, axis=1)
+        out_ref[PAIR + 16 * k : PAIR + 16 * k + 16, :] = jnp.broadcast_to(both, (16, ROW_WIDTH))
 
 
 def unpack(hots, seg, got):
@@ -279,8 +283,9 @@
 
 
 def attend_kernel(
-    where_ref, seg_ref, early_ref, late_ref, a0, a1, a2, b0, b1, b2, out_ref, keys, values, bias, queries
+    packed, where_ref, seg_ref, hot_ref, q_ref, a0, a1, a2, b0, b1, b2, *rest
 ):
+    out_ref, keys, values, bias, queries = rest[-5:]
     core = where_ref[0]
     ctx = where_ref[3]
     head = pl.program_id(0)
@@ -301,9 +306,11 @@
                 dst[LOC : LOC + PAIR, :] = s1[0:PAIR, :]
                 dst[LOC + PAIR : WINDOW, :] = s0[0:PAIR, :]
 
-        segs = [a[PAIR:SENT, :][0:1].astype(F32) for a in (a2, a1, a0)]
-        left = jnp.concatenate([segs[0], segs[1], segs[2][:, 0:LOC]], axis=1)
-        right = jnp.concatenate([segs[0][:, LOC:PAIR], segs[1], segs[2]], axis=1)
+        segs = []
+        for a in (a2, a1, a0):
+            for start in (PAIR, PAIR + 16):
+                segs.append(a[start : start + 16, :][0:1].astype(F32))
+        left, right = jnp.concatenate(segs[:5], axis=1), jnp.concatenate(segs[1:], axis=1)
         key_seg = jnp.where(core == 0, left, right)
         query_seg = seg_ref[...].astype(F32)
         k = iota((LOC, WINDOW), 1)
@@ -311,14 +318,10 @@
         allowed = (k <= q + REACH) & (k >= REACH - ctx * LOC) & (key_seg == query_seg)
         bias[...] = jnp.where(allowed, F32(0), F32(-1e30))
 
-    @pl.when(head < EARLY)
-    def _():
-        queries[...] = early_ref[...]
-
-    @pl.when(head >= EARLY)
-    def _():
-        queries[...] = late_ref[...]
-
+    if packed:
+        queries[...] = jnp.dot(hot_ref[core], q_ref[...], preferred_element_type=F32).astype(BF16)
+    else:
+        queries[...] = q_ref[...]
     columns = pl.ds(pl.multiple_of(head * HEAD_SIZE, HEAD_SIZE), HEAD_SIZE)
     key_rows = keys[:, columns]
     value_rows = values[:, columns]
@@ -335,33 +338,38 @@
         out_ref[:, cols] = (summed[:, :HEAD_SIZE] / summed[:, HEAD_SIZE:]).astype(BF16)
 
 
-def attend(where, seg_col, early, late, mine, other):
-    return pl.pallas_call(
-        attend_kernel,
-        grid=(KEY_VALUE_HEADS,),
+def attend(where, seg_col, hots, queries, part, mine, other, start):
+    heads = KEY_VALUE_HEADS // 2
+    packed = queries.shape[0] == SLOTS
+    first = 0 if part * heads < EARLY else EARLY
+    return pl.pallas_call(
+        functools.partial(attend_kernel, packed),
+        grid=(heads,),
         in_specs=[
             pl.BlockSpec(memory_space=pltpu.SMEM),
             whole((LOC, 1)),
-            pl.BlockSpec((LOC, GROUP_WIDTH), lambda i: (0, jnp.minimum(i, EARLY - 1))),
-            pl.BlockSpec((LOC, GROUP_WIDTH), lambda i: (0, jnp.maximum(i - EARLY, 0))),
+            whole((2, LOC, SLOTS)),
+            pl.BlockSpec((queries.shape[0], GROUP_WIDTH), lambda i: (0, part * heads - first + i)),
         ]
-        + [whole((SENT, ROW_WIDTH))] * 6,
-        out_specs=pl.BlockSpec((LOC, GROUP_WIDTH), lambda i: (0, i)),
+        + [pl.BlockSpec((SENT, HALF), lambda i: (0, part))] * 6
+        + [pl.BlockSpec(memory_space=pl.ANY)] * len(start),
+        out_specs=pl.BlockSpec((LOC, GROUP_WIDTH), lambda i: (0, part * heads + i)),
         out_shape=jax.ShapeDtypeStruct((LOC, QUERY_WIDTH), BF16),
+        input_output_aliases={10: 0} if start else {},
         scratch_shapes=[
-            pltpu.VMEM((WINDOW, ROW_WIDTH), BF16),
-            pltpu.VMEM((WINDOW, ROW_WIDTH), BF16),
+            pltpu.VMEM((WINDOW, HALF), BF16),
+            pltpu.VMEM((WINDOW, HALF), BF16),
             pltpu.VMEM((LOC, WINDOW), F32),
             pltpu.VMEM((LOC, GROUP_WIDTH), BF16),
         ],
         compiler_params=pltpu.CompilerParams(**PARAMS),
         cost_estimate=pl.CostEstimate(
-            flops=4 * LOC * WINDOW * QUERY_WIDTH,
-            bytes_accessed=8 << 20,
-            transcendentals=LOC * WINDOW * QUERY_HEADS,
+            flops=2 * LOC * WINDOW * QUERY_WIDTH,
+            bytes_accessed=4 << 20,
+            transcendentals=LOC * WINDOW * QUERY_HEADS // 2,
         ),
         name="attend",
-    )(where, seg_col, early, late, *mine, *other)
+    )(where, seg_col, hots, queries, *mine, *other, *start)
 
 
 def chips():
@@ -421,8 +429,9 @@
     )
     run = along_z(part)
     early_slots, late_slots = pack_queries(col, row, gen_queries)
-    line = jnp.concatenate([run] + [along_first(run, -by) for by in NEAR[1:]])
-    early_slots, line = lax.optimization_barrier((early_slots, line))
+    near = jnp.concatenate([run, along_first(run, 1)])
+    far = jnp.concatenate([along_first(run, -1), along_first(run, 2)])
+    early_slots, near, far = lax.optimization_barrier((early_slots, near, far))
     got_early = move(early_slots, CAPACITY)
 
     sib = swap_cores(jnp.stack([place, seg]))
@@ -431,10 +440,13 @@
     pair_seg = jnp.where(core == 0, jnp.concatenate([seg, sib[1]]), jnp.concatenate([sib[1], seg]))
     pair_seg = pair_seg.reshape(1, PAIR)
 
-    weights = [line] + [along_second(line, -by) for by in NEAR[1:]]
+    below, below_far = along_second(near, 1), along_second(far, 1)
+    above, above_far = along_second(near, -1), along_second(far, -1)
+    opposite, opposite_far = along_second(above, -1), along_second(below_far, 1)
+    weights = [near, far, below, below_far, above, above_far, opposite, opposite_far]
     hot = row_places(core_s, col, row, sib_col, sib_row)
-    near = jnp.array(NEAR)
-    table = jnp.concatenate([(chip_x + near) % 4, (chip_y + near) % 4, core_s])
+    offsets = jnp.array(NEAR)
+    table = jnp.concatenate([(chip_x + offsets) % 4, (chip_y + offsets) % 4, core_s])
     slots = project(table, hot, key_norm_gain.reshape(1, ROW_WIDTH), gen_rows, sib_rows, weights)
     slots, got_early = lax.optimization_barrier((slots, got_early))
     got = move(slots, 2 * CAPACITY)
@@ -446,9 +458,12 @@
     late_slots, own = lax.optimization_barrier((late_slots, own))
     up = [send_up(own, 1), send_up(own, 2)]
     got_late = move(late_slots, CAPACITY)
-    late = unpack_queries(core_s, hots, got_late, KEY_VALUE_HEADS - EARLY)
     other = [swap_cores(m) for m in [own] + up]
-    return attend(where, seg.reshape(LOC, 1), early, late, [own] + up, other)
+    seg_col = seg.reshape(LOC, 1)
+    mine = [own] + up
+    out = attend(where, seg_col, hots, early, 0, mine, other, [])
+    got_late, out = lax.optimization_barrier((got_late, out))
+    return attend(where, seg_col, hots, got_late, 1, mine, other, [out])
 
 
 def solution(mesh):

time: 180 us -> 171 us (0.950); the launches traced: 179 us -> 168 us
  Pallas kernels: 43.2 us -> 28.7 us
  starting transfers between devices: 38.1 us -> 43.5 us
  waiting for transfers between devices: 68 us -> 65 us
  local copies, waits for them, and re-layouts: 7.39 us -> 10 us
    unnamed x24 -> x34, local copies, waits for them, and re-layouts: 3.72 us -> 8.89 us
    pallas_call x2 -> x1, Pallas kernels: 5.49 us -> 1.02 us  [unpack_queries(): pl.pallas_call(unpack_queries_kernel, grid=(groups,), in_specs=[pl.BlockS...]
    ppermute x12 -> x15, starting transfers between devices: 14 us -> 18.1 us  [shift(): return lax.ppermute(array, ('dp', 'ctx'), pairs)]
    all_to_all x3, waiting for transfers between devices: 18.3 us -> 14.3 us  [move(): lax.all_to_all(sent, 'dp', split_axis=0, concat_axis=0, tiled=True)]
    pallas_call x1, Pallas kernels: 5.34 us -> 2.39 us  [pack_queries(): pl.pallas_call(pack_queries_kernel, grid=(KEY_VALUE_HEADS,), in_specs=[wh...]
    pallas_call x1, Pallas kernels: 10.3 us -> 7.66 us  [project(): pl.pallas_call(project_kernel, grid_spec=pltpu.PrefetchScalarGridSpec(num...]
    pallas_call x1, Pallas kernels: 2.65 us -> 0.43 us  [unpack(): pl.pallas_call(unpack_kernel, out_shape=jax.ShapeDtypeStruct((SENT, ROW_W...]
    pallas_call x1, Pallas kernels: 2.62 us -> 0.68 us  [row_places(): pl.pallas_call(row_places_kernel, in_specs=[pl.BlockSpec(memory_space=plt...]
  transfers between devices with their start and end apart: 17 -> 20, of which waited for: 8 -> 9; matrix products, arithmetic and copies ran while one was open for 3% -> 1% of each run, Pallas kernels for 14% -> 12%
where the time goes in v3:
time: 171 us; the launch traced here: 168 us
  waiting for transfers between devices  65 us (38%)
  starting transfers between devices  43.5 us (25%)
  Pallas kernels  28.7 us (17%)
  blocking collectives  20.5 us (12%)
  local copies, waits for them, and re-layouts  10 us (6%)
    ppermute x15, waiting for transfers between devices, shift(): return lax.ppermute(array, ('dp', 'ctx'), pairs)  39.1 us
    all_to_all x1, blocking collectives, along_z(): lax.all_to_all(copies, ('dp', 'ctx'), 0, 0, axis_index_groups=groups, til...  20.5 us
    ppermute x15, starting transfers between devices, shift(): return lax.ppermute(array, ('dp', 'ctx'), pairs)  18.1 us
    all_to_all x3, starting transfers between devices, move(): lax.all_to_all(sent, 'dp', split_axis=0, concat_axis=0, tiled=True)  17 us
    pallas_call x2, Pallas kernels, attend(): pl.pallas_call(functools.partial(attend_kernel, packed), grid=(heads,), i...  16.2 us
    all_to_all x3, waiting for transfers between devices, move(): lax.all_to_all(sent, 'dp', split_axis=0, concat_axis=0, tiled=True)  14.3 us
    ppermute x2, waiting for transfers between devices, send_up(): return lax.ppermute(array, ('dp', 'ctx'), pairs)  11.7 us
    unnamed x34, local copies, waits for them, and re-layouts  8.89 us
  transfers between devices with their start and end apart: 20, of which 9 were waited for; matrix products, arithmetic and copies ran while one was open for 1% of the time, Pallas kernels for 12%

profile of v3, /device:TPU:1, one launch (start us, length us, event | category | flops | bytes accessed | tf_op | source)
XLA Modules:
  0.0 168.3 jit_solution(18290121584182296604)
XLA Ops:
  0.0 1.0 copy-done
  1.0 20.5 %all_to_all.20 = bf16[8,160,128]{2,1,0:T(8,128)(2,1)S(1)} all-to-all(bf16[8,160,128]{2,1,0:T(8,128)(2,1)S(1)} %broadcast_in_dim.2), channel_id=1, replica_groups={{0,8,16,24,32,40,48,56},{1,9,17,25,33,41,49,57},{2,10,18,26,34,42,50,58..., dimensions={0} | all-to-all | bytes 655360 | tf_op jit(solution)/shard_map/all_to_all | solution.py:400
  21.5 1.3 collective-permute-start.2
  22.8 2.8 %collective-permute-start.1 = (bf16[256,5120]{1,0:T(8,128)(2,1)}, bf16[256,5120]{1,0:T(8,128)(2,1)}, u32[]{:S(2)}, u32[]{:S(2)}) collective-permute-start(bf16[256,5120]{1,0:T(8,128)(2,1)} %x_ref.1), channel_id=1, source_target_pairs={{0,1},{1,0},{2,3},{3,2},{4,5},{5,4},{6,7},{7,6},{8,9},{9,8},{10,11... | collective-permute-start | bytes 7864328 | tf_op jit(solution)/shard_map/ppermute | solution.py:385
  25.6 0.8 copy.9.col_ref
  26.4 0.7 copy-done.11
  27.1 1.3 copy-done.14
  28.4 2.4 %pack_queries.1 = (bf16[512,1408]{1,0:T(8,128)(2,1)S(1)}, bf16[512,1280]{1,0:T(8,128)(2,1)S(1)}) custom-call(s32[256,1]{1,0:T(8,128)S(1)} %copy.9.col_ref, s32[1,256]{1,0:T(1,128)S(1)} %bitcast.25, bf16[256,2560]{1,0:T(8,128)(2,1)S(1)} %copy-done.14), custom_call_target="tpu_custom_call" | custom-call | flops 671088640 | bytes 4194304 | tf_op jit(solution)/shard_map/pack_queries/pallas_call | solution.py:91
  30.8 2.8 %collective-permute-start.3 = (bf16[1280,128]{1,0:T(8,128)(2,1)S(1)}, bf16[1280,128]{1,0:T(8,128)(2,1)S(1)}, u32[]{:S(2)}, u32[]{:S(2)}) collective-permute-start(bf16[1280,128]{1,0:T(8,128)(2,1)S(1)} %bitcast.30), channel_id=1, source_target_pairs={{0,192},{1,7},{2,194},{3,1},{4,196},{5,3},{6,198},{7,5},{8,200},{9... | collective-permute-start | bytes 983048 | tf_op jit(solution)/shard_map/ppermute | solution.py:385
  33.6 0.3 collective-permute-start.4
  34.0 7.1 %collective-permute-done.3 = bf16[1280,128]{1,0:T(8,128)(2,1)S(1)} collective-permute-done((bf16[1280,128]{1,0:T(8,128)(2,1)S(1)}, bf16[1280,128]{1,0:T(8,128)(2,1)S(1)}, u32[]{:S(2)}, u32[]{:S(2)}) %collective-permute-start.3) | collective-permute-done | bytes 327712 | tf_op jit(solution)/shard_map/ppermute | solution.py:385
  41.3 4.3 %all-to-all-start.1 = ((bf16[32,16,1408]{2,1,0:T(8,128)(2,1)}), bf16[32,16,1408]{2,1,0:T(8,128)(2,1)S(1)}, u32[]{:S(2)}, u32[]{:S(2)}) async-start(bf16[32,16,1408]{2,1,0:T(8,128)(2,1)} %bitcast.22), calls=%async_computation.1 | async-start | bytes 2883584 | tf_op jit(solution)/shard_map/all_to_all | solution.py:415
  45.5 1.3 collective-permute-start.6
  46.8 1.4 collective-permute-start.7
  48.3 1.7 %collective-permute-start = (s32[2,256]{1,0:T(2,128)S(1)}, s32[2,256]{1,0:T(2,128)S(1)}, u32[]{:S(2)}, u32[]{:S(2)}) collective-permute-start(s32[2,256]{1,0:T(2,128)S(1)} %pad_add_fusion), channel_id=1, source_target_pairs={{0,1},{1,0},{2,3},{3,2},{4,5},{5,4},{6,7},{7,6},{8,9},{9,8},{10,11... | collective-permute-start | bytes 6152 | tf_op jit(solution)/shard_map/ppermute | solution.py:385
  50.0 1.5 collective-permute-start.5
  51.5 2.1 %collective-permute-start.8 = (bf16[2560,128]{1,0:T(8,128)(2,1)S(1)}, bf16[2560,128]{1,0:T(8,128)(2,1)}, u32[]{:S(2)}, u32[]{:S(2)}) collective-permute-start(bf16[2560,128]{1,0:T(8,128)(2,1)S(1)} %pad_maximum_fusion.1.rest_1_), channel_id=1, source_target_pairs={{0,6},{1,193},{2,0},{3,195},{4,2},{5,197},{6,4},{7,199},{8,14},{9,... | collective-permute-start | bytes 1966088 | tf_op jit(solution)/shard_map/ppermute | solution.py:385
  53.6 9.8 %collective-permute-done.6.rest_3_ = bf16[2560,128]{1,0:T(8,128)(2,1)} collective-permute-done((bf16[2560,128]{1,0:T(8,128)(2,1)S(1)}, bf16[2560,128]{1,0:T(8,128)(2,1)}, u32[]{:S(2)}, u32[]{:S(2)}) %collective-permute-start.6) | collective-permute-done | bytes 655392 | tf_op jit(solution)/shard_map/ppermute | solution.py:385
  63.5 2.7 %collective-permute-start.9 = (bf16[2560,128]{1,0:T(8,128)(2,1)}, bf16[2560,128]{1,0:T(8,128)(2,1)}, u32[]{:S(2)}, u32[]{:S(2)}) collective-permute-start(bf16[2560,128]{1,0:T(8,128)(2,1)} %collective-permute-done.7.rest_4_), channel_id=1, source_target_pairs={{0,6},{1,193},{2,0},{3,195},{4,2},{5,197},{6,4},{7,199},{8,14},{9,... | collective-permute-start | bytes 1966088 | tf_op jit(solution)/shard_map/ppermute | solution.py:385
  66.2 0.1 pad_add_fusion.2.table_ref
  66.2 0.1 copy.10.sib_col_ref
  66.4 0.7 row_places.1.hot_ref
  67.1 10.1 %collective-permute-done.5.rest_2_ = bf16[2560,128]{1,0:T(8,128)(2,1)} collective-permute-done((bf16[2560,128]{1,0:T(8,128)(2,1)S(1)}, bf16[2560,128]{1,0:T(8,128)(2,1)}, u32[]{:S(2)}, u32[]{:S(2)}) %collective-permute-start.5) | collective-permute-done | bytes 655392 | tf_op jit(solution)/shard_map/ppermute | solution.py:385
  77.2 8.6 %collective-permute-done.10.rest_7_ = bf16[2560,128]{1,0:T(8,128)(2,1)} collective-permute-done((bf16[2560,128]{1,0:T(8,128)(2,1)}, bf16[2560,128]{1,0:T(8,128)(2,1)}, u32[]{:S(2)}, u32[]{:S(2)}) %collective-permute-start.10) | collective-permute-done | bytes 655392 | tf_op jit(solution)/shard_map/ppermute | solution.py:385
  85.8 1.7 %copy-done.2 = bf16[256,5120]{1,0:T(8,128)(2,1)S(1)} copy-done((bf16[256,5120]{1,0:T(8,128)(2,1)S(1)}, bf16[256,5120]{1,0:T(8,128)(2,1)}, u32[]{:S(2)}) %copy-start.2) | copy-done | bytes 2621464
  87.5 7.7 %project.1 = bf16[1024,512]{1,0:T(8,128)(2,1)S(1)} custom-call(s32[9]{0:T(128)S(1)} %pad_add_fusion.2.table_ref, bf16[1024,512]{1,0:T(8,128)(2,1)S(1)} %row_places.1.hot_ref, f32[1,512]{1,0:T(1,128)S(1)} %bitcast.28, bf16[256,5120]{1,0:T(8,128)(2,1)S(1)} %copy-done.2, bf16[256,5120]{1,0:T(8,128)(2,1)} %collective-permute-done.1.sib_ref, ...), custom_call_target="tpu_custom_call" | custom-call | flops 2684354560 | bytes 12582912 | tf_op jit(solution)/shard_map/project/pallas_call | solution.py:191
  95.2 1.0 copy-done.1
  96.2 8.1 %all-to-all-start.2 = ((bf16[32,32,512]{2,1,0:T(8,128)(2,1)}), bf16[32,32,512]{2,1,0:T(8,128)(2,1)S(1)}, u32[]{:S(2)}, u32[]{:S(2)}) async-start(bf16[32,32,512]{2,1,0:T(8,128)(2,1)} %bitcast.21), calls=%async_computation.2 | async-start | bytes 2097152 | tf_op jit(solution)/shard_map/all_to_all | solution.py:415
  104.3 0.1 collective-permute-start.11
  104.4 1.3 collective-permute-done.11.sib_ref
  105.7 0.6 copy-done.9
  106.4 0.9 copy-done.10
  107.3 0.2 places.1.hot_ref
  107.5 1.0 unpack_queries.1.q_ref
  108.5 0.8 copy-done.7
  109.4 14.3 %all-to-all-done.2 = bf16[32,32,512]{2,1,0:T(8,128)(2,1)S(1)} async-done(((bf16[32,32,512]{2,1,0:T(8,128)(2,1)}), bf16[32,32,512]{2,1,0:T(8,128)(2,1)S(1)}, u32[]{:S(2)}, u32[]{:S(2)}) %all-to-all-start.2) | async-done | bytes 1048608 | tf_op jit(solution)/shard_map/all_to_all | solution.py:415
  123.7 0.4 unpack.1.a0
  124.1 0.8 copy-done.3
  124.9 4.7 %all-to-all-start.3 = ((bf16[32,16,1280]{2,1,0:T(8,128)(2,1)}), bf16[32,16,1280]{2,1,0:T(8,128)(2,1)S(1)}, u32[]{:S(2)}, u32[]{:S(2)}) async-start(bf16[32,16,1280]{2,1,0:T(8,128)(2,1)} %bitcast.23), calls=%async_computation.3 | async-start | bytes 2621440 | tf_op jit(solution)/shard_map/all_to_all | solution.py:415
  129.6 3.8 %collective-permute-start.12 = (bf16[544,512]{1,0:T(8,128)(2,1)S(1)}, bf16[544,512]{1,0:T(8,128)(2,1)}, u32[]{:S(2)}, u32[]{:S(2)}) collective-permute-start(bf16[544,512]{1,0:T(8,128)(2,1)S(1)} %copy-done.4), channel_id=1, source_target_pairs={{0,2},{1,3},{2,4},{3,5},{4,6},{5,7},{8,10},{9,11},{10,12},{11,13},... | collective-permute-start | bytes 1671176 | tf_op jit(solution)/shard_map/ppermute | solution.py:394
  133.4 4.6 %collective-permute-start.13 = (bf16[544,512]{1,0:T(8,128)(2,1)S(1)}, bf16[544,512]{1,0:T(8,128)(2,1)}, u32[]{:S(2)}, u32[]{:S(2)}) collective-permute-start(bf16[544,512]{1,0:T(8,128)(2,1)S(1)} %copy-done.4), channel_id=1, source_target_pairs={{0,4},{1,5},{2,6},{3,7},{8,12},{9,13},{10,14},{11,15},{16,20},{17,... | collective-permute-start | bytes 1671176 | tf_op jit(solution)/shard_map/ppermute | solution.py:394
  138.1 5.6 %collective-permute-done.12.a1 = bf16[544,512]{1,0:T(8,128)(2,1)} collective-permute-done((bf16[544,512]{1,0:T(8,128)(2,1)S(1)}, bf16[544,512]{1,0:T(8,128)(2,1)}, u32[]{:S(2)}, u32[]{:S(2)}) %collective-permute-start.12) | collective-permute-done | bytes 557088 | tf_op jit(solution)/shard_map/ppermute | solution.py:394
  143.7 6.0 %collective-permute-done.13.a2 = bf16[544,512]{1,0:T(8,128)(2,1)} collective-permute-done((bf16[544,512]{1,0:T(8,128)(2,1)S(1)}, bf16[544,512]{1,0:T(8,128)(2,1)}, u32[]{:S(2)}, u32[]{:S(2)}) %collective-permute-start.13) | collective-permute-done | bytes 557088 | tf_op jit(solution)/shard_map/ppermute | solution.py:394
  149.7 0.1 copy.13.seg_ref
  149.9 0.1 pad_add_fusion.1.where_ref
  150.0 2.1 %collective-permute-done.16.b2 = bf16[544,512]{1,0:T(8,128)(2,1)} collective-permute-done((bf16[544,512]{1,0:T(8,128)(2,1)}, bf16[544,512]{1,0:T(8,128)(2,1)}, u32[]{:S(2)}, u32[]{:S(2)}) %collective-permute-start.16) | collective-permute-done | bytes 557088 | tf_op jit(solution)/shard_map/ppermute | solution.py:385
  152.0 7.9 %attend.2.rest_0_ = bf16[256,2560]{1,0:T(8,128)(2,1)} custom-call(s32[4]{0:T(128)S(1)} %pad_add_fusion.1.where_ref, s32[256,1]{1,0:T(8,128)S(1)} %copy.13.seg_ref, bf16[2,256,512]{2,1,0:T(8,128)(2,1)S(1)} %places.1.hot_ref, bf16[256,1280]{1,0:T(8,128)(2,1)S(1)} %copy-done.8, bf16[544,512]{1,0:T(8,128)(2,1)S(1)} %copy-done.4, ...), custom_call_target="tpu_custom_call" | custom-call | flops 1677721600 | bytes 4194304 | tf_op jit(solution)/shard_map/attend/pallas_call | solution.py:345
  159.9 8.4 %attend.3 = bf16[256,2560]{1,0:T(8,128)(2,1)} custom-call(s32[4]{0:T(128)S(1)} %pad_add_fusion.1.where_ref, s32[256,1]{1,0:T(8,128)S(1)} %copy.13.seg_ref, bf16[2,256,512]{2,1,0:T(8,128)(2,1)S(1)} %places.1.hot_ref, bf16[512,1280]{1,0:T(8,128)(2,1)S(1)} %bitcast.19, bf16[544,512]{1,0:T(8,128)(2,1)S(1)} %copy-done.4, ...), custom_call_target="tpu_custom_call", output_to_operand_aliasing={{}: (10, {})} | custom-call | flops 1677721600 | bytes 4194304 | tf_op jit(solution)/shard_map/attend/pallas_call | solution.py:345
  (49 shorter events, 0.3 us)
Async XLA Ops:
  0.0 1.0 copy-start
  21.5 12.5 %collective-permute-start.2 = (bf16[1280,128]{1,0:T(8,128)(2,1)S(1)}, bf16[1280,128]{1,0:T(8,128)(2,1)S(1)}, u32[]{:S(2)}, u32[]{:S(2)}) collective-permute-start(bf16[1280,128]{1,0:T(8,128)(2,1)S(1)} %bitcast.29), channel_id=1, source_target_pairs={{0,64},{1,3},{2,66},{3,5},{4,68},{5,7},{6,70},{7,1},{8,72},{9,11},... | collective-permute-start | bytes 983048 | tf_op jit(solution)/shard_map/ppermute | solution.py:385
  22.8 62.9 %collective-permute-start.1 = (bf16[256,5120]{1,0:T(8,128)(2,1)}, bf16[256,5120]{1,0:T(8,128)(2,1)}, u32[]{:S(2)}, u32[]{:S(2)}) collective-permute-start(bf16[256,5120]{1,0:T(8,128)(2,1)} %x_ref.1), channel_id=1, source_target_pairs={{0,1},{1,0},{2,3},{3,2},{4,5},{5,4},{6,7},{7,6},{8,9},{9,8},{10,11... | collective-permute-start | bytes 7864328 | tf_op jit(solution)/shard_map/ppermute | solution.py:385
  26.4 0.7 copy-start.11
  27.1 1.3 copy-start.14
  30.8 10.4 %copy-start.6 = (bf16[512,1280]{1,0:T(8,128)(2,1)}, bf16[512,1280]{1,0:T(8,128)(2,1)S(1)}, u32[]{:S(2)}) copy-start(bf16[512,1280]{1,0:T(8,128)(2,1)S(1)} %get-tuple-element.28) | copy-start | bytes 3932164
  30.8 10.4 %copy-start.5 = (bf16[512,1408]{1,0:T(8,128)(2,1)}, bf16[512,1408]{1,0:T(8,128)(2,1)S(1)}, u32[]{:S(2)}) copy-start(bf16[512,1408]{1,0:T(8,128)(2,1)S(1)} %get-tuple-element.22) | copy-start | bytes 4325380
  30.8 10.3 %collective-permute-start.3 = (bf16[1280,128]{1,0:T(8,128)(2,1)S(1)}, bf16[1280,128]{1,0:T(8,128)(2,1)S(1)}, u32[]{:S(2)}, u32[]{:S(2)}) collective-permute-start(bf16[1280,128]{1,0:T(8,128)(2,1)S(1)} %bitcast.30), channel_id=1, source_target_pairs={{0,192},{1,7},{2,194},{3,1},{4,196},{5,3},{6,198},{7,5},{8,200},{9... | collective-permute-start | bytes 983048 | tf_op jit(solution)/shard_map/ppermute | solution.py:385
  33.6 7.5 %collective-permute-start.4 = (bf16[1280,128]{1,0:T(8,128)(2,1)S(1)}, bf16[1280,128]{1,0:T(8,128)(2,1)S(1)}, u32[]{:S(2)}, u32[]{:S(2)}) collective-permute-start(bf16[1280,128]{1,0:T(8,128)(2,1)S(1)} %bitcast.31), channel_id=1, source_target_pairs={{0,128},{1,5},{2,130},{3,7},{4,132},{5,1},{6,134},{7,3},{8,136},{9... | collective-permute-start | bytes 983048 | tf_op jit(solution)/shard_map/ppermute | solution.py:385
  41.2 7.1 %copy-start.12 = (s32[256]{0:T(256)S(1)}, s32[256]{0:T(256)}, u32[]{:S(2)}) copy-start(s32[256]{0:T(256)} %param.9) | copy-start | bytes 3076
  41.2 7.1 %copy-start.15 = (s32[1,256]{1,0:T(1,128)S(1)}, s32[1,256]{1,0:T(1,128)}, u32[]{:S(2)}) copy-start(s32[1,256]{1,0:T(1,128)} %param.10) | copy-start | bytes 3076
  41.2 24.9 %copy-start.16 = (s32[4]{0:T(128)S(1)}, s32[4]{0:T(128)}, u32[]{:S(2)}) copy-start(s32[4]{0:T(128)} %constant.71.clone) | copy-start | bytes 52
  41.3 54.9 %all-to-all-start.1 = ((bf16[32,16,1408]{2,1,0:T(8,128)(2,1)}), bf16[32,16,1408]{2,1,0:T(8,128)(2,1)S(1)}, u32[]{:S(2)}, u32[]{:S(2)}) async-start(bf16[32,16,1408]{2,1,0:T(8,128)(2,1)} %bitcast.22), calls=%async_computation.1 | async-start | bytes 2883584 | tf_op jit(solution)/shard_map/all_to_all | solution.py:415
  45.5 40.2 %copy-start.13 = (f32[512]{0:T(512)S(1)}, f32[512]{0:T(512)}, u32[]{:S(2)}) copy-start(f32[512]{0:T(512)} %param.12) | copy-start | bytes 6148
  45.5 17.9 %collective-permute-start.6 = (bf16[2560,128]{1,0:T(8,128)(2,1)S(1)}, bf16[2560,128]{1,0:T(8,128)(2,1)}, u32[]{:S(2)}, u32[]{:S(2)}) collective-permute-start(bf16[2560,128]{1,0:T(8,128)(2,1)S(1)} %pad_maximum_fusion.1.rest_1_), channel_id=1, source_target_pairs={{0,2},{1,65},{2,4},{3,67},{4,6},{5,69},{6,0},{7,71},{8,10},{9,73},... | collective-permute-start | bytes 1966088 | tf_op jit(solution)/shard_map/ppermute | solution.py:385
  46.8 16.6 %collective-permute-start.7 = (bf16[2560,128]{1,0:T(8,128)(2,1)S(1)}, bf16[2560,128]{1,0:T(8,128)(2,1)}, u32[]{:S(2)}, u32[]{:S(2)}) collective-permute-start(bf16[2560,128]{1,0:T(8,128)(2,1)S(1)} %pad_maximum_fusion.rest_0_), channel_id=1, source_target_pairs={{0,6},{1,193},{2,0},{3,195},{4,2},{5,197},{6,4},{7,199},{8,14},{9,... | collective-permute-start | bytes 1966088 | tf_op jit(solution)/shard_map/ppermute | solution.py:385
  48.3 3.2 %collective-permute-start = (s32[2,256]{1,0:T(2,128)S(1)}, s32[2,256]{1,0:T(2,128)S(1)}, u32[]{:S(2)}, u32[]{:S(2)}) collective-permute-start(s32[2,256]{1,0:T(2,128)S(1)} %pad_add_fusion), channel_id=1, source_target_pairs={{0,1},{1,0},{2,3},{3,2},{4,5},{5,4},{6,7},{7,6},{8,9},{9,8},{10,11... | collective-permute-start | bytes 6152 | tf_op jit(solution)/shard_map/ppermute | solution.py:385
  50.0 27.1 %collective-permute-start.5 = (bf16[2560,128]{1,0:T(8,128)(2,1)S(1)}, bf16[2560,128]{1,0:T(8,128)(2,1)}, u32[]{:S(2)}, u32[]{:S(2)}) collective-permute-start(bf16[2560,128]{1,0:T(8,128)(2,1)S(1)} %pad_maximum_fusion.rest_0_), channel_id=1, source_target_pairs={{0,2},{1,65},{2,4},{3,67},{4,6},{5,69},{6,0},{7,71},{8,10},{9,73},... | collective-permute-start | bytes 1966088 | tf_op jit(solution)/shard_map/ppermute | solution.py:385
  51.5 25.6 %collective-permute-start.8 = (bf16[2560,128]{1,0:T(8,128)(2,1)S(1)}, bf16[2560,128]{1,0:T(8,128)(2,1)}, u32[]{:S(2)}, u32[]{:S(2)}) collective-permute-start(bf16[2560,128]{1,0:T(8,128)(2,1)S(1)} %pad_maximum_fusion.1.rest_1_), channel_id=1, source_target_pairs={{0,6},{1,193},{2,0},{3,195},{4,2},{5,197},{6,4},{7,199},{8,14},{9,... | collective-permute-start | bytes 1966088 | tf_op jit(solution)/shard_map/ppermute | solution.py:385
  63.5 22.3 %collective-permute-start.10 = (bf16[2560,128]{1,0:T(8,128)(2,1)}, bf16[2560,128]{1,0:T(8,128)(2,1)}, u32[]{:S(2)}, u32[]{:S(2)}) collective-permute-start(bf16[2560,128]{1,0:T(8,128)(2,1)} %collective-permute-done.6.rest_3_), channel_id=1, source_target_pairs={{0,2},{1,65},{2,4},{3,67},{4,6},{5,69},{6,0},{7,71},{8,10},{9,73},... | collective-permute-start | bytes 1966088 | tf_op jit(solution)/shard_map/ppermute | solution.py:385
  63.5 22.3 %collective-permute-start.9 = (bf16[2560,128]{1,0:T(8,128)(2,1)}, bf16[2560,128]{1,0:T(8,128)(2,1)}, u32[]{:S(2)}, u32[]{:S(2)}) collective-permute-start(bf16[2560,128]{1,0:T(8,128)(2,1)} %collective-permute-done.7.rest_4_), channel_id=1, source_target_pairs={{0,6},{1,193},{2,0},{3,195},{4,2},{5,197},{6,4},{7,199},{8,14},{9,... | collective-permute-start | bytes 1966088 | tf_op jit(solution)/shard_map/ppermute | solution.py:385
  85.8 1.7 %copy-start.2 = (bf16[256,5120]{1,0:T(8,128)(2,1)S(1)}, bf16[256,5120]{1,0:T(8,128)(2,1)}, u32[]{:S(2)}) copy-start(bf16[256,5120]{1,0:T(8,128)(2,1)} %x_ref.1) | copy-start | bytes 7864324
  95.2 1.0 copy-start.1
  96.2 27.5 %all-to-all-start.2 = ((bf16[32,32,512]{2,1,0:T(8,128)(2,1)}), bf16[32,32,512]{2,1,0:T(8,128)(2,1)S(1)}, u32[]{:S(2)}, u32[]{:S(2)}) async-start(bf16[32,32,512]{2,1,0:T(8,128)(2,1)} %bitcast.21), calls=%async_computation.2 | async-start | bytes 2097152 | tf_op jit(solution)/shard_map/all_to_all | solution.py:415
  104.3 1.4 collective-permute-start.11
  105.7 0.6 copy-start.9
  106.4 0.9 copy-start.10
  108.5 0.8 copy-start.7
  124.1 0.8 copy-start.3
  124.9 4.7 %copy-start.4 = (bf16[544,512]{1,0:T(8,128)(2,1)S(1)}, bf16[544,512]{1,0:T(8,128)(2,1)}, u32[]{:S(2)}) copy-start(bf16[544,512]{1,0:T(8,128)(2,1)} %copy-done.3) | copy-start | bytes 1671172
  124.9 27.1 %copy-start.8 = (bf16[256,1280]{1,0:T(8,128)(2,1)S(1)}, bf16[256,1280]{1,0:T(8,128)(2,1)}, u32[]{:S(2)}) copy-start(bf16[256,1280]{1,0:T(8,128)(2,1)} %copy-done.7) | copy-start | bytes 1966084
  124.9 35.0 %all-to-all-start.3 = ((bf16[32,16,1280]{2,1,0:T(8,128)(2,1)}), bf16[32,16,1280]{2,1,0:T(8,128)(2,1)S(1)}, u32[]{:S(2)}, u32[]{:S(2)}) async-start(bf16[32,16,1280]{2,1,0:T(8,128)(2,1)} %bitcast.23), calls=%async_computation.3 | async-start | bytes 2621440 | tf_op jit(solution)/shard_map/all_to_all | solution.py:415
  129.6 14.1 %collective-permute-start.12 = (bf16[544,512]{1,0:T(8,128)(2,1)S(1)}, bf16[544,512]{1,0:T(8,128)(2,1)}, u32[]{:S(2)}, u32[]{:S(2)}) collective-permute-start(bf16[544,512]{1,0:T(8,128)(2,1)S(1)} %copy-done.4), channel_id=1, source_target_pairs={{0,2},{1,3},{2,4},{3,5},{4,6},{5,7},{8,10},{9,11},{10,12},{11,13},... | collective-permute-start | bytes 1671176 | tf_op jit(solution)/shard_map/ppermute | solution.py:394
  133.4 16.3 %collective-permute-start.13 = (bf16[544,512]{1,0:T(8,128)(2,1)S(1)}, bf16[544,512]{1,0:T(8,128)(2,1)}, u32[]{:S(2)}, u32[]{:S(2)}) collective-permute-start(bf16[544,512]{1,0:T(8,128)(2,1)S(1)} %copy-done.4), channel_id=1, source_target_pairs={{0,4},{1,5},{2,6},{3,7},{8,12},{9,13},{10,14},{11,15},{16,20},{17,... | collective-permute-start | bytes 1671176 | tf_op jit(solution)/shard_map/ppermute | solution.py:394
  138.1 11.9 %collective-permute-start.14 = (bf16[544,512]{1,0:T(8,128)(2,1)S(1)}, bf16[544,512]{1,0:T(8,128)(2,1)}, u32[]{:S(2)}, u32[]{:S(2)}) collective-permute-start(bf16[544,512]{1,0:T(8,128)(2,1)S(1)} %copy-done.4), channel_id=1, source_target_pairs={{0,1},{1,0},{2,3},{3,2},{4,5},{5,4},{6,7},{7,6},{8,9},{9,8},{10,11... | collective-permute-start | bytes 1671176 | tf_op jit(solution)/shard_map/ppermute | solution.py:385
  143.7 6.2 %collective-permute-start.15 = (bf16[544,512]{1,0:T(8,128)(2,1)}, bf16[544,512]{1,0:T(8,128)(2,1)}, u32[]{:S(2)}, u32[]{:S(2)}) collective-permute-start(bf16[544,512]{1,0:T(8,128)(2,1)} %collective-permute-done.12.a1), channel_id=1, source_target_pairs={{0,1},{1,0},{2,3},{3,2},{4,5},{5,4},{6,7},{7,6},{8,9},{9,8},{10,11... | collective-permute-start | bytes 1671176 | tf_op jit(solution)/shard_map/ppermute | solution.py:385
  149.7 2.3 %collective-permute-start.16 = (bf16[544,512]{1,0:T(8,128)(2,1)}, bf16[544,512]{1,0:T(8,128)(2,1)}, u32[]{:S(2)}, u32[]{:S(2)}) collective-permute-start(bf16[544,512]{1,0:T(8,128)(2,1)} %collective-permute-done.13.a2), channel_id=1, source_target_pairs={{0,1},{1,0},{2,3},{3,2},{4,5},{5,4},{6,7},{7,6},{8,9},{9,8},{10,11... | collective-permute-start | bytes 1671176 | tf_op jit(solution)/shard_map/ppermute | solution.py:385

commit v4 on v3

--- a/solution.py
+++ b/solution.py
@@ -428,7 +428,7 @@
         key_value_weight, core * ROW_WIDTH + chip_y * HEAD_SIZE, HEAD_SIZE, 1
     )
     run = along_z(part)
-    early_slots, late_slots = pack_queries(col, row, gen_queries)
+    (early_slots, late_slots), run = lax.optimization_barrier((pack_queries(col, row, gen_queries), run))
     near = jnp.concatenate([run, along_first(run, 1)])
     far = jnp.concatenate([along_first(run, -1), along_first(run, 2)])
     early_slots, near, far = lax.optimization_barrier((early_slots, near, far))

time: 171 us -> 165 us (0.965)
  blocking collectives: 20.5 us -> 0 us
  starting transfers between devices: 43.5 us -> 51.6 us
  waiting for transfers between devices: 65 us -> 69.6 us
    all_to_all x1 -> x0, blocking collectives: 20.5 us -> none  [along_z(): lax.all_to_all(copies, ('dp', 'ctx'), 0, 0, axis_index_groups=groups, til...]
    all_to_all x0 -> x1, starting transfers between devices: none -> 9.01 us  [along_z(): lax.all_to_all(copies, ('dp', 'ctx'), 0, 0, axis_index_groups=groups, til...]
    all_to_all x0 -> x1, waiting for transfers between devices: none -> 4.47 us  [along_z(): lax.all_to_all(copies, ('dp', 'ctx'), 0, 0, axis_index_groups=groups, til...]
    unnamed x34 -> x32, local copies, waits for them, and re-layouts: 8.89 us -> 9.37 us
  transfers between devices with their start and end apart: 20 -> 21, of which waited for: 9 -> 12; matrix products, arithmetic and copies ran while one was open for 1% -> 1% of each run, Pallas kernels for 12% -> 12%
where the time goes in v4:
time: 165 us; the launch traced here: 162 us
  waiting for transfers between devices  69.6 us (42%)
  starting transfers between devices  51.6 us (31%)
  Pallas kernels  29.1 us (18%)
  local copies, waits for them, and re-layouts  11.2 us (7%)
    ppermute x15, waiting for transfers between devices, shift(): return lax.ppermute(array, ('dp', 'ctx'), pairs)  39.5 us
    ppermute x15, starting transfers between devices, shift(): return lax.ppermute(array, ('dp', 'ctx'), pairs)  17.5 us
    all_to_all x3, starting transfers between devices, move(): lax.all_to_all(sent, 'dp', split_axis=0, concat_axis=0, tiled=True)  16.7 us
    pallas_call x2, Pallas kernels, attend(): pl.pallas_call(functools.partial(attend_kernel, packed), grid=(heads,), i...  16.2 us
    all_to_all x3, waiting for transfers between devices, move(): lax.all_to_all(sent, 'dp', split_axis=0, concat_axis=0, tiled=True)  14.2 us
    ppermute x2, waiting for transfers between devices, send_up(): return lax.ppermute(array, ('dp', 'ctx'), pairs)  11.5 us
    unnamed x32, local copies, waits for them, and re-layouts  9.37 us
    all_to_all x1, starting transfers between devices, along_z(): lax.all_to_all(copies, ('dp', 'ctx'), 0, 0, axis_index_groups=groups, til...  9.01 us
  transfers between devices with their start and end apart: 21, of which 12 were waited for; matrix products, arithmetic and copies ran while one was open for 1% of the time, Pallas kernels for 12%

profile of v4, /device:TPU:1, one launch (start us, length us, event | category | flops | bytes accessed | tf_op | source)
XLA Modules:
  0.0 162.0 jit_solution(15335337916196592156)
XLA Ops:
  0.0 1.0 copy-done
  1.0 0.8 broadcast_in_dim.2
  1.8 9.0 %all-to-all-start = ((bf16[8,160,128]{2,1,0:T(8,128)(2,1)}), bf16[8,160,128]{2,1,0:T(8,128)(2,1)S(1)}, u32[]{:S(2)}, u32[]{:S(2)}) async-start(bf16[8,160,128]{2,1,0:T(8,128)(2,1)} %broadcast_in_dim.2), calls=%async_computation | async-start | bytes 655360 | tf_op jit(solution)/shard_map/all_to_all | solution.py:400
  10.8 0.8 copy.9.col_ref
  11.6 0.7 copy-done.10
  12.3 1.3 copy-done.13
  13.6 2.4 %pack_queries.1 = (bf16[512,1408]{1,0:T(8,128)(2,1)S(1)}, bf16[512,1280]{1,0:T(8,128)(2,1)S(1)}) custom-call(s32[256,1]{1,0:T(8,128)S(1)} %copy.9.col_ref, s32[1,256]{1,0:T(1,128)S(1)} %bitcast.25, bf16[256,2560]{1,0:T(8,128)(2,1)S(1)} %copy-done.13), custom_call_target="tpu_custom_call" | custom-call | flops 671088640 | bytes 4194304 | tf_op jit(solution)/shard_map/pack_queries/pallas_call | solution.py:91
  16.0 1.1 copy-done.4
  17.1 1.1 copy-done.5
  18.2 4.5 %all-to-all-done = bf16[8,160,128]{2,1,0:T(8,128)(2,1)S(1)} async-done(((bf16[8,160,128]{2,1,0:T(8,128)(2,1)}), bf16[8,160,128]{2,1,0:T(8,128)(2,1)S(1)}, u32[]{:S(2)}, u32[]{:S(2)}) %all-to-all-start) | async-done | bytes 327712 | tf_op jit(solution)/shard_map/all_to_all | solution.py:400
  22.7 1.3 collective-permute-start.2
  24.0 2.5 %collective-permute-start.1 = (bf16[256,5120]{1,0:T(8,128)(2,1)}, bf16[256,5120]{1,0:T(8,128)(2,1)}, u32[]{:S(2)}, u32[]{:S(2)}) collective-permute-start(bf16[256,5120]{1,0:T(8,128)(2,1)} %x_ref.1), channel_id=1, source_target_pairs={{0,1},{1,0},{2,3},{3,2},{4,5},{5,4},{6,7},{7,6},{8,9},{9,8},{10,11... | collective-permute-start | bytes 7864328 | tf_op jit(solution)/shard_map/ppermute | solution.py:385
  26.5 2.7 %collective-permute-start.3 = (bf16[1280,128]{1,0:T(8,128)(2,1)S(1)}, bf16[1280,128]{1,0:T(8,128)(2,1)S(1)}, u32[]{:S(2)}, u32[]{:S(2)}) collective-permute-start(bf16[1280,128]{1,0:T(8,128)(2,1)S(1)} %bitcast.30), channel_id=1, source_target_pairs={{0,192},{1,7},{2,194},{3,1},{4,196},{5,3},{6,198},{7,5},{8,200},{9... | collective-permute-start | bytes 983048 | tf_op jit(solution)/shard_map/ppermute | solution.py:385
  29.2 0.3 collective-permute-start.4
  29.6 0.6 collective-permute-done.2
  30.2 6.5 %collective-permute-done.3 = bf16[1280,128]{1,0:T(8,128)(2,1)S(1)} collective-permute-done((bf16[1280,128]{1,0:T(8,128)(2,1)S(1)}, bf16[1280,128]{1,0:T(8,128)(2,1)S(1)}, u32[]{:S(2)}, u32[]{:S(2)}) %collective-permute-start.3) | collective-permute-done | bytes 327712 | tf_op jit(solution)/shard_map/ppermute | solution.py:385
  36.8 0.2 collective-permute-done.4
  37.0 4.1 %all-to-all-start.1 = ((bf16[32,16,1408]{2,1,0:T(8,128)(2,1)}), bf16[32,16,1408]{2,1,0:T(8,128)(2,1)S(1)}, u32[]{:S(2)}, u32[]{:S(2)}) async-start(bf16[32,16,1408]{2,1,0:T(8,128)(2,1)} %bitcast.22), calls=%async_computation.1 | async-start | bytes 2883584 | tf_op jit(solution)/shard_map/all_to_all | solution.py:415
  41.2 1.3 collective-permute-start.6
  42.4 1.5 collective-permute-start.7
  43.9 1.5 collective-permute-start
  45.4 1.5 collective-permute-start.5
  46.9 2.1 %collective-permute-start.8 = (bf16[2560,128]{1,0:T(8,128)(2,1)S(1)}, bf16[2560,128]{1,0:T(8,128)(2,1)}, u32[]{:S(2)}, u32[]{:S(2)}) collective-permute-start(bf16[2560,128]{1,0:T(8,128)(2,1)S(1)} %pad_maximum_fusion.1.rest_1_), channel_id=1, source_target_pairs={{0,6},{1,193},{2,0},{3,195},{4,2},{5,197},{6,4},{7,199},{8,14},{9,... | collective-permute-start | bytes 1966088 | tf_op jit(solution)/shard_map/ppermute | solution.py:385
  49.0 10.1 %collective-permute-done.6.rest_3_ = bf16[2560,128]{1,0:T(8,128)(2,1)} collective-permute-done((bf16[2560,128]{1,0:T(8,128)(2,1)S(1)}, bf16[2560,128]{1,0:T(8,128)(2,1)}, u32[]{:S(2)}, u32[]{:S(2)}) %collective-permute-start.6) | collective-permute-done | bytes 655392 | tf_op jit(solution)/shard_map/ppermute | solution.py:385
  59.1 2.7 %collective-permute-start.9 = (bf16[2560,128]{1,0:T(8,128)(2,1)}, bf16[2560,128]{1,0:T(8,128)(2,1)}, u32[]{:S(2)}, u32[]{:S(2)}) collective-permute-start(bf16[2560,128]{1,0:T(8,128)(2,1)} %collective-permute-done.7.rest_4_), channel_id=1, source_target_pairs={{0,6},{1,193},{2,0},{3,195},{4,2},{5,197},{6,4},{7,199},{8,14},{9,... | collective-permute-start | bytes 1966088 | tf_op jit(solution)/shard_map/ppermute | solution.py:385
  62.0 0.7 row_places.1.hot_ref
  62.7 10.1 %collective-permute-done.5.rest_2_ = bf16[2560,128]{1,0:T(8,128)(2,1)} collective-permute-done((bf16[2560,128]{1,0:T(8,128)(2,1)S(1)}, bf16[2560,128]{1,0:T(8,128)(2,1)}, u32[]{:S(2)}, u32[]{:S(2)}) %collective-permute-start.5) | collective-permute-done | bytes 655392 | tf_op jit(solution)/shard_map/ppermute | solution.py:385
  72.8 8.6 %collective-permute-done.10.rest_7_ = bf16[2560,128]{1,0:T(8,128)(2,1)} collective-permute-done((bf16[2560,128]{1,0:T(8,128)(2,1)}, bf16[2560,128]{1,0:T(8,128)(2,1)}, u32[]{:S(2)}, u32[]{:S(2)}) %collective-permute-start.10) | collective-permute-done | bytes 655392 | tf_op jit(solution)/shard_map/ppermute | solution.py:385
  81.4 8.0 %project.1 = bf16[1024,512]{1,0:T(8,128)(2,1)S(1)} custom-call(s32[9]{0:T(128)S(1)} %pad_add_fusion.2.table_ref, bf16[1024,512]{1,0:T(8,128)(2,1)S(1)} %row_places.1.hot_ref, f32[1,512]{1,0:T(1,128)S(1)} %bitcast.28, bf16[256,5120]{1,0:T(8,128)(2,1)} %x_ref.1, bf16[256,5120]{1,0:T(8,128)(2,1)} %collective-permute-done.1.sib_ref, ...), custom_call_target="tpu_custom_call" | custom-call | flops 2684354560 | bytes 12582912 | tf_op jit(solution)/shard_map/project/pallas_call | solution.py:191
  89.5 1.0 copy-done.1
  90.4 7.9 %all-to-all-start.2 = ((bf16[32,32,512]{2,1,0:T(8,128)(2,1)}), bf16[32,32,512]{2,1,0:T(8,128)(2,1)S(1)}, u32[]{:S(2)}, u32[]{:S(2)}) async-start(bf16[32,32,512]{2,1,0:T(8,128)(2,1)} %bitcast.21), calls=%async_computation.2 | async-start | bytes 2097152 | tf_op jit(solution)/shard_map/all_to_all | solution.py:415
  98.5 1.3 collective-permute-done.11.sib_ref
  99.8 0.6 copy-done.8
  100.5 0.9 copy-done.9
  101.4 0.2 places.1.hot_ref
  101.6 1.0 unpack_queries.1.q_ref
  102.6 0.8 copy-done.6
  103.5 14.2 %all-to-all-done.2 = bf16[32,32,512]{2,1,0:T(8,128)(2,1)S(1)} async-done(((bf16[32,32,512]{2,1,0:T(8,128)(2,1)}), bf16[32,32,512]{2,1,0:T(8,128)(2,1)S(1)}, u32[]{:S(2)}, u32[]{:S(2)}) %all-to-all-start.2) | async-done | bytes 1048608 | tf_op jit(solution)/shard_map/all_to_all | solution.py:415
  117.6 0.4 unpack.1.a0
  118.1 0.8 copy-done.2
  118.9 4.6 %all-to-all-start.3 = ((bf16[32,16,1280]{2,1,0:T(8,128)(2,1)}), bf16[32,16,1280]{2,1,0:T(8,128)(2,1)S(1)}, u32[]{:S(2)}, u32[]{:S(2)}) async-start(bf16[32,16,1280]{2,1,0:T(8,128)(2,1)} %bitcast.23), calls=%async_computation.3 | async-start | bytes 2621440 | tf_op jit(solution)/shard_map/all_to_all | solution.py:415
  123.5 4.0 %collective-permute-start.12 = (bf16[544,512]{1,0:T(8,128)(2,1)S(1)}, bf16[544,512]{1,0:T(8,128)(2,1)}, u32[]{:S(2)}, u32[]{:S(2)}) collective-permute-start(bf16[544,512]{1,0:T(8,128)(2,1)S(1)} %copy-done.3), channel_id=1, source_target_pairs={{0,2},{1,3},{2,4},{3,5},{4,6},{5,7},{8,10},{9,11},{10,12},{11,13},... | collective-permute-start | bytes 1671176 | tf_op jit(solution)/shard_map/ppermute | solution.py:394
  127.6 4.4 %collective-permute-start.13 = (bf16[544,512]{1,0:T(8,128)(2,1)S(1)}, bf16[544,512]{1,0:T(8,128)(2,1)}, u32[]{:S(2)}, u32[]{:S(2)}) collective-permute-start(bf16[544,512]{1,0:T(8,128)(2,1)S(1)} %copy-done.3), channel_id=1, source_target_pairs={{0,4},{1,5},{2,6},{3,7},{8,12},{9,13},{10,14},{11,15},{16,20},{17,... | collective-permute-start | bytes 1671176 | tf_op jit(solution)/shard_map/ppermute | solution.py:394
  132.0 5.5 %collective-permute-done.12.a1 = bf16[544,512]{1,0:T(8,128)(2,1)} collective-permute-done((bf16[544,512]{1,0:T(8,128)(2,1)S(1)}, bf16[544,512]{1,0:T(8,128)(2,1)}, u32[]{:S(2)}, u32[]{:S(2)}) %collective-permute-start.12) | collective-permute-done | bytes 557088 | tf_op jit(solution)/shard_map/ppermute | solution.py:394
  137.5 6.0 %collective-permute-done.13.a2 = bf16[544,512]{1,0:T(8,128)(2,1)} collective-permute-done((bf16[544,512]{1,0:T(8,128)(2,1)S(1)}, bf16[544,512]{1,0:T(8,128)(2,1)}, u32[]{:S(2)}, u32[]{:S(2)}) %collective-permute-start.13) | collective-permute-done | bytes 557088 | tf_op jit(solution)/shard_map/ppermute | solution.py:394
  143.7 2.1 %collective-permute-done.16.b2 = bf16[544,512]{1,0:T(8,128)(2,1)} collective-permute-done((bf16[544,512]{1,0:T(8,128)(2,1)}, bf16[544,512]{1,0:T(8,128)(2,1)}, u32[]{:S(2)}, u32[]{:S(2)}) %collective-permute-start.16) | collective-permute-done | bytes 557088 | tf_op jit(solution)/shard_map/ppermute | solution.py:385
  145.8 7.9 %attend.2.rest_0_ = bf16[256,2560]{1,0:T(8,128)(2,1)} custom-call(s32[4]{0:T(128)S(1)} %pad_add_fusion.1.where_ref, s32[256,1]{1,0:T(8,128)S(1)} %copy.13.seg_ref, bf16[2,256,512]{2,1,0:T(8,128)(2,1)S(1)} %places.1.hot_ref, bf16[256,1280]{1,0:T(8,128)(2,1)S(1)} %copy-done.7, bf16[544,512]{1,0:T(8,128)(2,1)S(1)} %copy-done.3, ...), custom_call_target="tpu_custom_call" | custom-call | flops 1677721600 | bytes 4194304 | tf_op jit(solution)/shard_map/attend/pallas_call | solution.py:345
  153.7 8.4 %attend.3 = bf16[256,2560]{1,0:T(8,128)(2,1)} custom-call(s32[4]{0:T(128)S(1)} %pad_add_fusion.1.where_ref, s32[256,1]{1,0:T(8,128)S(1)} %copy.13.seg_ref, bf16[2,256,512]{2,1,0:T(8,128)(2,1)S(1)} %places.1.hot_ref, bf16[512,1280]{1,0:T(8,128)(2,1)S(1)} %bitcast.19, bf16[544,512]{1,0:T(8,128)(2,1)S(1)} %copy-done.3, ...), custom_call_target="tpu_custom_call", output_to_operand_aliasing={{}: (10, {})} | custom-call | flops 1677721600 | bytes 4194304 | tf_op jit(solution)/shard_map/attend/pallas_call | solution.py:345
  (48 shorter events, 0.7 us)
Async XLA Ops:
  0.0 1.0 copy-start
  1.8 20.9 %all-to-all-start = ((bf16[8,160,128]{2,1,0:T(8,128)(2,1)}), bf16[8,160,128]{2,1,0:T(8,128)(2,1)S(1)}, u32[]{:S(2)}, u32[]{:S(2)}) async-start(bf16[8,160,128]{2,1,0:T(8,128)(2,1)} %broadcast_in_dim.2), calls=%async_computation | async-start | bytes 655360 | tf_op jit(solution)/shard_map/all_to_all | solution.py:400
  11.6 0.7 copy-start.10
  12.3 1.3 copy-start.13
  16.0 1.1 copy-start.4
  17.1 1.1 copy-start.5
  22.7 7.5 %collective-permute-start.2 = (bf16[1280,128]{1,0:T(8,128)(2,1)S(1)}, bf16[1280,128]{1,0:T(8,128)(2,1)S(1)}, u32[]{:S(2)}, u32[]{:S(2)}) collective-permute-start(bf16[1280,128]{1,0:T(8,128)(2,1)S(1)} %bitcast.29), channel_id=1, source_target_pairs={{0,64},{1,3},{2,66},{3,5},{4,68},{5,7},{6,70},{7,1},{8,72},{9,11},... | collective-permute-start | bytes 983048 | tf_op jit(solution)/shard_map/ppermute | solution.py:385
  24.0 57.4 %collective-permute-start.1 = (bf16[256,5120]{1,0:T(8,128)(2,1)}, bf16[256,5120]{1,0:T(8,128)(2,1)}, u32[]{:S(2)}, u32[]{:S(2)}) collective-permute-start(bf16[256,5120]{1,0:T(8,128)(2,1)} %x_ref.1), channel_id=1, source_target_pairs={{0,1},{1,0},{2,3},{3,2},{4,5},{5,4},{6,7},{7,6},{8,9},{9,8},{10,11... | collective-permute-start | bytes 7864328 | tf_op jit(solution)/shard_map/ppermute | solution.py:385
  26.5 10.3 %collective-permute-start.3 = (bf16[1280,128]{1,0:T(8,128)(2,1)S(1)}, bf16[1280,128]{1,0:T(8,128)(2,1)S(1)}, u32[]{:S(2)}, u32[]{:S(2)}) collective-permute-start(bf16[1280,128]{1,0:T(8,128)(2,1)S(1)} %bitcast.30), channel_id=1, source_target_pairs={{0,192},{1,7},{2,194},{3,1},{4,196},{5,3},{6,198},{7,5},{8,200},{9... | collective-permute-start | bytes 983048 | tf_op jit(solution)/shard_map/ppermute | solution.py:385
  29.2 7.7 %collective-permute-start.4 = (bf16[1280,128]{1,0:T(8,128)(2,1)S(1)}, bf16[1280,128]{1,0:T(8,128)(2,1)S(1)}, u32[]{:S(2)}, u32[]{:S(2)}) collective-permute-start(bf16[1280,128]{1,0:T(8,128)(2,1)S(1)} %bitcast.31), channel_id=1, source_target_pairs={{0,128},{1,5},{2,130},{3,7},{4,132},{5,1},{6,134},{7,3},{8,136},{9... | collective-permute-start | bytes 983048 | tf_op jit(solution)/shard_map/ppermute | solution.py:385
  37.0 6.9 %copy-start.11 = (s32[256]{0:T(256)S(1)}, s32[256]{0:T(256)}, u32[]{:S(2)}) copy-start(s32[256]{0:T(256)} %param.9) | copy-start | bytes 3076
  37.0 6.9 %copy-start.14 = (s32[1,256]{1,0:T(1,128)S(1)}, s32[1,256]{1,0:T(1,128)}, u32[]{:S(2)}) copy-start(s32[1,256]{1,0:T(1,128)} %param.10) | copy-start | bytes 3076
  37.0 24.7 %copy-start.15 = (s32[4]{0:T(128)S(1)}, s32[4]{0:T(128)}, u32[]{:S(2)}) copy-start(s32[4]{0:T(128)} %constant.71.clone) | copy-start | bytes 52
  37.0 53.4 %all-to-all-start.1 = ((bf16[32,16,1408]{2,1,0:T(8,128)(2,1)}), bf16[32,16,1408]{2,1,0:T(8,128)(2,1)S(1)}, u32[]{:S(2)}, u32[]{:S(2)}) async-start(bf16[32,16,1408]{2,1,0:T(8,128)(2,1)} %bitcast.22), calls=%async_computation.1 | async-start | bytes 2883584 | tf_op jit(solution)/shard_map/all_to_all | solution.py:415
  41.2 40.2 %copy-start.12 = (f32[512]{0:T(512)S(1)}, f32[512]{0:T(512)}, u32[]{:S(2)}) copy-start(f32[512]{0:T(512)} %param.12) | copy-start | bytes 6148
  41.2 17.9 %collective-permute-start.6 = (bf16[2560,128]{1,0:T(8,128)(2,1)S(1)}, bf16[2560,128]{1,0:T(8,128)(2,1)}, u32[]{:S(2)}, u32[]{:S(2)}) collective-permute-start(bf16[2560,128]{1,0:T(8,128)(2,1)S(1)} %pad_maximum_fusion.1.rest_1_), channel_id=1, source_target_pairs={{0,2},{1,65},{2,4},{3,67},{4,6},{5,69},{6,0},{7,71},{8,10},{9,73},... | collective-permute-start | bytes 1966088 | tf_op jit(solution)/shard_map/ppermute | solution.py:385
  42.4 16.6 %collective-permute-start.7 = (bf16[2560,128]{1,0:T(8,128)(2,1)S(1)}, bf16[2560,128]{1,0:T(8,128)(2,1)}, u32[]{:S(2)}, u32[]{:S(2)}) collective-permute-start(bf16[2560,128]{1,0:T(8,128)(2,1)S(1)} %pad_maximum_fusion.rest_0_), channel_id=1, source_target_pairs={{0,6},{1,193},{2,0},{3,195},{4,2},{5,197},{6,4},{7,199},{8,14},{9,... | collective-permute-start | bytes 1966088 | tf_op jit(solution)/shard_map/ppermute | solution.py:385
  43.9 3.0 %collective-permute-start = (s32[2,256]{1,0:T(2,128)S(1)}, s32[2,256]{1,0:T(2,128)S(1)}, u32[]{:S(2)}, u32[]{:S(2)}) collective-permute-start(s32[2,256]{1,0:T(2,128)S(1)} %pad_add_fusion), channel_id=1, source_target_pairs={{0,1},{1,0},{2,3},{3,2},{4,5},{5,4},{6,7},{7,6},{8,9},{9,8},{10,11... | collective-permute-start | bytes 6152 | tf_op jit(solution)/shard_map/ppermute | solution.py:385
  45.4 27.3 %collective-permute-start.5 = (bf16[2560,128]{1,0:T(8,128)(2,1)S(1)}, bf16[2560,128]{1,0:T(8,128)(2,1)}, u32[]{:S(2)}, u32[]{:S(2)}) collective-permute-start(bf16[2560,128]{1,0:T(8,128)(2,1)S(1)} %pad_maximum_fusion.rest_0_), channel_id=1, source_target_pairs={{0,2},{1,65},{2,4},{3,67},{4,6},{5,69},{6,0},{7,71},{8,10},{9,73},... | collective-permute-start | bytes 1966088 | tf_op jit(solution)/shard_map/ppermute | solution.py:385
  46.9 25.9 %collective-permute-start.8 = (bf16[2560,128]{1,0:T(8,128)(2,1)S(1)}, bf16[2560,128]{1,0:T(8,128)(2,1)}, u32[]{:S(2)}, u32[]{:S(2)}) collective-permute-start(bf16[2560,128]{1,0:T(8,128)(2,1)S(1)} %pad_maximum_fusion.1.rest_1_), channel_id=1, source_target_pairs={{0,6},{1,193},{2,0},{3,195},{4,2},{5,197},{6,4},{7,199},{8,14},{9,... | collective-permute-start | bytes 1966088 | tf_op jit(solution)/shard_map/ppermute | solution.py:385
  59.1 22.3 %collective-permute-start.10 = (bf16[2560,128]{1,0:T(8,128)(2,1)}, bf16[2560,128]{1,0:T(8,128)(2,1)}, u32[]{:S(2)}, u32[]{:S(2)}) collective-permute-start(bf16[2560,128]{1,0:T(8,128)(2,1)} %collective-permute-done.6.rest_3_), channel_id=1, source_target_pairs={{0,2},{1,65},{2,4},{3,67},{4,6},{5,69},{6,0},{7,71},{8,10},{9,73},... | collective-permute-start | bytes 1966088 | tf_op jit(solution)/shard_map/ppermute | solution.py:385
  59.1 22.3 %collective-permute-start.9 = (bf16[2560,128]{1,0:T(8,128)(2,1)}, bf16[2560,128]{1,0:T(8,128)(2,1)}, u32[]{:S(2)}, u32[]{:S(2)}) collective-permute-start(bf16[2560,128]{1,0:T(8,128)(2,1)} %collective-permute-done.7.rest_4_), channel_id=1, source_target_pairs={{0,6},{1,193},{2,0},{3,195},{4,2},{5,197},{6,4},{7,199},{8,14},{9,... | collective-permute-start | bytes 1966088 | tf_op jit(solution)/shard_map/ppermute | solution.py:385
  89.5 1.0 copy-start.1
  90.4 27.2 %all-to-all-start.2 = ((bf16[32,32,512]{2,1,0:T(8,128)(2,1)}), bf16[32,32,512]{2,1,0:T(8,128)(2,1)S(1)}, u32[]{:S(2)}, u32[]{:S(2)}) async-start(bf16[32,32,512]{2,1,0:T(8,128)(2,1)} %bitcast.21), calls=%async_computation.2 | async-start | bytes 2097152 | tf_op jit(solution)/shard_map/all_to_all | solution.py:415
  98.4 1.4 collective-permute-start.11
  99.8 0.6 copy-start.8
  100.5 0.9 copy-start.9
  102.6 0.8 copy-start.6
  118.1 0.8 copy-start.2
  118.9 4.7 %copy-start.3 = (bf16[544,512]{1,0:T(8,128)(2,1)S(1)}, bf16[544,512]{1,0:T(8,128)(2,1)}, u32[]{:S(2)}) copy-start(bf16[544,512]{1,0:T(8,128)(2,1)} %copy-done.2) | copy-start | bytes 1671172
  118.9 26.9 %copy-start.7 = (bf16[256,1280]{1,0:T(8,128)(2,1)S(1)}, bf16[256,1280]{1,0:T(8,128)(2,1)}, u32[]{:S(2)}) copy-start(bf16[256,1280]{1,0:T(8,128)(2,1)} %copy-done.6) | copy-start | bytes 1966084
  118.9 34.8 %all-to-all-start.3 = ((bf16[32,16,1280]{2,1,0:T(8,128)(2,1)}), bf16[32,16,1280]{2,1,0:T(8,128)(2,1)S(1)}, u32[]{:S(2)}, u32[]{:S(2)}) async-start(bf16[32,16,1280]{2,1,0:T(8,128)(2,1)} %bitcast.23), calls=%async_computation.3 | async-start | bytes 2621440 | tf_op jit(solution)/shard_map/all_to_all | solution.py:415
  123.5 13.9 %collective-permute-start.12 = (bf16[544,512]{1,0:T(8,128)(2,1)S(1)}, bf16[544,512]{1,0:T(8,128)(2,1)}, u32[]{:S(2)}, u32[]{:S(2)}) collective-permute-start(bf16[544,512]{1,0:T(8,128)(2,1)S(1)} %copy-done.3), channel_id=1, source_target_pairs={{0,2},{1,3},{2,4},{3,5},{4,6},{5,7},{8,10},{9,11},{10,12},{11,13},... | collective-permute-start | bytes 1671176 | tf_op jit(solution)/shard_map/ppermute | solution.py:394
  127.6 15.9 %collective-permute-start.13 = (bf16[544,512]{1,0:T(8,128)(2,1)S(1)}, bf16[544,512]{1,0:T(8,128)(2,1)}, u32[]{:S(2)}, u32[]{:S(2)}) collective-permute-start(bf16[544,512]{1,0:T(8,128)(2,1)S(1)} %copy-done.3), channel_id=1, source_target_pairs={{0,4},{1,5},{2,6},{3,7},{8,12},{9,13},{10,14},{11,15},{16,20},{17,... | collective-permute-start | bytes 1671176 | tf_op jit(solution)/shard_map/ppermute | solution.py:394
  132.0 11.7 %collective-permute-start.14 = (bf16[544,512]{1,0:T(8,128)(2,1)S(1)}, bf16[544,512]{1,0:T(8,128)(2,1)}, u32[]{:S(2)}, u32[]{:S(2)}) collective-permute-start(bf16[544,512]{1,0:T(8,128)(2,1)S(1)} %copy-done.3), channel_id=1, source_target_pairs={{0,1},{1,0},{2,3},{3,2},{4,5},{5,4},{6,7},{7,6},{8,9},{9,8},{10,11... | collective-permute-start | bytes 1671176 | tf_op jit(solution)/shard_map/ppermute | solution.py:385
  137.5 6.2 %collective-permute-start.15 = (bf16[544,512]{1,0:T(8,128)(2,1)}, bf16[544,512]{1,0:T(8,128)(2,1)}, u32[]{:S(2)}, u32[]{:S(2)}) collective-permute-start(bf16[544,512]{1,0:T(8,128)(2,1)} %collective-permute-done.12.a1), channel_id=1, source_target_pairs={{0,1},{1,0},{2,3},{3,2},{4,5},{5,4},{6,7},{7,6},{8,9},{9,8},{10,11... | collective-permute-start | bytes 1671176 | tf_op jit(solution)/shard_map/ppermute | solution.py:385
  143.5 2.3 %collective-permute-start.16 = (bf16[544,512]{1,0:T(8,128)(2,1)}, bf16[544,512]{1,0:T(8,128)(2,1)}, u32[]{:S(2)}, u32[]{:S(2)}) collective-permute-start(bf16[544,512]{1,0:T(8,128)(2,1)} %collective-permute-done.13.a2), channel_id=1, source_target_pairs={{0,1},{1,0},{2,3},{3,2},{4,5},{5,4},{6,7},{7,6},{8,9},{9,8},{10,11... | collective-permute-start | bytes 1671176 | tf_op jit(solution)/shard_map/ppermute | solution.py:385

commit v5 on v4

--- a/solution.py
+++ b/solution.py
@@ -128,52 +128,30 @@
     )(core, col, row, sib_col, sib_row)
 
 
-def project_kernel(
-    table_ref, hot_ref, gain_ref, x_ref, sib_ref, *rest
-):
+def project_kernel(table_ref, hot_ref, gain_ref, x_ref, sib_ref, *rest):
+    sources, (out_ref, acc, done) = rest[:8], rest[8:]
     step = pl.program_id(0)
     core = table_ref[8]
-    sources, (out_ref, weight, acc, sems) = rest[:8], rest[8:]
-
-    def copy(j, i, x, y):
-        return pltpu.make_async_copy(
-            sources[2 * j + i // 2].at[pl.ds(i % 2 * RUN, RUN), :],
-            weight.at[
-                pl.ds(pl.multiple_of(x * RUN, RUN), RUN),
-                pl.ds(pl.multiple_of(y * HEAD_SIZE, HEAD_SIZE), HEAD_SIZE),
-            ],
-            sems.at[x, y],
-        )
+
+    def add(blocks):
+        w = jnp.concatenate(blocks, axis=1)
+        x = jnp.concatenate([x_ref[...], sib_ref[...]], axis=0)
+        acc[...] += jnp.dot(x, w, preferred_element_type=F32)
 
     @pl.when(step == 0)
     def _():
-        @pl.when(core == 0)
-        def _():
-            for i in range(4):
-                for j in range(4):
-                    copy(j, i, table_ref[i], table_ref[4 + j]).start()
-
-        @pl.when(core != 0)
-        def _():
-            for j in range(4):
-                for i in range(4):
-                    copy(j, i, table_ref[j], table_ref[4 + i]).start()
-
-    x = table_ref[step]
-    for y in range(4):
-        copy(0, 0, x, y).wait()
-    w = weight[pl.ds(pl.multiple_of(x * RUN, RUN), RUN), :]
-    for n, ref in enumerate((x_ref, sib_ref)):
-        now = jnp.dot(ref[...], w, preferred_element_type=F32)
-        part = slice(n * LOC, (n + 1) * LOC)
-
-        @pl.when(step == 0)
-        def _(now=now, part=part):
-            acc[part, :] = now
-
-        @pl.when(step > 0)
-        def _(now=now, part=part):
-            acc[part, :] += now
+        acc[...] = jnp.zeros_like(acc)
+
+    for t in range(4):
+
+        @pl.when((step == t) & (core == 0))
+        def _(t=t):
+            rows = slice(t % 2 * RUN, (t % 2 + 1) * RUN)
+            add([sources[2 * j + t // 2][rows, :] for j in range(4)])
+
+        @pl.when((step == t) & (core != 0))
+        def _(t=t):
+            add([sources[2 * t + i // 2][i % 2 * RUN : (i % 2 + 1) * RUN, :] for i in range(4)])
 
     @pl.when(step == 3)
     def _():
@@ -181,9 +159,11 @@
         raw = acc[...]
         level = lax.rsqrt(jnp.mean(raw * raw, axis=-1, keepdims=True) + 1e-06)
         level = jnp.where(is_key, level, F32(1))
-        gain = jnp.where(is_key, gain_ref[...], F32(1))
-        done = (raw * level * gain).astype(BF16)
-        out_ref[...] = jnp.dot(hot_ref[...], done, preferred_element_type=F32).astype(BF16)
+        for n in range(4):
+            column = pl.ds(pl.multiple_of(table_ref[4 + n] * HEAD_SIZE, HEAD_SIZE), HEAD_SIZE)
+            gain = jnp.where(is_key, gain_ref[:, column], F32(1))
+            done[:, column] = (raw[:, n * HEAD_SIZE : (n + 1) * HEAD_SIZE] * level * gain).astype(BF16)
+        out_ref[...] = jnp.dot(hot_ref[...], done[...], preferred_element_type=F32).astype(BF16)
 
 
 def project(table, hot, gain, rows, sib_rows, weights):
@@ -199,13 +179,9 @@
                 across,
                 across,
             ]
-            + [pl.BlockSpec(memory_space=pl.ANY)] * 8,
+            + [pl.BlockSpec(memory_space=pltpu.VMEM)] * 8,
             out_specs=whole((2 * SLOTS, ROW_WIDTH)),
-            scratch_shapes=[
-                pltpu.VMEM((WIDTH, ROW_WIDTH), BF16),
-                pltpu.VMEM((PAIR, ROW_WIDTH), F32),
-                pltpu.SemaphoreType.DMA((4, 4)),
-            ],
+            scratch_shapes=[pltpu.VMEM((PAIR, ROW_WIDTH), F32), pltpu.VMEM((PAIR, ROW_WIDTH), BF16)],
         ),
         out_shape=jax.ShapeDtypeStruct((2 * SLOTS, ROW_WIDTH), BF16),
         compiler_params=pltpu.CompilerParams(**PARAMS),

time: 165 us -> 164 us (level)
  transfers between devices with their start and end apart: 21 -> 21, of which waited for: 12 -> 12; matrix products, arithmetic and copies ran while one was open for 1% -> 1% of each run, Pallas kernels for 12% -> 13%
where the time goes in v5:
time: 164 us; the launch traced here: 161 us
  waiting for transfers between devices  69.1 us (42%)
  starting transfers between devices  51.4 us (31%)
  Pallas kernels  29.2 us (18%)
  local copies, waits for them, and re-layouts  11.2 us (7%)
    ppermute x15, waiting for transfers between devices, shift(): return lax.ppermute(array, ('dp', 'ctx'), pairs)  39.5 us
    ppermute x15, starting transfers between devices, shift(): return lax.ppermute(array, ('dp', 'ctx'), pairs)  17.5 us
    pallas_call x2, Pallas kernels, attend(): pl.pallas_call(functools.partial(attend_kernel, packed), grid=(heads,), i...  16.2 us
    all_to_all x3, starting transfers between devices, move(): lax.all_to_all(sent, 'dp', split_axis=0, concat_axis=0, tiled=True)  16.2 us
    all_to_all x3, waiting for transfers between devices, move(): lax.all_to_all(sent, 'dp', split_axis=0, concat_axis=0, tiled=True)  13.9 us
    ppermute x2, waiting for transfers between devices, send_up(): return lax.ppermute(array, ('dp', 'ctx'), pairs)  11.2 us
    unnamed x32, local copies, waits for them, and re-layouts  9.37 us
    all_to_all x1, starting transfers between devices, along_z(): lax.all_to_all(copies, ('dp', 'ctx'), 0, 0, axis_index_groups=groups, til...  9.01 us
  transfers between devices with their start and end apart: 21, of which 12 were waited for; matrix products, arithmetic and copies ran while one was open for 1% of the time, Pallas kernels for 13%

profile of v5, /device:TPU:1, one launch (start us, length us, event | category | flops | bytes accessed | tf_op | source)
XLA Modules:
  0.0 161.4 jit_solution(5025435850237724149)
XLA Ops:
  0.0 1.0 copy-done
  1.0 0.8 broadcast_in_dim.2
  1.8 9.0 %all-to-all-start = ((bf16[8,160,128]{2,1,0:T(8,128)(2,1)}), bf16[8,160,128]{2,1,0:T(8,128)(2,1)S(1)}, u32[]{:S(2)}, u32[]{:S(2)}) async-start(bf16[8,160,128]{2,1,0:T(8,128)(2,1)} %broadcast_in_dim.2), calls=%async_computation | async-start | bytes 655360 | tf_op jit(solution)/shard_map/all_to_all | solution.py:376
  10.8 0.8 copy.9.col_ref
  11.6 0.7 copy-done.10
  12.3 1.3 copy-done.13
  13.6 2.4 %pack_queries.1 = (bf16[512,1408]{1,0:T(8,128)(2,1)S(1)}, bf16[512,1280]{1,0:T(8,128)(2,1)S(1)}) custom-call(s32[256,1]{1,0:T(8,128)S(1)} %copy.9.col_ref, s32[1,256]{1,0:T(1,128)S(1)} %bitcast.25, bf16[256,2560]{1,0:T(8,128)(2,1)S(1)} %copy-done.13), custom_call_target="tpu_custom_call" | custom-call | flops 671088640 | bytes 4194304 | tf_op jit(solution)/shard_map/pack_queries/pallas_call | solution.py:91
  16.0 1.1 copy-done.4
  17.1 1.1 copy-done.5
  18.2 4.5 %all-to-all-done = bf16[8,160,128]{2,1,0:T(8,128)(2,1)S(1)} async-done(((bf16[8,160,128]{2,1,0:T(8,128)(2,1)}), bf16[8,160,128]{2,1,0:T(8,128)(2,1)S(1)}, u32[]{:S(2)}, u32[]{:S(2)}) %all-to-all-start) | async-done | bytes 327712 | tf_op jit(solution)/shard_map/all_to_all | solution.py:376
  22.7 1.3 collective-permute-start.2
  24.0 2.5 %collective-permute-start.1 = (bf16[256,5120]{1,0:T(8,128)(2,1)}, bf16[256,5120]{1,0:T(8,128)(2,1)}, u32[]{:S(2)}, u32[]{:S(2)}) collective-permute-start(bf16[256,5120]{1,0:T(8,128)(2,1)} %x_ref.1), channel_id=1, source_target_pairs={{0,1},{1,0},{2,3},{3,2},{4,5},{5,4},{6,7},{7,6},{8,9},{9,8},{10,11... | collective-permute-start | bytes 7864328 | tf_op jit(solution)/shard_map/ppermute | solution.py:361
  26.5 2.7 %collective-permute-start.3 = (bf16[1280,128]{1,0:T(8,128)(2,1)S(1)}, bf16[1280,128]{1,0:T(8,128)(2,1)S(1)}, u32[]{:S(2)}, u32[]{:S(2)}) collective-permute-start(bf16[1280,128]{1,0:T(8,128)(2,1)S(1)} %bitcast.30), channel_id=1, source_target_pairs={{0,192},{1,7},{2,194},{3,1},{4,196},{5,3},{6,198},{7,5},{8,200},{9... | collective-permute-start | bytes 983048 | tf_op jit(solution)/shard_map/ppermute | solution.py:361
  29.2 0.3 collective-permute-start.4
  29.6 0.6 collective-permute-done.2
  30.2 6.5 %collective-permute-done.3 = bf16[1280,128]{1,0:T(8,128)(2,1)S(1)} collective-permute-done((bf16[1280,128]{1,0:T(8,128)(2,1)S(1)}, bf16[1280,128]{1,0:T(8,128)(2,1)S(1)}, u32[]{:S(2)}, u32[]{:S(2)}) %collective-permute-start.3) | collective-permute-done | bytes 327712 | tf_op jit(solution)/shard_map/ppermute | solution.py:361
  36.8 0.2 collective-permute-done.4
  37.0 4.1 %all-to-all-start.1 = ((bf16[32,16,1408]{2,1,0:T(8,128)(2,1)}), bf16[32,16,1408]{2,1,0:T(8,128)(2,1)S(1)}, u32[]{:S(2)}, u32[]{:S(2)}) async-start(bf16[32,16,1408]{2,1,0:T(8,128)(2,1)} %bitcast.22), calls=%async_computation.1 | async-start | bytes 2883584 | tf_op jit(solution)/shard_map/all_to_all | solution.py:391
  41.2 1.3 collective-permute-start.6
  42.4 1.5 collective-permute-start.7
  43.9 1.5 collective-permute-start
  45.4 1.5 collective-permute-start.5
  46.9 2.1 %collective-permute-start.8 = (bf16[2560,128]{1,0:T(8,128)(2,1)S(1)}, bf16[2560,128]{1,0:T(8,128)(2,1)}, u32[]{:S(2)}, u32[]{:S(2)}) collective-permute-start(bf16[2560,128]{1,0:T(8,128)(2,1)S(1)} %pad_maximum_fusion.1.rest_1_), channel_id=1, source_target_pairs={{0,6},{1,193},{2,0},{3,195},{4,2},{5,197},{6,4},{7,199},{8,14},{9,... | collective-permute-start | bytes 1966088 | tf_op jit(solution)/shard_map/ppermute | solution.py:361
  49.0 10.1 %collective-permute-done.6.rest_3_ = bf16[2560,128]{1,0:T(8,128)(2,1)} collective-permute-done((bf16[2560,128]{1,0:T(8,128)(2,1)S(1)}, bf16[2560,128]{1,0:T(8,128)(2,1)}, u32[]{:S(2)}, u32[]{:S(2)}) %collective-permute-start.6) | collective-permute-done | bytes 655392 | tf_op jit(solution)/shard_map/ppermute | solution.py:361
  59.1 2.7 %collective-permute-start.9 = (bf16[2560,128]{1,0:T(8,128)(2,1)}, bf16[2560,128]{1,0:T(8,128)(2,1)}, u32[]{:S(2)}, u32[]{:S(2)}) collective-permute-start(bf16[2560,128]{1,0:T(8,128)(2,1)} %collective-permute-done.7.rest_4_), channel_id=1, source_target_pairs={{0,6},{1,193},{2,0},{3,195},{4,2},{5,197},{6,4},{7,199},{8,14},{9,... | collective-permute-start | bytes 1966088 | tf_op jit(solution)/shard_map/ppermute | solution.py:361
  62.0 0.7 row_places.1.hot_ref
  62.7 10.1 %collective-permute-done.5.rest_2_ = bf16[2560,128]{1,0:T(8,128)(2,1)} collective-permute-done((bf16[2560,128]{1,0:T(8,128)(2,1)S(1)}, bf16[2560,128]{1,0:T(8,128)(2,1)}, u32[]{:S(2)}, u32[]{:S(2)}) %collective-permute-start.5) | collective-permute-done | bytes 655392 | tf_op jit(solution)/shard_map/ppermute | solution.py:361
  72.8 8.6 %collective-permute-done.10.rest_7_ = bf16[2560,128]{1,0:T(8,128)(2,1)} collective-permute-done((bf16[2560,128]{1,0:T(8,128)(2,1)}, bf16[2560,128]{1,0:T(8,128)(2,1)}, u32[]{:S(2)}, u32[]{:S(2)}) %collective-permute-start.10) | collective-permute-done | bytes 655392 | tf_op jit(solution)/shard_map/ppermute | solution.py:361
  81.4 8.2 %project.1 = bf16[1024,512]{1,0:T(8,128)(2,1)S(1)} custom-call(s32[9]{0:T(128)S(1)} %pad_add_fusion.2.table_ref, bf16[1024,512]{1,0:T(8,128)(2,1)S(1)} %row_places.1.hot_ref, f32[1,512]{1,0:T(1,128)S(1)} %bitcast.28, bf16[256,5120]{1,0:T(8,128)(2,1)} %x_ref.1, bf16[256,5120]{1,0:T(8,128)(2,1)} %collective-permute-done.1.sib_ref, ...), custom_call_target="tpu_custom_call" | custom-call | flops 2684354560 | bytes 12582912 | tf_op jit(solution)/shard_map/project/pallas_call | solution.py:171
  89.6 1.0 copy-done.1
  90.6 7.9 %all-to-all-start.2 = ((bf16[32,32,512]{2,1,0:T(8,128)(2,1)}), bf16[32,32,512]{2,1,0:T(8,128)(2,1)S(1)}, u32[]{:S(2)}, u32[]{:S(2)}) async-start(bf16[32,32,512]{2,1,0:T(8,128)(2,1)} %bitcast.21), calls=%async_computation.2 | async-start | bytes 2097152 | tf_op jit(solution)/shard_map/all_to_all | solution.py:391
  98.6 1.3 collective-permute-done.11.sib_ref
  99.9 0.6 copy-done.8
  100.6 0.9 copy-done.9
  101.5 0.2 places.1.hot_ref
  101.7 1.0 unpack_queries.1.q_ref
  102.8 0.8 copy-done.6
  103.6 13.9 %all-to-all-done.2 = bf16[32,32,512]{2,1,0:T(8,128)(2,1)S(1)} async-done(((bf16[32,32,512]{2,1,0:T(8,128)(2,1)}), bf16[32,32,512]{2,1,0:T(8,128)(2,1)S(1)}, u32[]{:S(2)}, u32[]{:S(2)}) %all-to-all-start.2) | async-done | bytes 1048608 | tf_op jit(solution)/shard_map/all_to_all | solution.py:391
  117.5 0.4 unpack.1.a0
  118.0 0.8 copy-done.2
  118.8 4.2 %all-to-all-start.3 = ((bf16[32,16,1280]{2,1,0:T(8,128)(2,1)}), bf16[32,16,1280]{2,1,0:T(8,128)(2,1)S(1)}, u32[]{:S(2)}, u32[]{:S(2)}) async-start(bf16[32,16,1280]{2,1,0:T(8,128)(2,1)} %bitcast.23), calls=%async_computation.3 | async-start | bytes 2621440 | tf_op jit(solution)/shard_map/all_to_all | solution.py:391
  123.0 4.1 %collective-permute-start.12 = (bf16[544,512]{1,0:T(8,128)(2,1)S(1)}, bf16[544,512]{1,0:T(8,128)(2,1)}, u32[]{:S(2)}, u32[]{:S(2)}) collective-permute-start(bf16[544,512]{1,0:T(8,128)(2,1)S(1)} %copy-done.3), channel_id=1, source_target_pairs={{0,2},{1,3},{2,4},{3,5},{4,6},{5,7},{8,10},{9,11},{10,12},{11,13},... | collective-permute-start | bytes 1671176 | tf_op jit(solution)/shard_map/ppermute | solution.py:370
  127.1 4.6 %collective-permute-start.13 = (bf16[544,512]{1,0:T(8,128)(2,1)S(1)}, bf16[544,512]{1,0:T(8,128)(2,1)}, u32[]{:S(2)}, u32[]{:S(2)}) collective-permute-start(bf16[544,512]{1,0:T(8,128)(2,1)S(1)} %copy-done.3), channel_id=1, source_target_pairs={{0,4},{1,5},{2,6},{3,7},{8,12},{9,13},{10,14},{11,15},{16,20},{17,... | collective-permute-start | bytes 1671176 | tf_op jit(solution)/shard_map/ppermute | solution.py:370
  131.7 5.2 %collective-permute-done.12.a1 = bf16[544,512]{1,0:T(8,128)(2,1)} collective-permute-done((bf16[544,512]{1,0:T(8,128)(2,1)S(1)}, bf16[544,512]{1,0:T(8,128)(2,1)}, u32[]{:S(2)}, u32[]{:S(2)}) %collective-permute-start.12) | collective-permute-done | bytes 557088 | tf_op jit(solution)/shard_map/ppermute | solution.py:370
  136.8 6.0 %collective-permute-done.13.a2 = bf16[544,512]{1,0:T(8,128)(2,1)} collective-permute-done((bf16[544,512]{1,0:T(8,128)(2,1)S(1)}, bf16[544,512]{1,0:T(8,128)(2,1)}, u32[]{:S(2)}, u32[]{:S(2)}) %collective-permute-start.13) | collective-permute-done | bytes 557088 | tf_op jit(solution)/shard_map/ppermute | solution.py:370
  143.1 2.1 %collective-permute-done.16.b2 = bf16[544,512]{1,0:T(8,128)(2,1)} collective-permute-done((bf16[544,512]{1,0:T(8,128)(2,1)}, bf16[544,512]{1,0:T(8,128)(2,1)}, u32[]{:S(2)}, u32[]{:S(2)}) %collective-permute-start.16) | collective-permute-done | bytes 557088 | tf_op jit(solution)/shard_map/ppermute | solution.py:361
  145.2 7.9 %attend.2.rest_0_ = bf16[256,2560]{1,0:T(8,128)(2,1)} custom-call(s32[4]{0:T(128)S(1)} %pad_add_fusion.1.where_ref, s32[256,1]{1,0:T(8,128)S(1)} %copy.13.seg_ref, bf16[2,256,512]{2,1,0:T(8,128)(2,1)S(1)} %places.1.hot_ref, bf16[256,1280]{1,0:T(8,128)(2,1)S(1)} %copy-done.7, bf16[544,512]{1,0:T(8,128)(2,1)S(1)} %copy-done.3, ...), custom_call_target="tpu_custom_call" | custom-call | flops 1677721600 | bytes 4194304 | tf_op jit(solution)/shard_map/attend/pallas_call | solution.py:321
  153.0 8.4 %attend.3 = bf16[256,2560]{1,0:T(8,128)(2,1)} custom-call(s32[4]{0:T(128)S(1)} %pad_add_fusion.1.where_ref, s32[256,1]{1,0:T(8,128)S(1)} %copy.13.seg_ref, bf16[2,256,512]{2,1,0:T(8,128)(2,1)S(1)} %places.1.hot_ref, bf16[512,1280]{1,0:T(8,128)(2,1)S(1)} %bitcast.19, bf16[544,512]{1,0:T(8,128)(2,1)S(1)} %copy-done.3, ...), custom_call_target="tpu_custom_call", output_to_operand_aliasing={{}: (10, {})} | custom-call | flops 1677721600 | bytes 4194304 | tf_op jit(solution)/shard_map/attend/pallas_call | solution.py:321
  (48 shorter events, 0.7 us)
Async XLA Ops:
  0.0 1.0 copy-start
  1.8 20.9 %all-to-all-start = ((bf16[8,160,128]{2,1,0:T(8,128)(2,1)}), bf16[8,160,128]{2,1,0:T(8,128)(2,1)S(1)}, u32[]{:S(2)}, u32[]{:S(2)}) async-start(bf16[8,160,128]{2,1,0:T(8,128)(2,1)} %broadcast_in_dim.2), calls=%async_computation | async-start | bytes 655360 | tf_op jit(solution)/shard_map/all_to_all | solution.py:376
  11.6 0.7 copy-start.10
  12.3 1.3 copy-start.13
  16.0 1.1 copy-start.4
  17.1 1.1 copy-start.5
  22.7 7.5 %collective-permute-start.2 = (bf16[1280,128]{1,0:T(8,128)(2,1)S(1)}, bf16[1280,128]{1,0:T(8,128)(2,1)S(1)}, u32[]{:S(2)}, u32[]{:S(2)}) collective-permute-start(bf16[1280,128]{1,0:T(8,128)(2,1)S(1)} %bitcast.29), channel_id=1, source_target_pairs={{0,64},{1,3},{2,66},{3,5},{4,68},{5,7},{6,70},{7,1},{8,72},{9,11},... | collective-permute-start | bytes 983048 | tf_op jit(solution)/shard_map/ppermute | solution.py:361
  24.0 57.4 %collective-permute-start.1 = (bf16[256,5120]{1,0:T(8,128)(2,1)}, bf16[256,5120]{1,0:T(8,128)(2,1)}, u32[]{:S(2)}, u32[]{:S(2)}) collective-permute-start(bf16[256,5120]{1,0:T(8,128)(2,1)} %x_ref.1), channel_id=1, source_target_pairs={{0,1},{1,0},{2,3},{3,2},{4,5},{5,4},{6,7},{7,6},{8,9},{9,8},{10,11... | collective-permute-start | bytes 7864328 | tf_op jit(solution)/shard_map/ppermute | solution.py:361
  26.5 10.3 %collective-permute-start.3 = (bf16[1280,128]{1,0:T(8,128)(2,1)S(1)}, bf16[1280,128]{1,0:T(8,128)(2,1)S(1)}, u32[]{:S(2)}, u32[]{:S(2)}) collective-permute-start(bf16[1280,128]{1,0:T(8,128)(2,1)S(1)} %bitcast.30), channel_id=1, source_target_pairs={{0,192},{1,7},{2,194},{3,1},{4,196},{5,3},{6,198},{7,5},{8,200},{9... | collective-permute-start | bytes 983048 | tf_op jit(solution)/shard_map/ppermute | solution.py:361
  29.2 7.7 %collective-permute-start.4 = (bf16[1280,128]{1,0:T(8,128)(2,1)S(1)}, bf16[1280,128]{1,0:T(8,128)(2,1)S(1)}, u32[]{:S(2)}, u32[]{:S(2)}) collective-permute-start(bf16[1280,128]{1,0:T(8,128)(2,1)S(1)} %bitcast.31), channel_id=1, source_target_pairs={{0,128},{1,5},{2,130},{3,7},{4,132},{5,1},{6,134},{7,3},{8,136},{9... | collective-permute-start | bytes 983048 | tf_op jit(solution)/shard_map/ppermute | solution.py:361
  37.0 6.9 %copy-start.11 = (s32[256]{0:T(256)S(1)}, s32[256]{0:T(256)}, u32[]{:S(2)}) copy-start(s32[256]{0:T(256)} %param.9) | copy-start | bytes 3076
  37.0 6.9 %copy-start.14 = (s32[1,256]{1,0:T(1,128)S(1)}, s32[1,256]{1,0:T(1,128)}, u32[]{:S(2)}) copy-start(s32[1,256]{1,0:T(1,128)} %param.10) | copy-start | bytes 3076
  37.0 24.7 %copy-start.15 = (s32[4]{0:T(128)S(1)}, s32[4]{0:T(128)}, u32[]{:S(2)}) copy-start(s32[4]{0:T(128)} %constant.71.clone) | copy-start | bytes 52
  37.0 53.5 %all-to-all-start.1 = ((bf16[32,16,1408]{2,1,0:T(8,128)(2,1)}), bf16[32,16,1408]{2,1,0:T(8,128)(2,1)S(1)}, u32[]{:S(2)}, u32[]{:S(2)}) async-start(bf16[32,16,1408]{2,1,0:T(8,128)(2,1)} %bitcast.22), calls=%async_computation.1 | async-start | bytes 2883584 | tf_op jit(solution)/shard_map/all_to_all | solution.py:391
  41.2 40.2 %copy-start.12 = (f32[512]{0:T(512)S(1)}, f32[512]{0:T(512)}, u32[]{:S(2)}) copy-start(f32[512]{0:T(512)} %param.12) | copy-start | bytes 6148
  41.2 17.9 %collective-permute-start.6 = (bf16[2560,128]{1,0:T(8,128)(2,1)S(1)}, bf16[2560,128]{1,0:T(8,128)(2,1)}, u32[]{:S(2)}, u32[]{:S(2)}) collective-permute-start(bf16[2560,128]{1,0:T(8,128)(2,1)S(1)} %pad_maximum_fusion.1.rest_1_), channel_id=1, source_target_pairs={{0,2},{1,65},{2,4},{3,67},{4,6},{5,69},{6,0},{7,71},{8,10},{9,73},... | collective-permute-start | bytes 1966088 | tf_op jit(solution)/shard_map/ppermute | solution.py:361
  42.4 16.6 %collective-permute-start.7 = (bf16[2560,128]{1,0:T(8,128)(2,1)S(1)}, bf16[2560,128]{1,0:T(8,128)(2,1)}, u32[]{:S(2)}, u32[]{:S(2)}) collective-permute-start(bf16[2560,128]{1,0:T(8,128)(2,1)S(1)} %pad_maximum_fusion.rest_0_), channel_id=1, source_target_pairs={{0,6},{1,193},{2,0},{3,195},{4,2},{5,197},{6,4},{7,199},{8,14},{9,... | collective-permute-start | bytes 1966088 | tf_op jit(solution)/shard_map/ppermute | solution.py:361
  43.9 3.0 %collective-permute-start = (s32[2,256]{1,0:T(2,128)S(1)}, s32[2,256]{1,0:T(2,128)S(1)}, u32[]{:S(2)}, u32[]{:S(2)}) collective-permute-start(s32[2,256]{1,0:T(2,128)S(1)} %pad_add_fusion), channel_id=1, source_target_pairs={{0,1},{1,0},{2,3},{3,2},{4,5},{5,4},{6,7},{7,6},{8,9},{9,8},{10,11... | collective-permute-start | bytes 6152 | tf_op jit(solution)/shard_map/ppermute | solution.py:361
  45.4 27.3 %collective-permute-start.5 = (bf16[2560,128]{1,0:T(8,128)(2,1)S(1)}, bf16[2560,128]{1,0:T(8,128)(2,1)}, u32[]{:S(2)}, u32[]{:S(2)}) collective-permute-start(bf16[2560,128]{1,0:T(8,128)(2,1)S(1)} %pad_maximum_fusion.rest_0_), channel_id=1, source_target_pairs={{0,2},{1,65},{2,4},{3,67},{4,6},{5,69},{6,0},{7,71},{8,10},{9,73},... | collective-permute-start | bytes 1966088 | tf_op jit(solution)/shard_map/ppermute | solution.py:361
  46.9 25.9 %collective-permute-start.8 = (bf16[2560,128]{1,0:T(8,128)(2,1)S(1)}, bf16[2560,128]{1,0:T(8,128)(2,1)}, u32[]{:S(2)}, u32[]{:S(2)}) collective-permute-start(bf16[2560,128]{1,0:T(8,128)(2,1)S(1)} %pad_maximum_fusion.1.rest_1_), channel_id=1, source_target_pairs={{0,6},{1,193},{2,0},{3,195},{4,2},{5,197},{6,4},{7,199},{8,14},{9,... | collective-permute-start | bytes 1966088 | tf_op jit(solution)/shard_map/ppermute | solution.py:361
  59.1 22.3 %collective-permute-start.10 = (bf16[2560,128]{1,0:T(8,128)(2,1)}, bf16[2560,128]{1,0:T(8,128)(2,1)}, u32[]{:S(2)}, u32[]{:S(2)}) collective-permute-start(bf16[2560,128]{1,0:T(8,128)(2,1)} %collective-permute-done.6.rest_3_), channel_id=1, source_target_pairs={{0,2},{1,65},{2,4},{3,67},{4,6},{5,69},{6,0},{7,71},{8,10},{9,73},... | collective-permute-start | bytes 1966088 | tf_op jit(solution)/shard_map/ppermute | solution.py:361
  59.1 22.3 %collective-permute-start.9 = (bf16[2560,128]{1,0:T(8,128)(2,1)}, bf16[2560,128]{1,0:T(8,128)(2,1)}, u32[]{:S(2)}, u32[]{:S(2)}) collective-permute-start(bf16[2560,128]{1,0:T(8,128)(2,1)} %collective-permute-done.7.rest_4_), channel_id=1, source_target_pairs={{0,6},{1,193},{2,0},{3,195},{4,2},{5,197},{6,4},{7,199},{8,14},{9,... | collective-permute-start | bytes 1966088 | tf_op jit(solution)/shard_map/ppermute | solution.py:361
  89.6 1.0 copy-start.1
  90.6 27.0 %all-to-all-start.2 = ((bf16[32,32,512]{2,1,0:T(8,128)(2,1)}), bf16[32,32,512]{2,1,0:T(8,128)(2,1)S(1)}, u32[]{:S(2)}, u32[]{:S(2)}) async-start(bf16[32,32,512]{2,1,0:T(8,128)(2,1)} %bitcast.21), calls=%async_computation.2 | async-start | bytes 2097152 | tf_op jit(solution)/shard_map/all_to_all | solution.py:391
  98.5 1.4 collective-permute-start.11
  99.9 0.6 copy-start.8
  100.6 0.9 copy-start.9
  102.8 0.8 copy-start.6
  118.0 0.8 copy-start.2
  118.8 4.2 %copy-start.3 = (bf16[544,512]{1,0:T(8,128)(2,1)S(1)}, bf16[544,512]{1,0:T(8,128)(2,1)}, u32[]{:S(2)}) copy-start(bf16[544,512]{1,0:T(8,128)(2,1)} %copy-done.2) | copy-start | bytes 1671172
  118.8 26.4 %copy-start.7 = (bf16[256,1280]{1,0:T(8,128)(2,1)S(1)}, bf16[256,1280]{1,0:T(8,128)(2,1)}, u32[]{:S(2)}) copy-start(bf16[256,1280]{1,0:T(8,128)(2,1)} %copy-done.6) | copy-start | bytes 1966084
  118.8 34.2 %all-to-all-start.3 = ((bf16[32,16,1280]{2,1,0:T(8,128)(2,1)}), bf16[32,16,1280]{2,1,0:T(8,128)(2,1)S(1)}, u32[]{:S(2)}, u32[]{:S(2)}) async-start(bf16[32,16,1280]{2,1,0:T(8,128)(2,1)} %bitcast.23), calls=%async_computation.3 | async-start | bytes 2621440 | tf_op jit(solution)/shard_map/all_to_all | solution.py:391
  123.0 13.9 %collective-permute-start.12 = (bf16[544,512]{1,0:T(8,128)(2,1)S(1)}, bf16[544,512]{1,0:T(8,128)(2,1)}, u32[]{:S(2)}, u32[]{:S(2)}) collective-permute-start(bf16[544,512]{1,0:T(8,128)(2,1)S(1)} %copy-done.3), channel_id=1, source_target_pairs={{0,2},{1,3},{2,4},{3,5},{4,6},{5,7},{8,10},{9,11},{10,12},{11,13},... | collective-permute-start | bytes 1671176 | tf_op jit(solution)/shard_map/ppermute | solution.py:370
  127.1 15.8 %collective-permute-start.13 = (bf16[544,512]{1,0:T(8,128)(2,1)S(1)}, bf16[544,512]{1,0:T(8,128)(2,1)}, u32[]{:S(2)}, u32[]{:S(2)}) collective-permute-start(bf16[544,512]{1,0:T(8,128)(2,1)S(1)} %copy-done.3), channel_id=1, source_target_pairs={{0,4},{1,5},{2,6},{3,7},{8,12},{9,13},{10,14},{11,15},{16,20},{17,... | collective-permute-start | bytes 1671176 | tf_op jit(solution)/shard_map/ppermute | solution.py:370
  131.7 11.4 %collective-permute-start.14 = (bf16[544,512]{1,0:T(8,128)(2,1)S(1)}, bf16[544,512]{1,0:T(8,128)(2,1)}, u32[]{:S(2)}, u32[]{:S(2)}) collective-permute-start(bf16[544,512]{1,0:T(8,128)(2,1)S(1)} %copy-done.3), channel_id=1, source_target_pairs={{0,1},{1,0},{2,3},{3,2},{4,5},{5,4},{6,7},{7,6},{8,9},{9,8},{10,11... | collective-permute-start | bytes 1671176 | tf_op jit(solution)/shard_map/ppermute | solution.py:361
  136.8 6.2 %collective-permute-start.15 = (bf16[544,512]{1,0:T(8,128)(2,1)}, bf16[544,512]{1,0:T(8,128)(2,1)}, u32[]{:S(2)}, u32[]{:S(2)}) collective-permute-start(bf16[544,512]{1,0:T(8,128)(2,1)} %collective-permute-done.12.a1), channel_id=1, source_target_pairs={{0,1},{1,0},{2,3},{3,2},{4,5},{5,4},{6,7},{7,6},{8,9},{9,8},{10,11... | collective-permute-start | bytes 1671176 | tf_op jit(solution)/shard_map/ppermute | solution.py:361
  142.9 2.3 %collective-permute-start.16 = (bf16[544,512]{1,0:T(8,128)(2,1)}, bf16[544,512]{1,0:T(8,128)(2,1)}, u32[]{:S(2)}, u32[]{:S(2)}) collective-permute-start(bf16[544,512]{1,0:T(8,128)(2,1)} %collective-permute-done.13.a2), channel_id=1, source_target_pairs={{0,1},{1,0},{2,3},{3,2},{4,5},{5,4},{6,7},{7,6},{8,9},{9,8},{10,11... | collective-permute-start | bytes 1671176 | tf_op jit(solution)/shard_map/ppermute | solution.py:361
